TPU v7x, 32 devices: a whole 2x2x4 slice. The times are simulated.
32 devices in a mesh: study: 2 (over x), vol: 8 (over z, y), tile: 2 (over core).
Axes of the slice: x: 2, y: 2, z: 4, core: 2. Of those that a mesh axis runs over, the one named last changes fastest.
Arguments:
- spectra: bfloat16 [16, 4, 768, 2048], P(('study', 'vol'), None, 'tile'), parts along dimension 0, may hold values from -6 to 6
- block_scales: float32 [16, 4, 768, 16], P(('study', 'vol'), None, 'tile'), parts along dimension 0, may hold values from 0.3 to 3
- retina_blocks: int32 [12, 2], P(('study', 'tile')), parts along dimension 0, may hold values from 0 to 3, as said below
- quality_block: int32 [16, 6], P(('study', 'vol'), 'tile'), parts along dimension 0, may hold values from 0 to 3, as said below
- quality_bias: float32 [16, 6], P(('study', 'vol'), 'tile'), parts along dimension 0, may hold values from -110 to 160
Outputs:
- angiogram: float32 [1024, 768], P(('study', 'vol'), 'tile'), parts along dimension 0
- joined_structure: float32 [1024, 768], P(('study', 'vol'), 'tile'), parts along dimension 0
- spread_map: float32 [1024, 768], P(('study', 'vol'), 'tile'), parts along dimension 0
There are 2 independent parts, one for each index of `study`. A program takes and returns all parts, laid end to end along the dimension named above; each array names one. Nothing has to cross between parts.
Inputs may be any that keep to these rules, and one draw needn't show every extreme that they name: retina_blocks[j,0] <= retina_blocks[j,1]. quality_block[v,j] lies between retina_blocks[j,0] and retina_blocks[j,1].
All inputs are finite; a program needn't handle non-finite values.
Results may differ from a plain program's by a relative error of at most 0.0015.
Values sent between devices are 32-bit elements; how exact they have to be, the bound alone decides.
No kernel may reach another device: no remote copies, remote signals or barrier semaphores. Data moves between devices by JAX's collectives and lax.ppermute only.
A program may use at most 128 MiB of HBM per device.

v0:
```python
import math

import jax
import jax.numpy as jnp
from jax import lax
from jax.sharding import PartitionSpec as P

K = 2048
DEPTH = 512
BANDS = 4
REPEATS = 4
DBLK = 128
ABLK = 128
SB = 128
NDB = 4


smooth_taps = (1.0 / 9.0, 2.0 / 9.0, 3.0 / 9.0, 2.0 / 9.0, 1.0 / 9.0)


def padded_2(array, sides, width):
    for axis, dim in sides:
        count, length = (lax.axis_size(axis), array.shape[dim])
        up = [(i, (i + 1) % count) for i in range(count - 1)]
        down = [(j, i) for i, j in up]
        last = lax.slice_in_dim(array, length - width, length, axis=dim)
        initial = lax.slice_in_dim(array, 0, width, axis=dim)
        before = lax.ppermute(last, axis, up)
        after = lax.ppermute(initial, axis, down)
        array = jnp.concatenate([before, array, after], axis=dim)
    return array


def window_tables():
    sample_index = jnp.arange(K, dtype=jnp.int32)
    depth_index = jnp.arange(DEPTH, dtype=jnp.int32)
    phase_angle = (sample_index[:, None] * depth_index[None, :] % K).astype(jnp.float32) * (
        2.0 * math.pi / K
    )
    kernel = jnp.stack([jnp.cos(phase_angle), -jnp.sin(phase_angle)], axis=1)
    centres = (jnp.arange(BANDS, dtype=jnp.float32)[:, None] + 0.5) * (K / BANDS)
    distance = sample_index.astype(jnp.float32)[None, :] - centres
    offsets = distance / (K / 8.0)
    window = jnp.where(jnp.abs(distance) <= K / 2.0, jnp.exp(-0.5 * offsets * offsets), 0.0)
    window = window / jnp.sqrt(jnp.sum(window * window, axis=1, keepdims=True))
    return (window[:, :, None, None] * kernel[None]).astype(jnp.bfloat16)


def spread_columns(values, repeat_width):
    widened = jnp.broadcast_to(values[..., None], values.shape + (repeat_width,))
    return widened.reshape(values.shape[:-1] + (values.shape[-1] * repeat_width,))


def scale_spectra(spectra_vol, scales_vol):
    shaped = spectra_vol.astype(jnp.float32).reshape(scales_vol.shape + (SB,))
    return (shaped * scales_vol[..., None]).reshape(spectra_vol.shape).astype(jnp.bfloat16)


def band_maps(scaled, tables):
    line_count = scaled.shape[1]
    decorrelation = jnp.zeros((DEPTH, line_count), jnp.float32)
    power_total = jnp.zeros((DEPTH, line_count), jnp.float32)
    for band_index in range(BANDS):
        fields = jnp.einsum(
            "kcd,rak->cdra", tables[band_index], scaled, preferred_element_type=jnp.float32
        )
        band_power = fields[0] * fields[0] + fields[1] * fields[1]
        amplitude = jnp.sqrt(band_power + 0.05)
        pair_ratio = (
            2.0
            * amplitude[:, :-1]
            * amplitude[:, 1:]
            / (band_power[:, :-1] + band_power[:, 1:] + 0.1)
        )
        decorrelation = decorrelation + jnp.sum(1.0 - pair_ratio, axis=1)
        power_total = power_total + jnp.sum(band_power, axis=1)
    decorrelation = decorrelation / (BANDS * (REPEATS - 1))
    structure = jnp.log(power_total / (BANDS * REPEATS) + 0.1)
    return (decorrelation, structure)


def retina_mask(first_col, last_col):
    depth_block = jnp.arange(DEPTH, dtype=jnp.int32) // DBLK
    return (depth_block[:, None] >= first_col[None, :]) & (
        depth_block[:, None] <= last_col[None, :]
    )


def lateral_smooth(padded, line_count):
    filtered = smooth_taps[0] * padded[:, 0:line_count]
    for offset_index in range(1, 5):
        filtered = (
            filtered
            + smooth_taps[offset_index] * padded[:, offset_index : offset_index + line_count]
        )
    return filtered


def block_quality(structure, qblock):
    tile_count = qblock.shape[0]
    block_means = jnp.mean(structure.reshape(NDB, DBLK, tile_count, ABLK), axis=(1, 3))
    chosen = jnp.arange(NDB, dtype=jnp.int32)[:, None] == qblock[None, :]
    return jnp.sum(jnp.where(chosen, block_means, 0.0), axis=0)


def on_device(spectra, block_scales, retina_blocks, quality_block, quality_bias):
    tables = window_tables()
    scaled = scale_spectra(spectra[0], block_scales[0])
    line_count = scaled.shape[1]
    decorrelation, structure = band_maps(scaled, tables)
    first_col = spread_columns(retina_blocks[:, 0], ABLK)
    last_col = spread_columns(retina_blocks[:, 1], ABLK)
    inside = retina_mask(first_col, last_col)
    masked_decorrelation = jnp.where(inside, decorrelation, 0.0)
    masked_structure = jnp.where(inside, structure, 0.0)
    padded = padded_2(masked_decorrelation, (("tile", 1),), 2)
    smoothed = lateral_smooth(padded, line_count)
    volume_score = block_quality(structure, quality_block[0]) + quality_bias[0]
    scores = lax.all_gather(volume_score[None, :], "vol", axis=0, tiled=True)
    top_score = jnp.max(scores, axis=0)
    weight_total = jnp.sum(jnp.exp(scores - top_score[None, :]), axis=0)
    own_weight = spread_columns(jnp.exp(volume_score - top_score) / weight_total, ABLK)[None, :]
    stacked = jnp.stack(
        [own_weight * smoothed, own_weight * smoothed * smoothed, own_weight * masked_structure]
    )
    joined_maps = lax.psum_scatter(stacked, "vol", scatter_dimension=1, tiled=True)
    angiogram = joined_maps[0]
    second_moment = joined_maps[1]
    joined_structure = joined_maps[2]
    spread_map = jnp.sqrt(second_moment - angiogram * angiogram + 0.01)
    return (angiogram, joined_structure, spread_map)


def solution(mesh):
    return jax.shard_map(
        on_device,
        mesh=mesh,
        in_specs=(
            P(("study", "vol"), None, "tile", None),
            P(("study", "vol"), None, "tile", None),
            P(("study", "tile"), None),
            P(("study", "vol"), "tile"),
            P(("study", "vol"), "tile"),
        ),
        out_specs=(
            P(("study", "vol"), "tile"),
            P(("study", "vol"), "tile"),
            P(("study", "vol"), "tile"),
        ),
        check_vma=False,
    )
```

profile of v0, /device:TPU:0, one launch (start us, length us, event | category | flops | bytes accessed | tf_op | source)
XLA Modules:
  0.0 233.3 jit_solution(10307218010125406644)
XLA Ops:
  7.2 0.0 reduce-scatter.2.cloned.1.call-start
  7.3 17.7 %sine_negate_fusion = (f32[2048,1,512]{0,2,1:T(8,128)}, f32[2048,1,512]{0,2,1:T(8,128)}) fusion(), kind=kLoop, calls=%fused_computation.18 | loop fusion | flops 15728640 | bytes 8388608 | tf_op jit(solution)/shard_map/neg | solution.py:40
  24.9 0.2 multiply_reduce_fusion
  25.2 0.1 broadcast_divide_fusion
  25.3 0.3 copy.13
  25.5 5.0 %copy.20 = f32[192,8,16,128]{3,2,1,0:T(8,128)S(1)} copy(bf16[192,8,16,128]{3,1,2,0:T(8,128)(2,1)} %bitcast.110) | data formatting | bytes 18874368
  30.6 5.9 %fusion = bf16[4,384,16,128]{3,2,1,0:T(8,128)(2,1)} fusion(f32[4,384,16]{2,1,0:T(8,128)S(1)} %copy.13, f32[4,384,16,128]{3,2,1,0:T(8,128)S(1)} %bitcast.107), kind=kLoop, calls=%fused_computation.2 | loop fusion | flops 6291456 | bytes 18972672 | tf_op jit(solution)/shard_map/convert_element_type | solution.py:56
  36.5 10.3 %reshape.414 = bf16[4,384,2048,1]{2,1,0,3:T(8,128)(2,1)} reshape(bf16[4,384,16,128]{3,2,1,0:T(8,128)(2,1)} %fusion) | data formatting | bytes 12582912 | tf_op jit(solution)/shard_map/convert_element_type | solution.py:56
  46.8 4.2 %pad_maximum_fusion = f32[2048,2,512]{0,2,1:T(8,128)S(1)} fusion(f32[2048,1,512]{0,2,1:T(8,128)} %get-tuple-element.19, f32[2048,1,512]{0,2,1:T(8,128)} %get-tuple-element.20), kind=kLoop, calls=%fused_computation.3 | loop fusion | flops 2097152 | bytes 16777216 | tf_op jit(solution)/shard_map/stack | solution.py:40
  51.0 6.3 %multiply_convert_fusion = bf16[4,2048,2,512]{1,3,2,0:T(8,128)(2,1)} fusion(f32[2048,2,512]{0,2,1:T(8,128)S(1)} %pad_maximum_fusion, f32[4,2048]{1,0:T(4,128)S(1)} %broadcast_divide_fusion), kind=kLoop, calls=%fused_computation | loop fusion | flops 16777216 | bytes 25198592 | tf_op jit(solution)/shard_map/convert_element_type | solution.py:46
  57.3 8.5 %fusion.4 = f32[2,512,4,384]{3,1,2,0:T(8,128)S(1)} fusion(bf16[4,384,2048,1]{2,1,0,3:T(8,128)(2,1)S(1)} %bitcast.109, bf16[4,2048,2,512]{1,3,2,0:T(8,128)(2,1)} %multiply_convert_fusion), kind=kOutput, calls=%fused_computation.11 | convolution fusion | flops 6442450944 | bytes 16777216 | tf_op jit(solution)/shard_map/kcd,rak->cdra/dot_general | solution.py:64
  65.9 8.6 %fusion.5 = f32[2,512,4,384]{3,1,2,0:T(8,128)S(1)} fusion(bf16[4,384,2048,1]{2,1,0,3:T(8,128)(2,1)S(1)} %bitcast.109, bf16[4,2048,2,512]{1,3,2,0:T(8,128)(2,1)} %multiply_convert_fusion), kind=kOutput, calls=%fused_computation.13 | convolution fusion | flops 6442450944 | bytes 16777216 | tf_op jit(solution)/shard_map/kcd,rak->cdra/dot_general | solution.py:64
  74.5 8.7 %fusion.6 = f32[2,512,4,384]{3,1,2,0:T(8,128)S(1)} fusion(bf16[4,384,2048,1]{2,1,0,3:T(8,128)(2,1)S(1)} %bitcast.109, bf16[4,2048,2,512]{1,3,2,0:T(8,128)(2,1)} %multiply_convert_fusion), kind=kOutput, calls=%fused_computation.15 | convolution fusion | flops 6442450944 | bytes 16777216 | tf_op jit(solution)/shard_map/kcd,rak->cdra/dot_general | solution.py:64
  83.2 10.3 %fusion.7 = f32[2,512,4,384]{3,1,2,0:T(8,128)S(1)} fusion(bf16[4,384,2048,1]{2,1,0,3:T(8,128)(2,1)} %reshape.414, bf16[4,2048,2,512]{1,3,2,0:T(8,128)(2,1)} %multiply_convert_fusion), kind=kOutput, calls=%fused_computation.17 | convolution fusion | flops 6442450944 | bytes 16777216 | tf_op jit(solution)/shard_map/kcd,rak->cdra/dot_general | solution.py:64
  93.5 3.8 %add_sqrt_fusion = (f32[512,4,384]{2,0,1:T(8,128)}, f32[512,4,384]{2,0,1:T(8,128)}) fusion(f32[2,512,4,384]{3,1,2,0:T(8,128)S(1)} %fusion.4), kind=kLoop, calls=%fused_computation.34 | loop fusion | flops 3145728 | bytes 12582912 | tf_op jit(solution)/shard_map/sqrt | solution.py:68
  97.3 3.8 %add_sqrt_fusion.1 = (f32[512,4,384]{2,0,1:T(8,128)}, f32[512,4,384]{2,0,1:T(8,128)}) fusion(f32[2,512,4,384]{3,1,2,0:T(8,128)S(1)} %fusion.5), kind=kLoop, calls=%fused_computation.35 | loop fusion | flops 3145728 | bytes 12582912 | tf_op jit(solution)/shard_map/sqrt | solution.py:68
  101.1 3.7 %add_sqrt_fusion.3 = (f32[512,4,384]{2,0,1:T(8,128)}, f32[512,4,384]{2,0,1:T(8,128)}) fusion(f32[2,512,4,384]{3,1,2,0:T(8,128)S(1)} %fusion.7), kind=kLoop, calls=%fused_computation.37 | loop fusion | flops 3145728 | bytes 12582912 | tf_op jit(solution)/shard_map/sqrt | solution.py:68
  104.8 1.1 add_sqrt_fusion.2
  106.0 0.1 broadcast_bitcast_fusion
  106.0 4.7 %fusion.30 = f32[512,384]{1,0:T(8,128)S(1)} fusion(f32[512,4,384]{2,0,1:T(8,128)} %get-tuple-element.14, f32[512,4,384]{2,0,1:T(8,128)} %get-tuple-element.13), kind=kLoop, calls=%fused_computation.66 | loop fusion | flops 3932160 | bytes 10223616 | tf_op jit(solution)/shard_map/reduce_sum | solution.py:75
  110.7 4.7 %fusion.29 = f32[512,384]{1,0:T(8,128)S(1)} fusion(f32[512,4,384]{2,0,1:T(8,128)} %get-tuple-element.12, f32[512,4,384]{2,0,1:T(8,128)} %get-tuple-element.11), kind=kLoop, calls=%fused_computation.65 | loop fusion | flops 3932160 | bytes 10223616 | tf_op jit(solution)/shard_map/reduce_sum | solution.py:75
  115.4 5.5 %fusion.27 = f32[512,384]{1,0:T(8,128)} fusion(f32[512,4,384]{2,0,1:T(8,128)} %get-tuple-element.10, f32[512,4,384]{2,0,1:T(8,128)} %get-tuple-element.9), kind=kLoop, calls=%fused_computation.63 | loop fusion | flops 3932160 | bytes 10223616 | tf_op jit(solution)/shard_map/reduce_sum | solution.py:75
  120.9 1.6 fusion.28
  122.5 1.7 multiply_select_fusion
  124.2 0.9 fusion.73
  125.0 2.4 %collective-permute-start = (f32[512,2]{1,0:T(8,128)}, f32[512,2]{1,0:T(8,128)S(1)}, u32[]{:S(2)}, u32[]{:S(2)}) collective-permute-start(f32[512,2]{1,0:T(8,128)} %get-tuple-element.15), channel_id=1, source_target_pairs={{0,1},{2,3},{4,5},{6,7},{8,9},{10,11},{12,13},{14,15},{16,17},{18,... | collective-permute-start | bytes 12296 | tf_op jit(solution)/shard_map/ppermute | solution.py:28
  127.4 0.5 fusion.51
  127.9 0.5 fusion.49
  128.3 0.5 fusion.45
  128.8 0.5 fusion.47
  129.3 0.3 add_log_fusion
  129.6 0.3 copy.14
  129.8 0.3 reshape.409
  130.1 0.2 reduce_sum.115
  130.4 0.2 select_reduce_fusion
  130.6 1.3 collective-permute-start.1
  131.9 21.5 %all-gather = f32[8,1,3]{2,1,0:T(1,128)S(1)} all-gather(f32[1,1,3]{2,1,0:T(1,128)S(1)} %fusion.64), channel_id=1, replica_groups=mesh['study'=2,'vol'=8,'tile'=2] {'vol'}, dimensions={0}, use_global_device_ids=true | all-gather | bytes 108 | tf_op jit(solution)/shard_map/all_gather | solution.py:119
  153.4 0.1 copy.15
  153.5 0.2 fusion.62
  153.7 0.1 broadcast_bitcast_fusion.2
  153.8 0.2 fusion.43
  154.0 1.1 multiply_bitcast_fusion
  155.1 0.1 fusion.40
  155.2 1.6 pad_maximum_fusion.1
  156.7 0.0 reduce-scatter.2.cloned.1.call-update
  156.8 66.5 %reduce-scatter.2.cloned.1.call-done = f32[3,64,384]{2,1,0:T(8,128)} async-done(((f32[3,512,384]{2,1,0:T(8,128)}), f32[3,64,384]{2,1,0:T(8,128)}) %reduce-scatter.2.cloned.1.call-update) | async-done | bytes 294928 | tf_op jit(solution)/shard_map/reduce_scatter | solution.py:126
  223.3 1.5 slice_bitcast_fusion.9
  224.8 1.6 fusion.54
  (23 shorter events, 0.1 us)
Async XLA Ops:
  7.2 216.1 %reduce-scatter.2.cloned.1.call-start = ((), (), s32[]{:S(2)}) async-start(), calls=%async_computation.1 | async-start | bytes 2654208 | tf_op jit(solution)/shard_map/reduce_scatter | solution.py:126
  7.2 18.0 %copy-start = (f32[1,4,384,16]{2,3,1,0:T(8,128)S(1)}, f32[1,4,384,16]{2,3,1,0:T(8,128)}, u32[]{:S(2)}) copy-start(f32[1,4,384,16]{2,3,1,0:T(8,128)} %param.6) | copy-start | bytes 294916
  46.8 10.5 %slice-start = ((s8[6291456]{0:T(1024)(128)(4,1)}), s8[4194304]{0:T(1024)(128)(4,1)S(1)}, s32[]{:S(2)}) async-start(s8[6291456]{0:T(1024)(128)(4,1)} %bitcast.108), calls=%async_computation.2 | async-start | bytes 8388608
  51.0 6.3 %slice-start.1 = ((s8[6291456]{0:T(1024)(128)(4,1)}), s8[2097152]{0:T(1024)(128)(4,1)S(1)}, s32[]{:S(2)}) async-start(s8[6291456]{0:T(1024)(128)(4,1)} %bitcast.108), calls=%async_computation.3 | async-start | bytes 4194304
  83.2 10.3 %copy-start.1 = (s32[3,2]{0,1:T(2,128)S(1)}, s32[3,2]{0,1:T(2,128)}, u32[]{:S(2)}) copy-start(s32[3,2]{0,1:T(2,128)} %param.7) | copy-start | bytes 76
  125.0 29.0 %collective-permute-start = (f32[512,2]{1,0:T(8,128)}, f32[512,2]{1,0:T(8,128)S(1)}, u32[]{:S(2)}, u32[]{:S(2)}) collective-permute-start(f32[512,2]{1,0:T(8,128)} %get-tuple-element.15), channel_id=1, source_target_pairs={{0,1},{2,3},{4,5},{6,7},{8,9},{10,11},{12,13},{14,15},{16,17},{18,... | collective-permute-start | bytes 12296 | tf_op jit(solution)/shard_map/ppermute | solution.py:28
  129.3 1.1 copy-start.3
  129.3 1.3 copy-start.2
  130.6 23.4 %collective-permute-start.1 = (f32[512,2]{1,0:T(8,128)}, f32[512,2]{1,0:T(8,128)S(1)}, u32[]{:S(2)}, u32[]{:S(2)}) collective-permute-start(f32[512,2]{1,0:T(8,128)} %get-tuple-element.16), channel_id=1, source_target_pairs={{1,0},{3,2},{5,4},{7,6},{9,8},{11,10},{13,12},{15,14},{17,16},{19,... | collective-permute-start | bytes 12296 | tf_op jit(solution)/shard_map/ppermute | solution.py:29
Sparse Core Ops, SparseCore 0:
  156.9 66.3 reduce-scatter.1
where the time goes:
time: 234 us; the launch traced here: 233 us
  other arithmetic  72.3 us (31%)
  waiting for transfers between devices  66.5 us (28%)
  matrix products  36.1 us (15%)
  blocking collectives  21.5 us (9%)
  local copies, waits for them, and re-layouts  18.8 us (8%)
  between operations  14.3 us (6%)
  starting transfers between devices  3.69 us (2%)
    reduce_scatter x1, waiting for transfers between devices, on_device(): lax.psum_scatter(stacked, 'vol', scatter_dimension=1, tiled=True)  66.5 us
    dot_general x4, matrix products, band_maps(): jnp.einsum('kcd,rak->cdra', tables[band_index], scaled, preferred_element...  36.1 us
    all_gather x1, blocking collectives, on_device(): scores = lax.all_gather(volume_score[None, :], 'vol', axis=0, tiled=True)  21.5 us
    neg x1, other arithmetic, window_tables(): kernel = jnp.stack([jnp.cos(phase_angle), -jnp.sin(phase_angle)], axis=1)  17.7 us
    reduce_sum x4, other arithmetic, band_maps(): decorrelation = decorrelation + jnp.sum(1.0 - pair_ratio, axis=1)  16.5 us
    sqrt x4, other arithmetic, band_maps(): amplitude = jnp.sqrt(band_power + 0.05)  12.4 us
    convert_element_type x1, local copies, waits for them, and re-layouts, scale_spectra(): (shaped * scales_vol[..., None]).reshape(spectra_vol.shape)  10.3 us
    convert_element_type x1, other arithmetic, window_tables(): return (window[:, :, None, None] * kernel[None]).astype(jnp.bfloat16)  6.29 us
  transfers between devices with their start and end apart: 3, of which 1 were waited for; matrix products, arithmetic and copies ran while one was open for 2% of the time, Pallas kernels for 0%

commit v1 on v0

v1 whole, which is shorter than its diff:
```python
import functools
import math

import jax
import jax.numpy as jnp
import ml_dtypes
import numpy as np
from jax import lax
from jax.experimental import pallas as pl
from jax.experimental.pallas import tpu as pltpu
from jax.sharding import PartitionSpec as P

DEPTH = 512
BANDS = 4
REPEATS = 4
LANES = 128
HALO = 8
TAPS = (1.0 / 9.0, 2.0 / 9.0, 3.0 / 9.0, 2.0 / 9.0, 1.0 / 9.0)


def constants(samples):
    half = samples // 2
    distance = np.arange(half, dtype=np.float64)
    gauss = np.exp(-0.5 * (distance / (samples / 8)) ** 2)
    turn = 2.0 * np.pi * ((np.arange(half)[:, None] * np.arange(DEPTH)[None, :]) % samples) / samples
    even = gauss[:, None] * np.cos(turn)
    even[0] *= 0.5
    odd = gauss[:, None] * np.sin(turn)
    norms = []
    for band in range(BANDS):
        away = np.arange(samples) - (band + 0.5) * samples / BANDS
        window = np.where(np.abs(away) <= half, np.exp(-0.5 * (away / (samples / 8)) ** 2), 0.0)
        norms.append(float(1.0 / np.sum(window * window)))
    edge = float(np.exp(-0.5 * (half / (samples / 8)) ** 2))
    return even.astype(ml_dtypes.bfloat16), odd.astype(ml_dtypes.bfloat16), norms, edge


def maps_kernel(
    norms, edge, strips, info, bias, x_ref, scale_ref, halo_ref, even_ref, odd_ref,
    send_ref, keep_ref,
    even_in, odd_in, edge_in, power_ref, rough_ref, struct_ref,
):
    lines = LANES
    samples = x_ref.shape[-1]
    blocks = samples // LANES
    rows = REPEATS * (lines + HALO)
    lane = lax.broadcasted_iota(jnp.int32, (16, LANES), 1)
    mirror = jnp.where(lane == 0, 0, LANES - lane)
    sign = jnp.where(lane % 2 == 0, edge, -edge)

    def fold(values, row0):
        forward = [v.astype(jnp.bfloat16) for v in values]
        turned = [
            jnp.take_along_axis(v, mirror, axis=1, mode="promise_in_bounds") for v in values
        ]
        zero = jnp.zeros((16, LANES), jnp.float32)
        backward = []
        for i in range(blocks + 1):
            first = turned[blocks - i] if i > 0 else zero
            rest = turned[blocks - 1 - i] if i < blocks else zero
            backward.append(jnp.where(lane == 0, first, rest).astype(jnp.bfloat16))
        span = blocks // BANDS
        for band in range(BANDS):
            centre = span // 2 + span * band
            for i in range(blocks // 2):
                ahead = forward[centre + i] if centre + i < blocks else None
                j = blocks - centre + i
                behind = backward[j] if j <= blocks else None
                if behind is None:
                    plus, minus = ahead, ahead
                elif ahead is None:
                    plus, minus = behind, -behind
                else:
                    plus, minus = ahead + behind, ahead - behind
                at = (band, pl.ds(row0, 16), pl.ds(i * LANES, LANES))
                even_in[at] = plus
                odd_in[at] = minus
            far = centre + blocks // 2
            far = far if far < blocks else centre - blocks // 2
            value = forward[far].astype(jnp.float32)[:, :1]
            edge_in[band, pl.ds(row0, 16), :] = value * sign

    per = lines // 16

    def fold_group(g, carry):
        r, line0 = g // per, pl.multiple_of((g % per) * 16, 16)
        values = []
        for kb in range(blocks):
            v = x_ref[r, pl.ds(line0, 16), pl.ds(kb * LANES, LANES)].astype(jnp.float32)
            values.append(v * scale_ref[r, pl.ds(line0, 16), kb : kb + 1])
        fold(values, pl.multiple_of(g * 16, 16))
        return carry

    lax.fori_loop(0, REPEATS * per, fold_group, 0, unroll=2)
    for h in range(REPEATS * HALO // 16):
        fold(
            [halo_ref[h * 16 : h * 16 + 16, kb * LANES : (kb + 1) * LANES] for kb in range(blocks)],
            REPEATS * lines + h * 16,
        )

    for band in range(BANDS):
        re = jnp.dot(even_in[band], even_ref[...], preferred_element_type=jnp.float32)
        im = jnp.dot(odd_in[band], odd_ref[...], preferred_element_type=jnp.float32)
        extra = edge_in[band]
        extra = jnp.concatenate([extra] * (DEPTH // LANES), axis=1)
        re = re + extra
        power_ref[band] = re * re + im * im + 0.05 / norms[band]

    def finish(starts):
        ratio, total = None, None
        for band in range(BANDS):
            powers = [power_ref[band, pl.ds(s, 8), :] for s in starts]
            level = (powers[0] + powers[1]) + (powers[2] + powers[3])
            level = level * (norms[band] / (BANDS * REPEATS))
            total = level if total is None else total + level
            for p, q in zip(powers[:-1], powers[1:]):
                product, both = p * q, p + q
                part = product * lax.rsqrt(product * (both * both))
                ratio = part if ratio is None else ratio + part
        rough = 1.0 - ratio * (2.0 / (BANDS * (REPEATS - 1)))
        return rough, jnp.log(total + 0.05)

    def shut(values, first, last):
        out = []
        for zb in range(DEPTH // LANES):
            inside = jnp.logical_and(first <= zb, zb <= last)
            out.append(jnp.where(inside, values[:, zb * LANES : (zb + 1) * LANES], 0.0))
        return jnp.concatenate(out, axis=1)

    first, last = info[3], info[4]

    def finish_group(g, carry):
        line0 = pl.multiple_of(g * 8, 8)
        rough, struct = finish([r * lines + line0 for r in range(REPEATS)])
        rough_ref[pl.ds(line0 + 8, 8), :] = shut(rough, first, last)
        struct_ref[pl.ds(line0, 8), :] = struct
        return carry

    lax.fori_loop(0, lines // 8, finish_group, 0)
    rough, _ = finish([REPEATS * lines + r * HALO for r in range(REPEATS)])
    rough_ref[6:8, :] = shut(rough[0:2], info[1], info[2])
    rough_ref[8 + lines : 10 + lines, :] = shut(rough[2:4], info[5], info[6])

    chosen = struct_ref[:, pl.ds(pl.multiple_of(info[7] * LANES, LANES), LANES)]
    score = jnp.sum(chosen) * (1.0 / (LANES * lines)) + bias[0]
    smooth = TAPS[0] * rough_ref[6 : 6 + lines, :]
    for k in range(1, 5):
        smooth = smooth + TAPS[k] * rough_ref[6 + k : 6 + k + lines, :]
    maps = (smooth, shut(struct_ref[...], first, last))
    half = (send_ref.shape[0] - 8) // 2
    strip = DEPTH // strips
    low = info[8] == 0
    for m, whole in enumerate(maps):
        for zb in range(DEPTH // LANES):
            block = whole[:, zb * LANES : (zb + 1) * LANES].T
            for s in range(LANES // (2 * strip)):
                a = block[2 * s * strip : (2 * s + 1) * strip]
                b = block[(2 * s + 1) * strip : (2 * s + 2) * strip]
                at = m * half + zb * (LANES // 2) + s * strip
                keep_ref[at : at + strip, :] = jnp.where(low, a, b)
                send_ref[at : at + strip, :] = jnp.where(low, b, a)
    row = jnp.full((8, lines), score, jnp.float32)
    keep_ref[2 * half :, :] = row
    send_ref[2 * half :, :] = row


def maps_call(info, bias, spectra, scales, halo, even, odd, norms, edge, strips):
    samples = spectra.shape[-1]
    rows = REPEATS * (LANES + HALO)
    out = jax.ShapeDtypeStruct((DEPTH + 8, LANES), jnp.float32)
    half = samples // 2
    return pl.pallas_call(
        functools.partial(maps_kernel, norms, edge, strips),
        grid_spec=pltpu.PrefetchScalarGridSpec(
            num_scalar_prefetch=2,
            grid=(1,),
            in_specs=[
                pl.BlockSpec((REPEATS, LANES, samples), lambda i, info, bias: (0, info[0], 0)),
                pl.BlockSpec((REPEATS, LANES, samples // LANES), lambda i, info, bias: (0, info[0], 0)),
                pl.BlockSpec((REPEATS * HALO, samples), lambda i, info, bias: (0, 0)),
                pl.BlockSpec((half, DEPTH), lambda i, info, bias: (0, 0)),
                pl.BlockSpec((half, DEPTH), lambda i, info, bias: (0, 0)),
            ],
            out_specs=[pl.BlockSpec((DEPTH + 8, LANES), lambda i, info, bias: (0, 0))] * 2,
            scratch_shapes=[
                pltpu.VMEM((BANDS, rows, half), jnp.bfloat16),
                pltpu.VMEM((BANDS, rows, half), jnp.bfloat16),
                pltpu.VMEM((BANDS, rows, LANES), jnp.float32),
                pltpu.VMEM((BANDS, rows, DEPTH), jnp.float32),
                pltpu.VMEM((LANES + 16, DEPTH), jnp.float32),
                pltpu.VMEM((LANES, DEPTH), jnp.float32),
            ],
        ),
        out_shape=[out, out],
        compiler_params=pltpu.CompilerParams(vmem_limit_bytes=48 * 1024 * 1024),
        name="maps",
    )(info, bias, spectra, scales, halo, even, odd)


def part_rows(half):
    return 3 * half + 16


def merged(stage_raw, keep_ref, recv_ref, rows):
    if stage_raw:
        half = rows
        top_a, top_b = keep_ref[2 * half : 2 * half + 1], recv_ref[2 * half : 2 * half + 1]
        top = jnp.maximum(top_a, top_b)
        wa, wb = jnp.exp(top_a - top), jnp.exp(top_b - top)
        sa, sb = keep_ref[:half], recv_ref[:half]
        first = wa * sa
        other = wb * sb
        maps = [
            first + other,
            first * sa + other * sb,
            wa * keep_ref[half : 2 * half] + wb * recv_ref[half : 2 * half],
        ]
        return maps, top, wa + wb
    at = 3 * rows
    top_a, top_b = keep_ref[at : at + 1], recv_ref[at : at + 1]
    top = jnp.maximum(top_a, top_b)
    wa, wb = jnp.exp(top_a - top), jnp.exp(top_b - top)
    maps = [
        wa * keep_ref[m * rows : (m + 1) * rows] + wb * recv_ref[m * rows : (m + 1) * rows]
        for m in range(3)
    ]
    return maps, top, wa * keep_ref[at + 8 : at + 9] + wb * recv_ref[at + 8 : at + 9]


def merge_kernel(stage_raw, rows, strip, bit, keep_ref, recv_ref, send_out, keep_out):
    maps, top, weight = merged(stage_raw, keep_ref, recv_ref, rows)
    low = bit[0] == 0
    half = rows // 2
    for m, whole in enumerate(maps):
        for s in range(half // strip):
            a = whole[2 * s * strip : (2 * s + 1) * strip]
            b = whole[(2 * s + 1) * strip : (2 * s + 2) * strip]
            at = m * half + s * strip
            keep_out[at : at + strip] = jnp.where(low, a, b)
            send_out[at : at + strip] = jnp.where(low, b, a)
    tail = 3 * half
    for out in (keep_out, send_out):
        out[tail : tail + 8] = jnp.broadcast_to(top, (8, LANES))
        out[tail + 8 : tail + 16] = jnp.broadcast_to(weight, (8, LANES))


def merge_call(bit, keep, recv, rows, strip, stage_raw):
    out = jax.ShapeDtypeStruct((part_rows(rows // 2), LANES), jnp.float32)
    whole = pl.BlockSpec(memory_space=pltpu.VMEM)
    return pl.pallas_call(
        functools.partial(merge_kernel, stage_raw, rows, strip),
        in_specs=[pl.BlockSpec(memory_space=pltpu.SMEM), whole, whole],
        out_specs=[whole, whole],
        out_shape=[out, out],
        name="merge",
    )(bit, keep, recv)


def final_kernel(stage_raw, rows, count, order, *refs):
    keeps, recvs = refs[:count], refs[count : 2 * count]
    angio_ref, joined_ref, spread_ref = refs[2 * count :]
    for i in range(count):
        maps, _, weight = merged(stage_raw, keeps[i], recvs[i], rows)
        scale = 1.0 / weight
        mean = maps[0] * scale
        columns = pl.ds(pl.multiple_of(order[i] * LANES, LANES), LANES)
        angio_ref[:, columns] = mean
        joined_ref[:, columns] = maps[2] * scale
        spread_ref[:, columns] = jnp.sqrt(maps[1] * scale - mean * mean + 0.01)


def final_call(order, keeps, recvs, rows, stage_raw):
    count = len(keeps)
    whole = pl.BlockSpec(memory_space=pltpu.VMEM)
    out = jax.ShapeDtypeStruct((rows, count * LANES), jnp.float32)
    return pl.pallas_call(
        functools.partial(final_kernel, stage_raw, rows, count),
        in_specs=[pl.BlockSpec(memory_space=pltpu.SMEM)] + [whole] * (2 * count),
        out_specs=[whole] * 3,
        out_shape=[out] * 3,
        name="final",
    )(order, *keeps, *recvs)


def scaled_lines(spectra, scales, start):
    lines = lax.dynamic_slice_in_dim(spectra, start, 2, axis=1).astype(jnp.float32)
    level = lax.dynamic_slice_in_dim(scales, start, 2, axis=1)
    shaped = lines.reshape(level.shape + (-1,)) * level[..., None]
    return shaped.reshape(lines.shape)


def on_device(tiles, strips, spectra, scales, retina, quality, bias):
    spectra, scales, quality, bias = spectra[0], scales[0], quality[0], bias[0]
    samples = spectra.shape[-1]
    count = retina.shape[0]
    even, odd, norms, edge = constants(samples)
    even, odd = jnp.asarray(even), jnp.asarray(odd)
    here = lax.axis_index("tile")
    vol = lax.axis_index("vol")
    lines = spectra.shape[1]
    none = jnp.array([1 << 20, -1], jnp.int32)

    def packed(start, block):
        rows = scaled_lines(spectra, scales, start).reshape(-1, samples)
        extra = jnp.broadcast_to(block.astype(jnp.float32)[:, None], (2, samples))
        return jnp.concatenate([rows, extra], axis=0)

    def unpacked(array):
        block = array[-2:, 0].astype(jnp.int32)
        return array[:-2].reshape(REPEATS, 2, samples), block

    if tiles == 2:
        flip = here == 1
        start = jnp.where(flip, 0, lines - 2)
        own = packed(start, jnp.where(flip, retina[0], retina[count - 1]))
        ahead, block = unpacked(lax.ppermute(own, "tile", [(0, 1), (1, 0)]))
        before, before_block, after, after_block = ahead, block, ahead, block
        outside = [(False, False)] * (count - 1) + [(True, True)]
    else:
        flip = here < 0
        up = [(i, i + 1) for i in range(tiles - 1)]
        down = [(i + 1, i) for i in range(tiles - 1)]
        before, before_block = unpacked(
            lax.ppermute(packed(lines - 2, retina[count - 1]), "tile", up)
        )
        after, after_block = unpacked(lax.ppermute(packed(0, retina[0]), "tile", down))
        outside = [(i == 0, i == count - 1) for i in range(count)]
    before_block = jnp.where(here == 0, none, before_block)
    after_block = jnp.where(here == tiles - 1, none, after_block)

    bits = strips.bit_length() - 1
    order, keeps, sends = [], [], []
    for i in range(count):
        t = jnp.where(flip, count - 1 - i, i)
        order.append(t)
        prev_line = jnp.maximum(t * LANES - 2, 0)
        next_line = jnp.minimum(t * LANES + LANES, lines - 2)
        prev = scaled_lines(spectra, scales, prev_line)
        nxt = scaled_lines(spectra, scales, next_line)
        prev_block = lax.dynamic_index_in_dim(retina, jnp.maximum(t - 1, 0), 0, False)
        next_block = lax.dynamic_index_in_dim(retina, jnp.minimum(t + 1, count - 1), 0, False)
        if outside[i][0]:
            prev = jnp.where(t == 0, before, prev)
            prev_block = jnp.where(t == 0, before_block, prev_block)
        else:
            prev_block = jnp.where(t == 0, none, prev_block)
        if outside[i][1]:
            nxt = jnp.where(t == count - 1, after, nxt)
            next_block = jnp.where(t == count - 1, after_block, next_block)
        else:
            next_block = jnp.where(t == count - 1, none, next_block)
        halo = jnp.concatenate([prev, nxt, jnp.zeros((REPEATS, HALO - 4, samples), jnp.float32)], axis=1)
        block = lax.dynamic_index_in_dim(retina, t, 0, False)
        pick = lax.dynamic_index_in_dim(quality, t, 0)
        info = jnp.concatenate(
            [t[None], prev_block, block, next_block, pick, (vol & 1)[None]]
        ).astype(jnp.int32)
        send, keep = maps_call(
            info, lax.dynamic_index_in_dim(bias, t, 0), spectra, scales,
            halo.reshape(REPEATS * HALO, samples), even, odd, norms, edge, strips,
        )
        keeps.append(keep)
        sends.append(send)

    strip = DEPTH // strips
    rows = DEPTH // 2
    for stage in range(bits):
        pairs = [(v, v ^ (1 << stage)) for v in range(strips)]
        recvs = [lax.ppermute(s, "vol", pairs) for s in sends]
        if stage == bits - 1:
            return tuple(final_call(jnp.stack(order), keeps, recvs, rows, stage == 0))
        bit = ((vol >> (stage + 1)) & 1)[None]
        both = [
            merge_call(bit, k, r, rows, strip, stage == 0) for k, r in zip(keeps, recvs)
        ]
        sends, keeps = [b[0] for b in both], [b[1] for b in both]
        rows //= 2


def solution(mesh):
    return jax.shard_map(
        functools.partial(on_device, mesh.shape["tile"], mesh.shape["vol"]),
        mesh=mesh,
        in_specs=(
            P(("study", "vol"), None, "tile", None),
            P(("study", "vol"), None, "tile", None),
            P(("study", "tile"), None),
            P(("study", "vol"), "tile"),
            P(("study", "vol"), "tile"),
        ),
        out_specs=(P(("study", "vol"), "tile"),) * 3,
        check_vma=False,
    )
```

time: 234 us -> 99.9 us (0.43)
  other arithmetic: 72.3 us -> 5.65 us
  waiting for transfers between devices: 66.5 us -> 7.63 us
  Pallas kernels: 0 us -> 55.7 us
  matrix products: 36.1 us -> 0 us
  blocking collectives: 21.5 us -> 0 us
  between operations: 14.3 us -> 0.89 us
  starting transfers between devices: 3.69 us -> 14.1 us
  local copies, waits for them, and re-layouts: 18.8 us -> 15.3 us
    reduce_scatter x1 -> x0, waiting for transfers between devices: 66.5 us -> none  [on_device(): lax.psum_scatter(stacked, 'vol', scatter_dimension=1, tiled=True)]
    pallas_call x0 -> x10, Pallas kernels: none -> 55.7 us  [the longest x3 42.9 us: maps_call(): pl.pallas_call(functools.partial(maps_kernel, norms, edge, strips), grid_...]
    dot_general x4 -> x0, matrix products: 36.1 us -> none  [band_maps(): jnp.einsum('kcd,rak->cdra', tables[band_index], scaled, preferred_element...]
    all_gather x1 -> x0, blocking collectives: 21.5 us -> none  [on_device(): scores = lax.all_gather(volume_score[None, :], 'vol', axis=0, tiled=True)]
    reduce_sum x12 -> x0, other arithmetic: 19.2 us -> none  [the longest x4 16.5 us: band_maps(): decorrelation = decorrelation + jnp.sum(1.0 - pair_ratio, axis=1)]
    neg x1 -> x0, other arithmetic: 17.7 us -> none  [window_tables(): kernel = jnp.stack([jnp.cos(phase_angle), -jnp.sin(phase_angle)], axis=1)]
    sqrt x5 -> x0, other arithmetic: 14.1 us -> none  [the longest x4 12.4 us: band_maps(): amplitude = jnp.sqrt(band_power + 0.05)]
    convert_element_type x3 -> x2, other arithmetic: 12.2 us -> 0.95 us  [the longest x1 0.94 us: scaled_lines(): lax.dynamic_slice_in_dim(spectra, start, 2, axis=1).astype(jnp.float32)]
  transfers between devices with their start and end apart: 3 -> 10, of which waited for: 1 -> 4; matrix products, arithmetic and copies ran while one was open for 2% -> 7% of each run, Pallas kernels for 0% -> 39%
where the time goes in v1:
time: 99.9 us; the launch traced here: 99.3 us
  Pallas kernels  55.7 us (56%)
  local copies, waits for them, and re-layouts  15.3 us (15%)
  starting transfers between devices  14.1 us (14%)
  waiting for transfers between devices  7.63 us (8%)
  other arithmetic  5.65 us (6%)
    pallas_call x3, Pallas kernels, maps_call(): pl.pallas_call(functools.partial(maps_kernel, norms, edge, strips), grid_...  42.9 us
    ppermute x9, starting transfers between devices, on_device(): recvs = [lax.ppermute(s, 'vol', pairs) for s in sends]  13.5 us
    pallas_call x6, Pallas kernels, merge_call(): pl.pallas_call(functools.partial(merge_kernel, stage_raw, rows, strip), i...  10.9 us
    ppermute x9, waiting for transfers between devices, on_device(): recvs = [lax.ppermute(s, 'vol', pairs) for s in sends]  7.62 us
    unnamed x25, local copies, waits for them, and re-layouts  6.58 us
    concatenate x3, local copies, waits for them, and re-layouts, on_device(): jnp.concatenate([t[None], prev_block, block, next_block, pick, (vol & 1)[...  2.14 us
  transfers between devices with their start and end apart: 10, of which 4 were waited for; matrix products, arithmetic and copies ran while one was open for 7% of the time, Pallas kernels for 39%

profile of v1, /device:TPU:0, one launch (start us, length us, event | category | flops | bytes accessed | tf_op | source)
XLA Modules:
  0.0 99.3 jit_solution(7647966563270699075)
XLA Ops:
  0.7 1.2 %constant_dynamic-slice_fusion.1 = (f32[1,4,2,16]{2,3,1,0:T(8,128)S(1)}, f32[1,4,2,16]{2,3,1,0:T(8,128)S(1)}, f32[1,4,2,16]{2,3,1,0:T(8,128)S(1)}, f32[1,4,2,16]...) fusion(f32[1,4,384,16]{2,3,1,0:T(8,128)} %param.9, ...), kind=kLoop, calls=%fused_computation.15 | loop fusion | bytes 7188 | tf_op jit(solution)/shard_map/dynamic_slice | solution.py:287
  1.9 0.1 copy.35
  2.0 0.9 dynamic-slice_convert_fusion
  3.0 1.4 %fusion.9 = (s32[2]{0:T(128)S(1)}, s32[2]{0:T(128)S(1)}, s32[2]{0:T(128)S(1)}, s32[2]{0:T(128)S(1)}, s32[2]{0:T(128)S(1)}, /*index=5*/s32[2]{0:T(128)S(1)}, s32[2]{0:T(128)S(1)}, s32[2]{0:T(128)S(1)}, s32[2]{0:T(128)S(1)}) fusion(s32[3,2]{0,1:T(2,128)} %param.10, s32[]{:T(128)S(6)} %select_n.138, s32[]{:T(128)S(6)} %max.16, s32[1,2]{0,1:T(2,128)} %constant.127, ...), kind=kLoop, calls=%fused_computation.36 | loop fusion | flops 4 | bytes 178 | tf_op jit(solution)/shard_map/jit(dynamic_index_in_dim)/dynamic_slice | solution.py:341
  4.7 0.5 collective-permute-start.4
  5.2 1.2 %copy.30 = f32[1,4,384,16]{3,2,1,0:T(8,128)S(1)} copy(f32[1,4,384,16]{2,3,1,0:T(8,128)} %param.9) | data formatting | bytes 196608 | tf_op args[1]
  6.3 0.1 copy.31
  6.6 0.1 copy.32
  7.8 1.4 %constant_dynamic-slice_fusion.3 = (s32[1,1]{1,0:T(1,128)}, s32[1,1]{1,0:T(1,128)}, s32[1,1]{1,0:T(1,128)}) fusion(s32[1,3]{1,0:T(1,128)} %param.11, s32[]{:T(128)} %select_n.122, s32[]{:T(128)} %select_n.121), kind=kLoop, calls=%fused_computation.17 | loop fusion | bytes 32 | tf_op jit(solution)/shard_map/jit(dynamic_index_in_dim)/dynamic_slice | solution.py:354
  9.2 0.7 concatenate.23.info
  9.9 0.7 concatenate.21.info
  10.6 1.4 %constant_dynamic-slice_fusion.2 = (f32[1,1]{1,0:T(1,128)}, f32[1,1]{1,0:T(1,128)}, f32[1,1]{1,0:T(1,128)}) fusion(f32[1,3]{1,0:T(1,128)} %param.12, s32[]{:T(128)} %select_n.122, s32[]{:T(128)} %select_n.121), kind=kLoop, calls=%fused_computation.16 | loop fusion | bytes 32 | tf_op jit(solution)/shard_map/jit(dynamic_index_in_dim)/dynamic_slice | solution.py:359
  12.0 0.8 slice.20
  12.9 0.8 select_reduce_fusion
  13.8 0.7 concatenate.26.info
  14.5 1.6 %fusion.1 = (f32[4,2,2048]{2,1,0:T(2,128)S(1)}, f32[4,2,2048]{2,1,0:T(2,128)S(1)}, f32[4,2,2048]{2,1,0:T(2,128)S(1)}, f32[4,2,2048]{2,1,0:T(2,128)S(1)}, f32[4,2...) fusion(f32[4,2,2048]{2,1,0:T(2,128)S(1)} %reshape.113, f32[4,2,2048]{2,1,0:T(2,128)S(1)} %mul.125, pred[]{:T(512)S(6)} %eq.26, ...), kind=kLoop, calls=%fused_computation.8 | loop fusion | flops 229376 | bytes 1048594 | tf_op jit(solution)/shard_map/jit(_where)/select_n | solution.py:343
  16.1 0.2 maximum_bitcast_fusion.2
  16.3 14.7 %maps.5 = (f32[520,128]{1,0:T(8,128)}, f32[520,128]{1,0:T(8,128)S(1)}) custom-call(s32[9]{0:T(128)S(1)} %concatenate.26.info, f32[1]{0:T(128)} %bitcast.23.bias, bf16[4,384,2048]{2,1,0:T(8,128)(2,1)} %bitcast.63, f32[4,384,16]{2,1,0:T(8,128)S(1)} %bitcast.60, f32[32,2048]{1,0:T(8,128)S(1)} %get-tuple-element.65.halo_ref, bf16[1024,512]{1,0:T(8,128)(2,1)S(1)} %copy-done, ...), custom_call_target="tpu_custom_call" | custom-call | tf_op jit(solution)/shard_map/maps/pallas_call | solution.py:172
  31.1 0.7 copy-done.4
  31.8 2.5 %collective-permute-start.5 = (f32[520,128]{1,0:T(8,128)}, f32[520,128]{1,0:T(8,128)}, u32[]{:S(2)}, u32[]{:S(2)}) collective-permute-start(f32[520,128]{1,0:T(8,128)} %get-tuple-element.32), channel_id=1, source_target_pairs={{0,2},{2,0},{4,6},{6,4},{8,10},{10,8},{12,14},{14,12},{1,3},{3,1},... | collective-permute-start | bytes 798728 | tf_op jit(solution)/shard_map/ppermute | solution.py:369
  34.3 14.1 %maps.4 = (f32[520,128]{1,0:T(8,128)S(1)}, f32[520,128]{1,0:T(8,128)S(1)}) custom-call(s32[9]{0:T(128)S(1)} %concatenate.23.info, f32[1]{0:T(128)} %bitcast.15.bias, bf16[4,384,2048]{2,1,0:T(8,128)(2,1)} %bitcast.64, f32[4,384,16]{2,1,0:T(8,128)S(1)} %bitcast.61, f32[32,2048]{1,0:T(8,128)S(1)} %get-tuple-element.66.halo_ref, bf16[1024,512]{1,0:T(8,128)(2,1)S(1)} %copy-done, ...), custom_call_target="tpu_custom_call" | custom-call | tf_op jit(solution)/shard_map/maps/pallas_call | solution.py:172
  48.4 0.7 copy-done.3
  49.1 14.1 %maps.3 = (f32[520,128]{1,0:T(8,128)S(1)}, f32[520,128]{1,0:T(8,128)S(1)}) custom-call(s32[9]{0:T(128)S(1)} %concatenate.21.info, f32[1]{0:T(128)} %bitcast.6.bias, bf16[4,384,2048]{2,1,0:T(8,128)(2,1)} %bitcast.65, f32[4,384,16]{2,1,0:T(8,128)S(1)} %bitcast.62, f32[32,2048]{1,0:T(8,128)S(1)} %get-tuple-element.67.halo_ref, bf16[1024,512]{1,0:T(8,128)(2,1)S(1)} %copy-done, ...), custom_call_target="tpu_custom_call" | custom-call | tf_op jit(solution)/shard_map/maps/pallas_call | solution.py:172
  63.2 0.7 copy-done.2
  63.9 2.0 %collective-permute-start = (f32[520,128]{1,0:T(8,128)S(1)}, f32[520,128]{1,0:T(8,128)S(1)}, u32[]{:S(2)}, u32[]{:S(2)}) collective-permute-start(f32[520,128]{1,0:T(8,128)S(1)} %get-tuple-element.22), channel_id=1, source_target_pairs={{0,2},{2,0},{4,6},{6,4},{8,10},{10,8},{12,14},{14,12},{1,3},{3,1},... | collective-permute-start | bytes 798728 | tf_op jit(solution)/shard_map/ppermute | solution.py:369
  65.9 1.9 %merge.10 = (f32[400,128]{1,0:T(8,128)}, f32[400,128]{1,0:T(8,128)}) custom-call(s32[1]{0:T(128)} %bitcast.3.bit, f32[520,128]{1,0:T(8,128)} %copy-done.4, f32[520,128]{1,0:T(8,128)} %collective-permute-done.5.recv_ref), custom_call_target="tpu_custom_call" | custom-call | tf_op jit(solution)/shard_map/merge/pallas_call | solution.py:250
  67.8 1.6 %collective-permute-start.6 = (f32[400,128]{1,0:T(8,128)}, f32[400,128]{1,0:T(8,128)S(1)}, u32[]{:S(2)}, u32[]{:S(2)}) collective-permute-start(f32[400,128]{1,0:T(8,128)} %get-tuple-element.34), channel_id=1, source_target_pairs={{0,4},{2,6},{4,0},{6,2},{8,12},{10,14},{12,8},{14,10},{1,5},{3,7},... | collective-permute-start | bytes 614408 | tf_op jit(solution)/shard_map/ppermute | solution.py:369
  69.4 1.9 %merge.8 = (f32[400,128]{1,0:T(8,128)}, f32[400,128]{1,0:T(8,128)}) custom-call(s32[1]{0:T(128)} %bitcast.3.bit, f32[520,128]{1,0:T(8,128)} %copy-done.3, f32[520,128]{1,0:T(8,128)} %collective-permute-done.2.recv_ref), custom_call_target="tpu_custom_call" | custom-call | tf_op jit(solution)/shard_map/merge/pallas_call | solution.py:250
  71.2 0.4 collective-permute-start.3
  71.7 0.7 collective-permute-done.recv_ref
  72.3 0.7 copy-done.5
  73.0 1.9 %merge.6 = (f32[400,128]{1,0:T(8,128)}, f32[400,128]{1,0:T(8,128)}) custom-call(s32[1]{0:T(128)} %bitcast.3.bit, f32[520,128]{1,0:T(8,128)} %copy-done.2, f32[520,128]{1,0:T(8,128)} %copy-done.5), custom_call_target="tpu_custom_call" | custom-call | tf_op jit(solution)/shard_map/merge/pallas_call | solution.py:250
  74.9 1.8 %collective-permute-start.1 = (f32[400,128]{1,0:T(8,128)}, f32[400,128]{1,0:T(8,128)S(1)}, u32[]{:S(2)}, u32[]{:S(2)}) collective-permute-start(f32[400,128]{1,0:T(8,128)} %get-tuple-element.24), channel_id=1, source_target_pairs={{0,4},{2,6},{4,0},{6,2},{8,12},{10,14},{12,8},{14,10},{1,5},{3,7},... | collective-permute-start | bytes 614408 | tf_op jit(solution)/shard_map/ppermute | solution.py:369
  76.7 0.7 copy-done.6
  77.4 1.8 %merge.11 = (f32[208,128]{1,0:T(8,128)}, f32[208,128]{1,0:T(8,128)}) custom-call(s32[1]{0:T(128)} %bitcast.2.bit, f32[400,128]{1,0:T(8,128)} %get-tuple-element.33.keep_ref, f32[400,128]{1,0:T(8,128)} %copy-done.6), custom_call_target="tpu_custom_call" | custom-call | tf_op jit(solution)/shard_map/merge/pallas_call | solution.py:250
  79.1 2.6 %collective-permute-start.9 = (f32[208,128]{1,0:T(8,128)}, f32[208,128]{1,0:T(8,128)S(1)}, u32[]{:S(2)}, u32[]{:S(2)}) collective-permute-start(f32[208,128]{1,0:T(8,128)} %get-tuple-element.38), channel_id=1, source_target_pairs={{0,8},{2,10},{4,12},{6,14},{8,0},{10,2},{12,4},{14,6},{1,9},{3,11}... | collective-permute-start | bytes 319496 | tf_op jit(solution)/shard_map/ppermute | solution.py:369
  81.7 0.7 copy-done.7
  82.4 1.8 %merge.9 = (f32[208,128]{1,0:T(8,128)}, f32[208,128]{1,0:T(8,128)}) custom-call(s32[1]{0:T(128)} %bitcast.2.bit, f32[400,128]{1,0:T(8,128)} %get-tuple-element.28.keep_ref, f32[400,128]{1,0:T(8,128)} %copy-done.7), custom_call_target="tpu_custom_call" | custom-call | tf_op jit(solution)/shard_map/merge/pallas_call | solution.py:250
  84.2 1.0 collective-permute-start.8
  85.1 0.4 collective-permute-done.1.recv_ref
  85.5 0.7 copy-done.8
  86.2 1.7 %merge.7 = (f32[208,128]{1,0:T(8,128)}, f32[208,128]{1,0:T(8,128)}) custom-call(s32[1]{0:T(128)} %bitcast.2.bit, f32[400,128]{1,0:T(8,128)} %get-tuple-element.23.keep_ref, f32[400,128]{1,0:T(8,128)} %copy-done.8), custom_call_target="tpu_custom_call" | custom-call | tf_op jit(solution)/shard_map/merge/pallas_call | solution.py:250
  87.9 1.6 %collective-permute-start.7 = (f32[208,128]{1,0:T(8,128)}, f32[208,128]{1,0:T(8,128)S(1)}, u32[]{:S(2)}, u32[]{:S(2)}) collective-permute-start(f32[208,128]{1,0:T(8,128)} %get-tuple-element.36), channel_id=1, source_target_pairs={{0,8},{2,10},{4,12},{6,14},{8,0},{10,2},{12,4},{14,6},{1,9},{3,11}... | collective-permute-start | bytes 319496 | tf_op jit(solution)/shard_map/ppermute | solution.py:369
  89.5 0.6 pad_add_fusion.order
  90.1 3.3 %collective-permute-done.8.refs_4_ = f32[208,128]{1,0:T(8,128)S(1)} collective-permute-done((f32[208,128]{1,0:T(8,128)}, f32[208,128]{1,0:T(8,128)S(1)}, u32[]{:S(2)}, u32[]{:S(2)}) %collective-permute-start.8) | collective-permute-done | bytes 106528 | tf_op jit(solution)/shard_map/ppermute | solution.py:369
  93.4 3.2 %collective-permute-done.7.refs_3_ = f32[208,128]{1,0:T(8,128)S(1)} collective-permute-done((f32[208,128]{1,0:T(8,128)}, f32[208,128]{1,0:T(8,128)S(1)}, u32[]{:S(2)}, u32[]{:S(2)}) %collective-permute-start.7) | collective-permute-done | bytes 106528 | tf_op jit(solution)/shard_map/ppermute | solution.py:369
  96.7 0.6 copy-done.11
  97.3 1.9 %final.1 = (f32[64,384]{1,0:T(8,128)}, f32[64,384]{1,0:T(8,128)}, f32[64,384]{1,0:T(8,128)}) custom-call(s32[3]{0:T(128)} %pad_add_fusion.order, f32[208,128]{1,0:T(8,128)} %get-tuple-element.25.refs_0_, f32[208,128]{1,0:T(8,128)} %get-tuple-element.30.refs_1_, f32[208,128]{1,0:T(8,128)} %get-tuple-element.35.refs_2_, f32[208,128]{1,0:T(8,128)} %copy-done.11, ...), custom_call_target="tpu_custom_call" | custom-call | tf_op jit(solution)/shard_map/final/pallas_call | solution.py:276
  (49 shorter events, 1.6 us)
Async XLA Ops:
  0.6 15.7 %copy-start = (bf16[1024,512]{1,0:T(8,128)(2,1)S(1)}, bf16[1024,512]{1,0:T(8,128)(2,1)}, u32[]{:S(2)}) copy-start(bf16[1024,512]{1,0:T(8,128)(2,1)} %constant.119.clone.even_ref) | copy-start | bytes 3145732
  0.6 15.7 %copy-start.1 = (bf16[1024,512]{1,0:T(8,128)(2,1)S(1)}, bf16[1024,512]{1,0:T(8,128)(2,1)}, u32[]{:S(2)}) copy-start(bf16[1024,512]{1,0:T(8,128)(2,1)} %constant.120.clone.odd_ref) | copy-start | bytes 3145732
  4.7 7.4 %collective-permute-start.4 = (f32[10,2048]{1,0:T(8,128)S(1)}, f32[10,2048]{1,0:T(8,128)}, u32[]{:S(2)}, u32[]{:S(2)}) collective-permute-start(f32[10,2048]{1,0:T(8,128)S(1)} %pad_maximum_fusion), channel_id=1, source_target_pairs={{0,1},{1,0},{2,3},{3,2},{4,5},{5,4},{6,7},{7,6},{8,9},{9,8},{10,11... | collective-permute-start | bytes 245768 | tf_op jit(solution)/shard_map/ppermute | solution.py:316
  31.1 0.7 copy-start.4
  31.8 34.1 %collective-permute-start.5 = (f32[520,128]{1,0:T(8,128)}, f32[520,128]{1,0:T(8,128)}, u32[]{:S(2)}, u32[]{:S(2)}) collective-permute-start(f32[520,128]{1,0:T(8,128)} %get-tuple-element.32), channel_id=1, source_target_pairs={{0,2},{2,0},{4,6},{6,4},{8,10},{10,8},{12,14},{14,12},{1,3},{3,1},... | collective-permute-start | bytes 798728 | tf_op jit(solution)/shard_map/ppermute | solution.py:369
  48.4 0.7 copy-start.3
  49.1 20.3 %collective-permute-start.2 = (f32[520,128]{1,0:T(8,128)S(1)}, f32[520,128]{1,0:T(8,128)}, u32[]{:S(2)}, u32[]{:S(2)}) collective-permute-start(f32[520,128]{1,0:T(8,128)S(1)} %get-tuple-element.27), channel_id=1, source_target_pairs={{0,2},{2,0},{4,6},{6,4},{8,10},{10,8},{12,14},{14,12},{1,3},{3,1},... | collective-permute-start | bytes 798728 | tf_op jit(solution)/shard_map/ppermute | solution.py:369
  63.2 0.7 copy-start.2
  63.9 8.5 %collective-permute-start = (f32[520,128]{1,0:T(8,128)S(1)}, f32[520,128]{1,0:T(8,128)S(1)}, u32[]{:S(2)}, u32[]{:S(2)}) collective-permute-start(f32[520,128]{1,0:T(8,128)S(1)} %get-tuple-element.22), channel_id=1, source_target_pairs={{0,2},{2,0},{4,6},{6,4},{8,10},{10,8},{12,14},{14,12},{1,3},{3,1},... | collective-permute-start | bytes 798728 | tf_op jit(solution)/shard_map/ppermute | solution.py:369
  67.8 8.9 %collective-permute-start.6 = (f32[400,128]{1,0:T(8,128)}, f32[400,128]{1,0:T(8,128)S(1)}, u32[]{:S(2)}, u32[]{:S(2)}) collective-permute-start(f32[400,128]{1,0:T(8,128)} %get-tuple-element.34), channel_id=1, source_target_pairs={{0,4},{2,6},{4,0},{6,2},{8,12},{10,14},{12,8},{14,10},{1,5},{3,7},... | collective-permute-start | bytes 614408 | tf_op jit(solution)/shard_map/ppermute | solution.py:369
  71.2 10.5 %collective-permute-start.3 = (f32[400,128]{1,0:T(8,128)}, f32[400,128]{1,0:T(8,128)S(1)}, u32[]{:S(2)}, u32[]{:S(2)}) collective-permute-start(f32[400,128]{1,0:T(8,128)} %get-tuple-element.29), channel_id=1, source_target_pairs={{0,4},{2,6},{4,0},{6,2},{8,12},{10,14},{12,8},{14,10},{1,5},{3,7},... | collective-permute-start | bytes 614408 | tf_op jit(solution)/shard_map/ppermute | solution.py:369
  72.3 0.7 copy-start.5
  74.9 10.6 %collective-permute-start.1 = (f32[400,128]{1,0:T(8,128)}, f32[400,128]{1,0:T(8,128)S(1)}, u32[]{:S(2)}, u32[]{:S(2)}) collective-permute-start(f32[400,128]{1,0:T(8,128)} %get-tuple-element.24), channel_id=1, source_target_pairs={{0,4},{2,6},{4,0},{6,2},{8,12},{10,14},{12,8},{14,10},{1,5},{3,7},... | collective-permute-start | bytes 614408 | tf_op jit(solution)/shard_map/ppermute | solution.py:369
  76.7 0.7 copy-start.6
  79.1 11.0 %collective-permute-start.9 = (f32[208,128]{1,0:T(8,128)}, f32[208,128]{1,0:T(8,128)S(1)}, u32[]{:S(2)}, u32[]{:S(2)}) collective-permute-start(f32[208,128]{1,0:T(8,128)} %get-tuple-element.38), channel_id=1, source_target_pairs={{0,8},{2,10},{4,12},{6,14},{8,0},{10,2},{12,4},{14,6},{1,9},{3,11}... | collective-permute-start | bytes 319496 | tf_op jit(solution)/shard_map/ppermute | solution.py:369
  81.7 0.7 copy-start.7
  84.2 9.3 %collective-permute-start.8 = (f32[208,128]{1,0:T(8,128)}, f32[208,128]{1,0:T(8,128)S(1)}, u32[]{:S(2)}, u32[]{:S(2)}) collective-permute-start(f32[208,128]{1,0:T(8,128)} %get-tuple-element.37), channel_id=1, source_target_pairs={{0,8},{2,10},{4,12},{6,14},{8,0},{10,2},{12,4},{14,6},{1,9},{3,11}... | collective-permute-start | bytes 319496 | tf_op jit(solution)/shard_map/ppermute | solution.py:369
  85.5 0.7 copy-start.8
  87.9 8.8 %collective-permute-start.7 = (f32[208,128]{1,0:T(8,128)}, f32[208,128]{1,0:T(8,128)S(1)}, u32[]{:S(2)}, u32[]{:S(2)}) collective-permute-start(f32[208,128]{1,0:T(8,128)} %get-tuple-element.36), channel_id=1, source_target_pairs={{0,8},{2,10},{4,12},{6,14},{8,0},{10,2},{12,4},{14,6},{1,9},{3,11}... | collective-permute-start | bytes 319496 | tf_op jit(solution)/shard_map/ppermute | solution.py:369
  90.1 6.6 %copy-start.9 = (f32[208,128]{1,0:T(8,128)}, f32[208,128]{1,0:T(8,128)S(1)}, u32[]{:S(2)}) copy-start(f32[208,128]{1,0:T(8,128)S(1)} %collective-permute-done.9.refs_5_) | copy-start | bytes 319492
  93.4 3.3 %copy-start.10 = (f32[208,128]{1,0:T(8,128)}, f32[208,128]{1,0:T(8,128)S(1)}, u32[]{:S(2)}) copy-start(f32[208,128]{1,0:T(8,128)S(1)} %collective-permute-done.8.refs_4_) | copy-start | bytes 319492
  96.7 0.6 copy-start.11

commit v2 on v1

v2 whole, which is shorter than its diff:
```python
import functools
import math

import jax
import jax.numpy as jnp
import ml_dtypes
import numpy as np
from jax import lax
from jax.experimental import pallas as pl
from jax.experimental.pallas import tpu as pltpu
from jax.sharding import PartitionSpec as P

DEPTH = 512
BANDS = 4
REPEATS = 4
LANES = 128
HALO = 8
TAPS = (1.0 / 9.0, 2.0 / 9.0, 3.0 / 9.0, 2.0 / 9.0, 1.0 / 9.0)


def constants(samples):
    half = samples // 2
    distance = np.arange(half, dtype=np.float64)
    gauss = np.exp(-0.5 * (distance / (samples / 8)) ** 2)
    turn = 2.0 * np.pi * ((np.arange(half)[:, None] * np.arange(DEPTH)[None, :]) % samples) / samples
    even = gauss[:, None] * np.cos(turn)
    even[0] *= 0.5
    odd = gauss[:, None] * np.sin(turn)
    norms = []
    for band in range(BANDS):
        away = np.arange(samples) - (band + 0.5) * samples / BANDS
        window = np.where(np.abs(away) <= half, np.exp(-0.5 * (away / (samples / 8)) ** 2), 0.0)
        norms.append(float(1.0 / np.sum(window * window)))
    edge = float(np.exp(-0.5 * (half / (samples / 8)) ** 2))
    return even.astype(ml_dtypes.bfloat16), odd.astype(ml_dtypes.bfloat16), norms, edge


def maps_kernel(
    norms, edge, strips, step, count, outer, info, bias, x_hbm, scale_ref, ext_ref, even_hbm, odd_hbm,
    send_ref, keep_ref,
    rough_ref, struct_ref, x_ref, level_ref, near_ref, even_ref, odd_ref, sems, *scratch,
):
    lines = LANES
    samples = x_hbm.shape[-1]
    blocks = samples // LANES
    parts = lines // SUB
    rows = REPEATS * SUB
    flip = info[0]
    tile = jnp.where(flip == 1, count - 1 - step, step)
    lane = lax.broadcasted_iota(jnp.int32, (SUB, LANES), 1)
    mirror = jnp.where(lane == 0, 0, LANES - lane)
    sign = jnp.where(lane % 2 == 0, edge, -edge)

    line_count = x_hbm.shape[1]
    base = pl.multiple_of(tile * lines, lines)
    base_prev = pl.multiple_of(jnp.maximum(base - SUB, 0), SUB)
    base_next = pl.multiple_of(jnp.minimum(base + lines, line_count - SUB), SUB)
    own = pltpu.make_async_copy(
        x_hbm.at[:, pl.ds(base, lines), :], x_ref.at[:, :lines, :], sems.at[0]
    )
    tables = [
        pltpu.make_async_copy(even_hbm, even_ref, sems.at[1]),
        pltpu.make_async_copy(odd_hbm, odd_ref, sems.at[2]),
    ]
    edges = [
        pltpu.make_async_copy(x_hbm.at[:, pl.ds(start, SUB), :], near_ref.at[n], sems.at[3 + n])
        for n, start in enumerate((base_prev, base_next))
    ]
    for copy in [own] + edges + tables:
        copy.start()

    at_start, at_end = tile == 0, tile == count - 1
    whole_prev = pl.ds(pl.multiple_of(jnp.maximum(base - lines, 0), lines), lines)
    whole_next = pl.ds(pl.multiple_of(jnp.minimum(base + lines, line_count - lines), lines), lines)

    def placed(values, at):
        above = jnp.zeros((at, values.shape[1]), values.dtype)
        below = jnp.zeros((SUB - 2 - at, values.shape[1]), values.dtype)
        return jnp.concatenate([piece for piece in (above, values, below) if piece.shape[0]], axis=0)

    row_of = lax.broadcasted_iota(jnp.int32, (SUB, blocks), 0)
    for r in range(REPEATS):
        level_ref[r, :lines, :] = scale_ref[r, :, pl.ds(base, lines)].T
        level_prev = scale_ref[r, :, whole_prev].T[lines - SUB :]
        level_next = scale_ref[r, :, whole_next].T[:SUB]
        outside = ext_ref[2 * r : 2 * r + 2, samples : samples + blocks]
        if outer[0]:
            level_prev = jnp.where(at_start, placed(outside, SUB - 2), level_prev)
        if outer[1]:
            level_next = jnp.where(at_end, placed(outside, 0), level_next)
        level_ref[r, lines:, :] = jnp.where(row_of < 2, level_next, level_prev)

    for copy in [own] + edges:
        copy.wait()
    for r in range(REPEATS):
        for kb in range(blocks):
            columns = slice(kb * LANES, (kb + 1) * LANES)
            a = near_ref[0, r, :, columns].astype(jnp.float32)
            b = near_ref[1, r, :, columns].astype(jnp.float32)
            if outer[0]:
                a = jnp.where(at_start, placed(ext_ref[2 * r : 2 * r + 2, columns], SUB - 2), a)
            if outer[1]:
                b = jnp.where(at_end, placed(ext_ref[2 * r : 2 * r + 2, columns], 0), b)
            low = lax.broadcasted_iota(jnp.int32, (SUB, LANES), 0) < 2
            x_ref[r, lines:, columns] = jnp.where(low, b, a).astype(jnp.bfloat16)

    def fold(s, buffers):
        even_in, odd_in, edge_in = buffers
        for r in range(REPEATS):
            at = pl.ds(pl.multiple_of(s * SUB, SUB), SUB)
            level = level_ref[r, at, :]
            values = [
                x_ref[r, at, kb * LANES : (kb + 1) * LANES].astype(jnp.float32)
                * level[:, kb : kb + 1]
                for kb in range(blocks)
            ]
            forward = [v.astype(jnp.bfloat16) for v in values]
            turned = [
                jnp.take_along_axis(v, mirror, axis=1, mode="promise_in_bounds") for v in values
            ]
            zero = jnp.zeros((SUB, LANES), jnp.float32)
            backward = []
            for i in range(blocks + 1):
                first = turned[blocks - i] if i > 0 else zero
                rest = turned[blocks - 1 - i] if i < blocks else zero
                backward.append(jnp.where(lane == 0, first, rest).astype(jnp.bfloat16))
            span = blocks // BANDS
            for band in range(BANDS):
                to = slice(band * rows + r * SUB, band * rows + r * SUB + SUB)
                centre = span // 2 + span * band
                for i in range(blocks // 2):
                    ahead = forward[centre + i] if centre + i < blocks else None
                    j = blocks - centre + i
                    behind = backward[j] if j <= blocks else None
                    if behind is None:
                        plus, minus = ahead, ahead
                    elif ahead is None:
                        plus, minus = behind, -behind
                    else:
                        plus, minus = ahead + behind, ahead - behind
                    even_in[to, i * LANES : (i + 1) * LANES] = plus
                    odd_in[to, i * LANES : (i + 1) * LANES] = minus
                far = centre + blocks // 2
                far = far if far < blocks else centre - blocks // 2
                edge_in[to, :] = forward[far].astype(jnp.float32)[:, :1] * sign

    def limits(t):
        return info[2 + 2 * t], info[3 + 2 * t]

    first, last = limits(tile)
    prev_first, prev_last = limits(jnp.maximum(tile - 1, 0))
    next_first, next_last = limits(jnp.minimum(tile + 1, count - 1))
    out_at = 2 + 3 * count
    prev_first = jnp.where(at_start, info[out_at] if outer[0] else 1 << 20, prev_first)
    prev_last = jnp.where(at_start, info[out_at + 1] if outer[0] else -1, prev_last)
    next_first = jnp.where(at_end, info[out_at + 2] if outer[1] else 1 << 20, next_first)
    next_last = jnp.where(at_end, info[out_at + 3] if outer[1] else -1, next_last)

    def shut(values, low, high, at=0):
        out = []
        for n in range(values.shape[1] // LANES):
            inside = jnp.logical_and(low <= at + n, at + n <= high)
            out.append(jnp.where(inside, values[:, n * LANES : (n + 1) * LANES], 0.0))
        return jnp.concatenate(out, axis=1)

    def finish(powers_of):
        ratio, total = None, None
        for band in range(BANDS):
            powers = [powers_of(band, r) for r in range(REPEATS)]
            level = (powers[0] + powers[1]) + (powers[2] + powers[3])
            level = level * (norms[band] / (BANDS * REPEATS))
            total = level if total is None else total + level
            for p, q in zip(powers[:-1], powers[1:]):
                product, both = p * q, p + q
                part = product * lax.rsqrt(product * (both * both))
                ratio = part if ratio is None else ratio + part
        rough = 1.0 - ratio * (2.0 / (BANDS * (REPEATS - 1)))
        return rough, jnp.log(total + 0.05)

    def dots(s, buffers, border):
        even_in, odd_in, edge_in = buffers
        wide = DEPTH // SPLIT
        for part in range(SPLIT):
            columns = slice(part * wide, (part + 1) * wide)
            re = jnp.dot(even_in[...], even_ref[:, columns], preferred_element_type=jnp.float32)
            im = jnp.dot(odd_in[...], odd_ref[:, columns], preferred_element_type=jnp.float32)
            block0 = part * (wide // LANES)
            for g in range(SUB // 8):

                def power(band, r):
                    at = slice(band * rows + r * SUB + g * 8, band * rows + r * SUB + g * 8 + 8)
                    extra = jnp.concatenate([edge_in[at]] * (wide // LANES), axis=1)
                    a, b = re[at] + extra, im[at]
                    return a * a + b * b + 0.05 / norms[band]

                rough, struct = finish(power)
                if border:
                    rough_ref[g * 8 : g * 8 + 8, columns] = shut(rough, prev_first, prev_last, block0)
                    at = SUB + lines + g * 8
                    rough_ref[at : at + 8, columns] = shut(rough, next_first, next_last, block0)
                else:
                    line0 = pl.multiple_of(s * SUB + g * 8, 8)
                    rough_ref[pl.ds(line0 + SUB, 8), columns] = shut(rough, first, last, block0)
                    struct_ref[pl.ds(line0, 8), columns] = struct

    bufs = [scratch[0:3], scratch[3:6]]
    fold(0, bufs[0])
    for copy in tables:
        copy.wait()

    def pair(i, carry):
        dots(2 * i, bufs[0], False)
        fold(2 * i + 1, bufs[1])
        dots(2 * i + 1, bufs[1], False)
        fold(2 * i + 2, bufs[0])
        return carry

    lax.fori_loop(0, parts // 2, pair, 0)
    dots(parts, bufs[0], True)

    pick = info[2 + 2 * count + tile]
    chosen = struct_ref[:, pl.ds(pl.multiple_of(pick * LANES, LANES), LANES)]
    score = jnp.sum(chosen) * (1.0 / (LANES * lines)) + bias[tile]
    smooth = TAPS[0] * rough_ref[SUB - 2 : SUB - 2 + lines, :]
    for k in range(1, 5):
        smooth = smooth + TAPS[k] * rough_ref[SUB - 2 + k : SUB - 2 + k + lines, :]
    maps = (smooth, shut(struct_ref[...], first, last))
    half = (send_ref.shape[0] - 8) // 2
    strip = DEPTH // strips
    low = info[1] % 2 == 0
    for m, whole in enumerate(maps):
        for zb in range(DEPTH // LANES):
            block = whole[:, zb * LANES : (zb + 1) * LANES].T
            for s in range(LANES // (2 * strip)):
                a = block[2 * s * strip : (2 * s + 1) * strip]
                b = block[(2 * s + 1) * strip : (2 * s + 2) * strip]
                at = m * half + zb * (LANES // 2) + s * strip
                keep_ref[at : at + strip, :] = jnp.where(low, a, b)
                send_ref[at : at + strip, :] = jnp.where(low, b, a)
    row = jnp.full((8, lines), score, jnp.float32)
    keep_ref[2 * half :, :] = row
    send_ref[2 * half :, :] = row


SUB = 16
SPLIT = 2


def maps_call(step, count, outer, info, bias, spectra, scales, ext, even, odd, norms, edge, strips):
    samples = spectra.shape[-1]
    rows = BANDS * REPEATS * SUB
    out = jax.ShapeDtypeStruct((DEPTH + 8, LANES), jnp.float32)
    half = samples // 2
    whole = pl.BlockSpec(memory_space=pltpu.VMEM)
    remote = pl.BlockSpec(memory_space=pl.ANY)
    pair = [
        pltpu.VMEM((rows, half), jnp.bfloat16),
        pltpu.VMEM((rows, half), jnp.bfloat16),
        pltpu.VMEM((rows, LANES), jnp.float32),
    ]
    return pl.pallas_call(
        functools.partial(maps_kernel, norms, edge, strips, step, count, outer),
        in_specs=[pl.BlockSpec(memory_space=pltpu.SMEM)] * 2 + [remote, whole, whole, remote, remote],
        out_specs=[whole] * 2,
        scratch_shapes=[
            pltpu.VMEM((LANES + 2 * SUB, DEPTH), jnp.float32),
            pltpu.VMEM((LANES, DEPTH), jnp.float32),
            pltpu.VMEM((REPEATS, LANES + SUB, samples), jnp.bfloat16),
            pltpu.VMEM((REPEATS, LANES + SUB, samples // LANES), jnp.float32),
            pltpu.VMEM((2, REPEATS, SUB, samples), jnp.bfloat16),
            pltpu.VMEM((half, DEPTH), jnp.bfloat16),
            pltpu.VMEM((half, DEPTH), jnp.bfloat16),
            pltpu.SemaphoreType.DMA((5,)),
        ] + pair + pair,
        out_shape=[out, out],
        compiler_params=pltpu.CompilerParams(vmem_limit_bytes=48 * 1024 * 1024),
        name="maps",
    )(info, bias, spectra, jnp.swapaxes(scales, 1, 2), ext, even, odd)


def part_rows(half):
    return 3 * half + 16


def merged(stage_raw, keep_ref, recv_ref, rows):
    if stage_raw:
        half = rows
        top_a, top_b = keep_ref[2 * half : 2 * half + 1], recv_ref[2 * half : 2 * half + 1]
        top = jnp.maximum(top_a, top_b)
        wa, wb = jnp.exp(top_a - top), jnp.exp(top_b - top)
        sa, sb = keep_ref[:half], recv_ref[:half]
        first = wa * sa
        other = wb * sb
        maps = [
            first + other,
            first * sa + other * sb,
            wa * keep_ref[half : 2 * half] + wb * recv_ref[half : 2 * half],
        ]
        return maps, top, wa + wb
    at = 3 * rows
    top_a, top_b = keep_ref[at : at + 1], recv_ref[at : at + 1]
    top = jnp.maximum(top_a, top_b)
    wa, wb = jnp.exp(top_a - top), jnp.exp(top_b - top)
    maps = [
        wa * keep_ref[m * rows : (m + 1) * rows] + wb * recv_ref[m * rows : (m + 1) * rows]
        for m in range(3)
    ]
    return maps, top, wa * keep_ref[at + 8 : at + 9] + wb * recv_ref[at + 8 : at + 9]


def merge_kernel(stage_raw, rows, strip, bit, keep_ref, recv_ref, send_out, keep_out):
    maps, top, weight = merged(stage_raw, keep_ref, recv_ref, rows)
    low = bit[0] == 0
    half = rows // 2
    for m, whole in enumerate(maps):
        for s in range(half // strip):
            a = whole[2 * s * strip : (2 * s + 1) * strip]
            b = whole[(2 * s + 1) * strip : (2 * s + 2) * strip]
            at = m * half + s * strip
            keep_out[at : at + strip] = jnp.where(low, a, b)
            send_out[at : at + strip] = jnp.where(low, b, a)
    tail = 3 * half
    for out in (keep_out, send_out):
        out[tail : tail + 8] = jnp.broadcast_to(top, (8, LANES))
        out[tail + 8 : tail + 16] = jnp.broadcast_to(weight, (8, LANES))


def merge_call(bit, keep, recv, rows, strip, stage_raw):
    out = jax.ShapeDtypeStruct((part_rows(rows // 2), LANES), jnp.float32)
    whole = pl.BlockSpec(memory_space=pltpu.VMEM)
    return pl.pallas_call(
        functools.partial(merge_kernel, stage_raw, rows, strip),
        in_specs=[pl.BlockSpec(memory_space=pltpu.SMEM), whole, whole],
        out_specs=[whole, whole],
        out_shape=[out, out],
        name="merge",
    )(bit, keep, recv)


def final_kernel(stage_raw, rows, count, order, *refs):
    keeps, recvs = refs[:count], refs[count : 2 * count]
    angio_ref, joined_ref, spread_ref = refs[2 * count :]
    for i in range(count):
        maps, _, weight = merged(stage_raw, keeps[i], recvs[i], rows)
        scale = 1.0 / weight
        mean = maps[0] * scale
        columns = pl.ds(pl.multiple_of(order[i] * LANES, LANES), LANES)
        angio_ref[:, columns] = mean
        joined_ref[:, columns] = maps[2] * scale
        spread_ref[:, columns] = jnp.sqrt(maps[1] * scale - mean * mean + 0.01)


def final_call(order, keeps, recvs, rows, stage_raw):
    count = len(keeps)
    whole = pl.BlockSpec(memory_space=pltpu.VMEM)
    out = jax.ShapeDtypeStruct((rows, count * LANES), jnp.float32)
    return pl.pallas_call(
        functools.partial(final_kernel, stage_raw, rows, count),
        in_specs=[pl.BlockSpec(memory_space=pltpu.SMEM)] + [whole] * (2 * count),
        out_specs=[whole] * 3,
        out_shape=[out] * 3,
        name="final",
    )(order, *keeps, *recvs)


def edge_rows(spectra, scales, start, block):
    lines = lax.dynamic_slice_in_dim(spectra, start, 2, axis=1).astype(jnp.float32)
    level = lax.dynamic_slice_in_dim(scales, start, 2, axis=1)
    rows = lines.shape[0] * 2
    limits = jnp.broadcast_to(block.astype(jnp.float32)[None], (rows, 2))
    rest = jnp.zeros((rows, LANES - level.shape[2] - 2), jnp.float32)
    return jnp.concatenate(
        [lines.reshape(rows, -1), level.reshape(rows, -1), limits, rest], axis=1
    )


def on_device(tiles, strips, spectra, scales, retina, quality, bias):
    spectra, scales, quality, bias = spectra[0], scales[0], quality[0], bias[0]
    samples = spectra.shape[-1]
    count = retina.shape[0]
    even, odd, norms, edge = constants(samples)
    even, odd = jnp.asarray(even), jnp.asarray(odd)
    here = lax.axis_index("tile")
    vol = lax.axis_index("vol")
    lines = spectra.shape[1]

    if tiles == 2:
        flip = (here == 1).astype(jnp.int32)
        start = jnp.where(here == 1, 0, lines - 2)
        own = edge_rows(spectra, scales, start, jnp.where(here == 1, retina[0], retina[count - 1]))
        before = after = lax.ppermute(own, "tile", [(0, 1), (1, 0)])
        outside = [(False, False)] * (count - 1) + [(True, True)]
    else:
        flip = jnp.zeros((), jnp.int32)
        up = [(i, i + 1) for i in range(tiles - 1)]
        down = [(i + 1, i) for i in range(tiles - 1)]
        before = lax.ppermute(edge_rows(spectra, scales, lines - 2, retina[count - 1]), "tile", up)
        after = lax.ppermute(edge_rows(spectra, scales, 0, retina[0]), "tile", down)
        outside = [(i == 0, i == count - 1) for i in range(count)]
    info = jnp.concatenate([flip[None], vol[None], retina.reshape(-1), quality]).astype(jnp.int32)
    none = jnp.array([1 << 20, -1], jnp.int32)
    at = samples + scales.shape[2]
    before_block = jnp.where(here == 0, none, before[0, at : at + 2].astype(jnp.int32))
    after_block = jnp.where(here == tiles - 1, none, after[0, at : at + 2].astype(jnp.int32))
    info_outer = jnp.concatenate([info, before_block, after_block])

    bits = strips.bit_length() - 1
    order, keeps, sends = [], [], []
    for i in range(count):
        order.append(jnp.where(flip == 1, count - 1 - i, i))
        outer = outside[i]
        ext = after if outer[1] else (before if outer[0] else jnp.zeros((2 * REPEATS, samples + LANES), jnp.float32))
        if tiles != 2 and outer[0] and outer[1]:
            raise ValueError("one tile")
        send, keep = maps_call(
            i, count, outer, info_outer if outer[0] or outer[1] else info, bias,
            spectra, scales, ext, even, odd, norms, edge, strips,
        )
        keeps.append(keep)
        sends.append(send)

    strip = DEPTH // strips
    rows = DEPTH // 2
    for stage in range(bits):
        pairs = [(v, v ^ (1 << stage)) for v in range(strips)]
        recvs = [lax.ppermute(s, "vol", pairs) for s in sends]
        if stage == bits - 1:
            return tuple(final_call(jnp.stack(order), keeps, recvs, rows, stage == 0))
        bit = ((vol >> (stage + 1)) & 1)[None]
        both = [
            merge_call(bit, k, r, rows, strip, stage == 0) for k, r in zip(keeps, recvs)
        ]
        sends, keeps = [b[0] for b in both], [b[1] for b in both]
        rows //= 2


def solution(mesh):
    return jax.shard_map(
        functools.partial(on_device, mesh.shape["tile"], mesh.shape["vol"]),
        mesh=mesh,
        in_specs=(
            P(("study", "vol"), None, "tile", None),
            P(("study", "vol"), None, "tile", None),
            P(("study", "tile"), None),
            P(("study", "vol"), "tile"),
            P(("study", "vol"), "tile"),
        ),
        out_specs=(P(("study", "vol"), "tile"),) * 3,
        check_vma=False,
    )
```

time: 99.9 us -> 80.5 us (0.81)
  Pallas kernels: 55.7 us -> 43.5 us
  other arithmetic: 5.65 us -> 2.4 us
  local copies, waits for them, and re-layouts: 15.3 us -> 12.2 us
    pallas_call x3, Pallas kernels: 42.9 us -> 30.7 us  [maps_call(): pl.pallas_call(functools.partial(maps_kernel, norms, edge, strips, step,...]
    unnamed x25 -> x43, local copies, waits for them, and re-layouts: 6.58 us -> 11 us
    dynamic_slice x10 -> x2, local copies, waits for them, and re-layouts: 4.7 us -> 0.93 us  [edge_rows(): level = lax.dynamic_slice_in_dim(scales, start, 2, axis=1)]
    select_n x3 -> x1, other arithmetic: 2.45 us -> 0.07 us  [on_device(): jnp.where(here == tiles - 1, none, after[0, at:at + 2].astype(jnp.int32))]
    concatenate x5 -> x2, local copies, waits for them, and re-layouts: 2.29 us -> 0.15 us  [the longest x1 0.08 us: edge_rows(): jnp.concatenate([lines.reshape(rows, -1), level.reshape(rows, -1), limits...]
    dynamic_slice x1 -> x0, other arithmetic: 1.35 us -> none  [on_device(): lax.dynamic_index_in_dim(retina, jnp.minimum(t + 1, count - 1), 0, False)]
  transfers between devices with their start and end apart: 10 -> 10, of which waited for: 4 -> 3; matrix products, arithmetic and copies ran while one was open for 7% -> 2% of each run, Pallas kernels for 39% -> 52%
where the time goes in v2:
time: 80.5 us; the launch traced here: 79.9 us
  Pallas kernels  43.5 us (54%)
  starting transfers between devices  13.9 us (17%)
  local copies, waits for them, and re-layouts  12.2 us (15%)
  waiting for transfers between devices  7.04 us (9%)
  other arithmetic  2.4 us (3%)
    pallas_call x3, Pallas kernels, maps_call(): pl.pallas_call(functools.partial(maps_kernel, norms, edge, strips, step,...  30.7 us
    ppermute x9, starting transfers between devices, on_device(): recvs = [lax.ppermute(s, 'vol', pairs) for s in sends]  13.5 us
    unnamed x43, local copies, waits for them, and re-layouts  11 us
    pallas_call x6, Pallas kernels, merge_call(): pl.pallas_call(functools.partial(merge_kernel, stage_raw, rows, strip), i...  10.9 us
    ppermute x9, waiting for transfers between devices, on_device(): recvs = [lax.ppermute(s, 'vol', pairs) for s in sends]  7.04 us
    pallas_call x1, Pallas kernels, final_call(): pl.pallas_call(functools.partial(final_kernel, stage_raw, rows, count), i...  1.94 us
  transfers between devices with their start and end apart: 10, of which 3 were waited for; matrix products, arithmetic and copies ran while one was open for 2% of the time, Pallas kernels for 52%

profile of v2, /device:TPU:0, one launch (start us, length us, event | category | flops | bytes accessed | tf_op | source)
XLA Modules:
  0.0 79.9 jit_solution(10815722880333121819)
XLA Ops:
  0.6 0.8 copy.15
  1.4 0.8 %constant_dynamic-slice_fusion = f32[1,4,2,16]{2,3,1,0:T(8,128)S(1)} fusion(f32[1,4,384,16]{2,3,1,0:T(8,128)} %param.9, s32[]{:T(128)S(6)} %select_n.39), kind=kLoop, calls=%fused_computation.11 | loop fusion | bytes 1028 | tf_op jit(solution)/shard_map/dynamic_slice | solution.py:368
  2.2 0.1 copy.16
  2.3 0.9 %dynamic-slice_convert_fusion = f32[1,4,2,2048]{3,2,1,0:T(2,128)S(1)} fusion(bf16[1,4,384,2048]{3,2,1,0:T(8,128)(2,1)} %param.8, s32[]{:T(128)S(6)} %select_n.39), kind=kLoop, calls=%fused_computation | loop fusion | flops 16384 | bytes 98308 | tf_op jit(solution)/shard_map/convert_element_type | solution.py:367
  3.4 0.1 concatenate.11
  3.4 0.5 collective-permute-start.4
  3.9 0.1 reshape.20
  4.0 0.7 pad_add_fusion.1.info
  4.7 0.0 copy-start
  4.7 1.2 %copy-done = bf16[1024,512]{1,0:T(8,128)(2,1)S(1)} copy-done((bf16[1024,512]{1,0:T(8,128)(2,1)S(1)}, bf16[1024,512]{1,0:T(8,128)(2,1)}, u32[]{:S(2)}) %copy-start) | copy-done | bytes 1048600
  5.9 1.2 %copy-done.2 = bf16[1024,512]{1,0:T(8,128)(2,1)S(1)} copy-done((bf16[1024,512]{1,0:T(8,128)(2,1)S(1)}, bf16[1024,512]{1,0:T(8,128)(2,1)}, u32[]{:S(2)}) %copy-start.2) | copy-done | bytes 1048600
  7.2 0.9 %copy-done.4 = f32[1,4,384,16]{2,3,1,0:T(8,128)S(1)} copy-done((f32[1,4,384,16]{2,3,1,0:T(8,128)S(1)}, f32[1,4,384,16]{2,3,1,0:T(8,128)}, u32[]{:S(2)}) %copy-start.4) | copy-done | bytes 98328
  8.1 0.7 copy-done.9
  8.7 10.2 %maps.4 = (f32[520,128]{1,0:T(8,128)S(1)}, f32[520,128]{1,0:T(8,128)S(1)}) custom-call(s32[11]{0:T(128)S(1)} %pad_add_fusion.1.info, f32[3]{0:T(128)S(1)} %bitcast.22, bf16[4,384,2048]{2,1,0:T(8,128)(2,1)} %bitcast.25, f32[4,16,384]{2,1,0:T(8,128)S(1)} %bitcast.19, f32[8,2176]{1,0:T(8,128)S(1)} %broadcast_1_ext_ref.2.ext_ref, ...), custom_call_target="tpu_custom_call" | custom-call | tf_op jit(solution)/shard_map/maps/pallas_call | solution.py:261
  19.0 0.7 copy-done.7
  19.7 2.6 %collective-permute-start.2 = (f32[520,128]{1,0:T(8,128)S(1)}, f32[520,128]{1,0:T(8,128)}, u32[]{:S(2)}, u32[]{:S(2)}) collective-permute-start(f32[520,128]{1,0:T(8,128)S(1)} %get-tuple-element.27), channel_id=1, source_target_pairs={{0,2},{2,0},{4,6},{6,4},{8,10},{10,8},{12,14},{14,12},{1,3},{3,1},... | collective-permute-start | bytes 798728 | tf_op jit(solution)/shard_map/ppermute | solution.py:426
  22.3 10.2 %maps.3 = (f32[520,128]{1,0:T(8,128)S(1)}, f32[520,128]{1,0:T(8,128)S(1)}) custom-call(s32[11]{0:T(128)S(1)} %pad_add_fusion.1.info, f32[3]{0:T(128)S(1)} %bitcast.23, bf16[4,384,2048]{2,1,0:T(8,128)(2,1)} %bitcast.26, f32[4,16,384]{2,1,0:T(8,128)S(1)} %bitcast.20, f32[8,2176]{1,0:T(8,128)S(1)} %broadcast_1_ext_ref.2.ext_ref, ...), custom_call_target="tpu_custom_call" | custom-call | tf_op jit(solution)/shard_map/maps/pallas_call | solution.py:261
  32.6 0.7 copy-done.6
  33.3 0.1 collective-permute-start
  33.3 0.1 fusion.2
  33.4 0.1 concatenate.12.info
  33.5 10.2 %maps.5 = (f32[520,128]{1,0:T(8,128)S(1)}, f32[520,128]{1,0:T(8,128)S(1)}) custom-call(s32[15]{0:T(128)S(1)} %concatenate.12.info, f32[3]{0:T(128)S(1)} %bitcast.24, bf16[4,384,2048]{2,1,0:T(8,128)(2,1)} %bitcast.27, f32[4,16,384]{2,1,0:T(8,128)S(1)} %bitcast.21, f32[8,2176]{1,0:T(8,128)S(1)} %collective-permute-done.4.ext_ref, ...), custom_call_target="tpu_custom_call" | custom-call | tf_op jit(solution)/shard_map/maps/pallas_call | solution.py:261
  43.8 0.7 copy-done.8
  44.5 2.0 %collective-permute-start.5 = (f32[520,128]{1,0:T(8,128)S(1)}, f32[520,128]{1,0:T(8,128)S(1)}, u32[]{:S(2)}, u32[]{:S(2)}) collective-permute-start(f32[520,128]{1,0:T(8,128)S(1)} %get-tuple-element.32), channel_id=1, source_target_pairs={{0,2},{2,0},{4,6},{6,4},{8,10},{10,8},{12,14},{14,12},{1,3},{3,1},... | collective-permute-start | bytes 798728 | tf_op jit(solution)/shard_map/ppermute | solution.py:426
  46.4 1.9 %merge.8 = (f32[400,128]{1,0:T(8,128)}, f32[400,128]{1,0:T(8,128)}) custom-call(s32[1]{0:T(128)} %bitcast.3.bit, f32[520,128]{1,0:T(8,128)} %copy-done.7, f32[520,128]{1,0:T(8,128)} %collective-permute-done.2.recv_ref), custom_call_target="tpu_custom_call" | custom-call | tf_op jit(solution)/shard_map/merge/pallas_call | solution.py:331
  48.3 1.6 %collective-permute-start.3 = (f32[400,128]{1,0:T(8,128)}, f32[400,128]{1,0:T(8,128)S(1)}, u32[]{:S(2)}, u32[]{:S(2)}) collective-permute-start(f32[400,128]{1,0:T(8,128)} %get-tuple-element.29), channel_id=1, source_target_pairs={{0,4},{2,6},{4,0},{6,2},{8,12},{10,14},{12,8},{14,10},{1,5},{3,7},... | collective-permute-start | bytes 614408 | tf_op jit(solution)/shard_map/ppermute | solution.py:426
  49.9 0.7 copy-done.11
  50.6 1.9 %merge.6 = (f32[400,128]{1,0:T(8,128)}, f32[400,128]{1,0:T(8,128)}) custom-call(s32[1]{0:T(128)} %bitcast.3.bit, f32[520,128]{1,0:T(8,128)} %copy-done.6, f32[520,128]{1,0:T(8,128)} %copy-done.11), custom_call_target="tpu_custom_call" | custom-call | tf_op jit(solution)/shard_map/merge/pallas_call | solution.py:331
  52.5 0.4 collective-permute-start.1
  52.9 0.0 collective-permute-done.5.recv_ref
  53.0 0.7 copy-done.12
  53.7 1.9 %merge.10 = (f32[400,128]{1,0:T(8,128)}, f32[400,128]{1,0:T(8,128)}) custom-call(s32[1]{0:T(128)} %bitcast.3.bit, f32[520,128]{1,0:T(8,128)} %copy-done.8, f32[520,128]{1,0:T(8,128)} %copy-done.12), custom_call_target="tpu_custom_call" | custom-call | tf_op jit(solution)/shard_map/merge/pallas_call | solution.py:331
  55.5 1.7 %collective-permute-start.6 = (f32[400,128]{1,0:T(8,128)}, f32[400,128]{1,0:T(8,128)S(1)}, u32[]{:S(2)}, u32[]{:S(2)}) collective-permute-start(f32[400,128]{1,0:T(8,128)} %get-tuple-element.34), channel_id=1, source_target_pairs={{0,4},{2,6},{4,0},{6,2},{8,12},{10,14},{12,8},{14,10},{1,5},{3,7},... | collective-permute-start | bytes 614408 | tf_op jit(solution)/shard_map/ppermute | solution.py:426
  57.3 0.7 copy-done.13
  58.0 1.7 %merge.9 = (f32[208,128]{1,0:T(8,128)}, f32[208,128]{1,0:T(8,128)}) custom-call(s32[1]{0:T(128)} %bitcast.2.bit, f32[400,128]{1,0:T(8,128)} %get-tuple-element.28.keep_ref, f32[400,128]{1,0:T(8,128)} %copy-done.13), custom_call_target="tpu_custom_call" | custom-call | tf_op jit(solution)/shard_map/merge/pallas_call | solution.py:331
  59.7 2.6 %collective-permute-start.8 = (f32[208,128]{1,0:T(8,128)}, f32[208,128]{1,0:T(8,128)S(1)}, u32[]{:S(2)}, u32[]{:S(2)}) collective-permute-start(f32[208,128]{1,0:T(8,128)} %get-tuple-element.37), channel_id=1, source_target_pairs={{0,8},{2,10},{4,12},{6,14},{8,0},{10,2},{12,4},{14,6},{1,9},{3,11}... | collective-permute-start | bytes 319496 | tf_op jit(solution)/shard_map/ppermute | solution.py:426
  62.3 0.7 copy-done.14
  63.0 1.8 %merge.7 = (f32[208,128]{1,0:T(8,128)}, f32[208,128]{1,0:T(8,128)}) custom-call(s32[1]{0:T(128)} %bitcast.2.bit, f32[400,128]{1,0:T(8,128)} %get-tuple-element.23.keep_ref, f32[400,128]{1,0:T(8,128)} %copy-done.14), custom_call_target="tpu_custom_call" | custom-call | tf_op jit(solution)/shard_map/merge/pallas_call | solution.py:331
  64.7 1.0 %collective-permute-start.7 = (f32[208,128]{1,0:T(8,128)}, f32[208,128]{1,0:T(8,128)S(1)}, u32[]{:S(2)}, u32[]{:S(2)}) collective-permute-start(f32[208,128]{1,0:T(8,128)} %get-tuple-element.36), channel_id=1, source_target_pairs={{0,8},{2,10},{4,12},{6,14},{8,0},{10,2},{12,4},{14,6},{1,9},{3,11}... | collective-permute-start | bytes 319496 | tf_op jit(solution)/shard_map/ppermute | solution.py:426
  65.7 0.5 collective-permute-done.6.recv_ref
  66.2 0.7 copy-done.15
  66.9 1.7 %merge.11 = (f32[208,128]{1,0:T(8,128)}, f32[208,128]{1,0:T(8,128)}) custom-call(s32[1]{0:T(128)} %bitcast.2.bit, f32[400,128]{1,0:T(8,128)} %get-tuple-element.33.keep_ref, f32[400,128]{1,0:T(8,128)} %copy-done.15), custom_call_target="tpu_custom_call" | custom-call | tf_op jit(solution)/shard_map/merge/pallas_call | solution.py:331
  68.7 1.5 %collective-permute-start.9 = (f32[208,128]{1,0:T(8,128)}, f32[208,128]{1,0:T(8,128)S(1)}, u32[]{:S(2)}, u32[]{:S(2)}) collective-permute-start(f32[208,128]{1,0:T(8,128)} %get-tuple-element.38), channel_id=1, source_target_pairs={{0,8},{2,10},{4,12},{6,14},{8,0},{10,2},{12,4},{14,6},{1,9},{3,11}... | collective-permute-start | bytes 319496 | tf_op jit(solution)/shard_map/ppermute | solution.py:426
  70.1 0.7 pad_add_fusion.order
  70.8 3.3 %collective-permute-done.7.refs_3_ = f32[208,128]{1,0:T(8,128)S(1)} collective-permute-done((f32[208,128]{1,0:T(8,128)}, f32[208,128]{1,0:T(8,128)S(1)}, u32[]{:S(2)}, u32[]{:S(2)}) %collective-permute-start.7) | collective-permute-done | bytes 106528 | tf_op jit(solution)/shard_map/ppermute | solution.py:426
  74.1 3.2 %collective-permute-done.9.refs_5_ = f32[208,128]{1,0:T(8,128)S(1)} collective-permute-done((f32[208,128]{1,0:T(8,128)}, f32[208,128]{1,0:T(8,128)S(1)}, u32[]{:S(2)}, u32[]{:S(2)}) %collective-permute-start.9) | collective-permute-done | bytes 106528 | tf_op jit(solution)/shard_map/ppermute | solution.py:426
  77.3 0.6 copy-done.18
  78.0 1.9 %final.1 = (f32[64,384]{1,0:T(8,128)}, f32[64,384]{1,0:T(8,128)}, f32[64,384]{1,0:T(8,128)}) custom-call(s32[3]{0:T(128)} %pad_add_fusion.order, f32[208,128]{1,0:T(8,128)} %get-tuple-element.25.refs_0_, f32[208,128]{1,0:T(8,128)} %get-tuple-element.30.refs_1_, f32[208,128]{1,0:T(8,128)} %get-tuple-element.35.refs_2_, f32[208,128]{1,0:T(8,128)} %copy-done.17, ...), custom_call_target="tpu_custom_call" | custom-call | tf_op jit(solution)/shard_map/final/pallas_call | solution.py:357
  (39 shorter events, 0.1 us)
Async XLA Ops:
  3.4 29.9 %collective-permute-start.4 = (f32[8,2176]{1,0:T(8,128)S(1)}, f32[8,2176]{1,0:T(8,128)S(1)}, u32[]{:S(2)}, u32[]{:S(2)}) collective-permute-start(f32[8,2176]{1,0:T(8,128)S(1)} %concatenate.11), channel_id=1, source_target_pairs={{0,1},{1,0},{2,3},{3,2},{4,5},{5,4},{6,7},{7,6},{8,9},{9,8},{10,11... | collective-permute-start | bytes 208904 | tf_op jit(solution)/shard_map/ppermute | solution.py:391
  4.7 1.2 %copy-start = (bf16[1024,512]{1,0:T(8,128)(2,1)S(1)}, bf16[1024,512]{1,0:T(8,128)(2,1)}, u32[]{:S(2)}) copy-start(bf16[1024,512]{1,0:T(8,128)(2,1)} %constant.32.clone.odd_hbm) | copy-start | bytes 3145732
  5.9 1.2 %copy-start.2 = (bf16[1024,512]{1,0:T(8,128)(2,1)S(1)}, bf16[1024,512]{1,0:T(8,128)(2,1)}, u32[]{:S(2)}) copy-start(bf16[1024,512]{1,0:T(8,128)(2,1)} %constant.31.clone.even_hbm) | copy-start | bytes 3145732
  7.2 0.9 %copy-start.4 = (f32[1,4,384,16]{2,3,1,0:T(8,128)S(1)}, f32[1,4,384,16]{2,3,1,0:T(8,128)}, u32[]{:S(2)}) copy-start(f32[1,4,384,16]{2,3,1,0:T(8,128)} %param.9) | copy-start | bytes 294916
  8.1 0.7 copy-start.9
  19.0 0.7 copy-start.7
  19.7 13.7 %copy-start.20 = (s32[1,2]{1,0:T(1,128)S(1)}, s32[1,2]{1,0:T(1,128)}, u32[]{:S(2)}) copy-start(s32[1,2]{1,0:T(1,128)} %constant.39) | copy-start | bytes 28
  19.7 13.7 %copy-start.19 = (s32[1,3]{1,0:T(1,128)S(1)}, s32[1,3]{1,0:T(1,128)}, u32[]{:S(2)}) copy-start(s32[1,3]{1,0:T(1,128)} %param.11) | copy-start | bytes 40
  19.7 13.8 %copy-start.1 = (bf16[1024,512]{1,0:T(8,128)(2,1)S(1)}, bf16[1024,512]{1,0:T(8,128)(2,1)}, u32[]{:S(2)}) copy-start(bf16[1024,512]{1,0:T(8,128)(2,1)} %constant.32.clone.odd_hbm) | copy-start | bytes 3145732
  19.7 13.8 %copy-start.3 = (bf16[1024,512]{1,0:T(8,128)(2,1)S(1)}, bf16[1024,512]{1,0:T(8,128)(2,1)}, u32[]{:S(2)}) copy-start(bf16[1024,512]{1,0:T(8,128)(2,1)} %constant.31.clone.even_hbm) | copy-start | bytes 3145732
  19.7 13.8 %copy-start.5 = (f32[1,4,384,16]{2,3,1,0:T(8,128)S(1)}, f32[1,4,384,16]{2,3,1,0:T(8,128)}, u32[]{:S(2)}) copy-start(f32[1,4,384,16]{2,3,1,0:T(8,128)} %param.9) | copy-start | bytes 294916
  19.7 13.8 %copy-start.10 = (f32[1,3]{1,0:T(1,128)S(1)}, f32[1,3]{1,0:T(1,128)}, u32[]{:S(2)}) copy-start(f32[1,3]{1,0:T(1,128)} %param.12) | copy-start | bytes 40
  19.7 26.7 %collective-permute-start.2 = (f32[520,128]{1,0:T(8,128)S(1)}, f32[520,128]{1,0:T(8,128)}, u32[]{:S(2)}, u32[]{:S(2)}) collective-permute-start(f32[520,128]{1,0:T(8,128)S(1)} %get-tuple-element.27), channel_id=1, source_target_pairs={{0,2},{2,0},{4,6},{6,4},{8,10},{10,8},{12,14},{14,12},{1,3},{3,1},... | collective-permute-start | bytes 798728 | tf_op jit(solution)/shard_map/ppermute | solution.py:426
  32.6 0.7 copy-start.6
  33.3 16.7 %collective-permute-start = (f32[520,128]{1,0:T(8,128)S(1)}, f32[520,128]{1,0:T(8,128)S(1)}, u32[]{:S(2)}, u32[]{:S(2)}) collective-permute-start(f32[520,128]{1,0:T(8,128)S(1)} %get-tuple-element.22), channel_id=1, source_target_pairs={{0,2},{2,0},{4,6},{6,4},{8,10},{10,8},{12,14},{14,12},{1,3},{3,1},... | collective-permute-start | bytes 798728 | tf_op jit(solution)/shard_map/ppermute | solution.py:426
  43.8 0.7 copy-start.8
  44.5 8.5 %collective-permute-start.5 = (f32[520,128]{1,0:T(8,128)S(1)}, f32[520,128]{1,0:T(8,128)S(1)}, u32[]{:S(2)}, u32[]{:S(2)}) collective-permute-start(f32[520,128]{1,0:T(8,128)S(1)} %get-tuple-element.32), channel_id=1, source_target_pairs={{0,2},{2,0},{4,6},{6,4},{8,10},{10,8},{12,14},{14,12},{1,3},{3,1},... | collective-permute-start | bytes 798728 | tf_op jit(solution)/shard_map/ppermute | solution.py:426
  48.3 8.9 %collective-permute-start.3 = (f32[400,128]{1,0:T(8,128)}, f32[400,128]{1,0:T(8,128)S(1)}, u32[]{:S(2)}, u32[]{:S(2)}) collective-permute-start(f32[400,128]{1,0:T(8,128)} %get-tuple-element.29), channel_id=1, source_target_pairs={{0,4},{2,6},{4,0},{6,2},{8,12},{10,14},{12,8},{14,10},{1,5},{3,7},... | collective-permute-start | bytes 614408 | tf_op jit(solution)/shard_map/ppermute | solution.py:426
  49.9 0.7 copy-start.11
  52.5 9.8 %collective-permute-start.1 = (f32[400,128]{1,0:T(8,128)}, f32[400,128]{1,0:T(8,128)S(1)}, u32[]{:S(2)}, u32[]{:S(2)}) collective-permute-start(f32[400,128]{1,0:T(8,128)} %get-tuple-element.24), channel_id=1, source_target_pairs={{0,4},{2,6},{4,0},{6,2},{8,12},{10,14},{12,8},{14,10},{1,5},{3,7},... | collective-permute-start | bytes 614408 | tf_op jit(solution)/shard_map/ppermute | solution.py:426
  53.0 0.7 copy-start.12
  55.5 10.7 %collective-permute-start.6 = (f32[400,128]{1,0:T(8,128)}, f32[400,128]{1,0:T(8,128)S(1)}, u32[]{:S(2)}, u32[]{:S(2)}) collective-permute-start(f32[400,128]{1,0:T(8,128)} %get-tuple-element.34), channel_id=1, source_target_pairs={{0,4},{2,6},{4,0},{6,2},{8,12},{10,14},{12,8},{14,10},{1,5},{3,7},... | collective-permute-start | bytes 614408 | tf_op jit(solution)/shard_map/ppermute | solution.py:426
  57.3 0.7 copy-start.13
  59.7 11.1 %collective-permute-start.8 = (f32[208,128]{1,0:T(8,128)}, f32[208,128]{1,0:T(8,128)S(1)}, u32[]{:S(2)}, u32[]{:S(2)}) collective-permute-start(f32[208,128]{1,0:T(8,128)} %get-tuple-element.37), channel_id=1, source_target_pairs={{0,8},{2,10},{4,12},{6,14},{8,0},{10,2},{12,4},{14,6},{1,9},{3,11}... | collective-permute-start | bytes 319496 | tf_op jit(solution)/shard_map/ppermute | solution.py:426
  62.3 0.7 copy-start.14
  64.7 9.3 %collective-permute-start.7 = (f32[208,128]{1,0:T(8,128)}, f32[208,128]{1,0:T(8,128)S(1)}, u32[]{:S(2)}, u32[]{:S(2)}) collective-permute-start(f32[208,128]{1,0:T(8,128)} %get-tuple-element.36), channel_id=1, source_target_pairs={{0,8},{2,10},{4,12},{6,14},{8,0},{10,2},{12,4},{14,6},{1,9},{3,11}... | collective-permute-start | bytes 319496 | tf_op jit(solution)/shard_map/ppermute | solution.py:426
  66.2 0.7 copy-start.15
  68.7 8.6 %collective-permute-start.9 = (f32[208,128]{1,0:T(8,128)}, f32[208,128]{1,0:T(8,128)S(1)}, u32[]{:S(2)}, u32[]{:S(2)}) collective-permute-start(f32[208,128]{1,0:T(8,128)} %get-tuple-element.38), channel_id=1, source_target_pairs={{0,8},{2,10},{4,12},{6,14},{8,0},{10,2},{12,4},{14,6},{1,9},{3,11}... | collective-permute-start | bytes 319496 | tf_op jit(solution)/shard_map/ppermute | solution.py:426
  70.8 6.5 %copy-start.16 = (f32[208,128]{1,0:T(8,128)}, f32[208,128]{1,0:T(8,128)S(1)}, u32[]{:S(2)}) copy-start(f32[208,128]{1,0:T(8,128)S(1)} %collective-permute-done.8.refs_4_) | copy-start | bytes 319492
  74.1 3.2 %copy-start.17 = (f32[208,128]{1,0:T(8,128)}, f32[208,128]{1,0:T(8,128)S(1)}, u32[]{:S(2)}) copy-start(f32[208,128]{1,0:T(8,128)S(1)} %collective-permute-done.7.refs_3_) | copy-start | bytes 319492
  77.3 0.7 copy-start.18

commit v3 on v2

--- a/solution.py
+++ b/solution.py
@@ -32,14 +32,20 @@
         window = np.where(np.abs(away) <= half, np.exp(-0.5 * (away / (samples / 8)) ** 2), 0.0)
         norms.append(float(1.0 / np.sum(window * window)))
     edge = float(np.exp(-0.5 * (half / (samples / 8)) ** 2))
-    return even.astype(ml_dtypes.bfloat16), odd.astype(ml_dtypes.bfloat16), norms, edge
+    return np.stack([even, odd]).astype(ml_dtypes.bfloat16), norms, edge
 
 
 def maps_kernel(
-    norms, edge, strips, step, count, outer, info, bias, x_hbm, scale_ref, ext_ref, even_hbm, odd_hbm,
-    send_ref, keep_ref,
-    rough_ref, struct_ref, x_ref, level_ref, near_ref, even_ref, odd_ref, sems, *scratch,
+    norms, edge, strips, step, count, outer, gives_edge, waits, info, bias, x_hbm, scale_ref,
+    table_hbm, *refs,
 ):
+    refs = list(refs)
+    ext_ref = refs.pop(0) if outer[0] or outer[1] else None
+    if waits:
+        refs.pop(0)
+    send_ref, keep_ref = refs.pop(0), refs.pop(0)
+    give_ref = refs.pop(0) if gives_edge else None
+    rough_ref, struct_ref, x_ref, level_ref, near_ref, even_ref, odd_ref, sems, *scratch = refs
     lines = LANES
     samples = x_hbm.shape[-1]
     blocks = samples // LANES
@@ -55,18 +61,27 @@
     base = pl.multiple_of(tile * lines, lines)
     base_prev = pl.multiple_of(jnp.maximum(base - SUB, 0), SUB)
     base_next = pl.multiple_of(jnp.minimum(base + lines, line_count - SUB), SUB)
+    first_copy = pltpu.make_async_copy(
+        x_hbm.at[:, pl.ds(base, SUB), :], x_ref.at[:, :SUB, :], sems.at[0]
+    )
     own = pltpu.make_async_copy(
-        x_hbm.at[:, pl.ds(base, lines), :], x_ref.at[:, :lines, :], sems.at[0]
+        x_hbm.at[:, pl.ds(pl.multiple_of(base + SUB, SUB), lines - SUB), :],
+        x_ref.at[:, SUB:lines, :],
+        sems.at[5],
     )
     tables = [
-        pltpu.make_async_copy(even_hbm, even_ref, sems.at[1]),
-        pltpu.make_async_copy(odd_hbm, odd_ref, sems.at[2]),
+        pltpu.make_async_copy(table_hbm.at[n], ref, sems.at[1 + n])
+        for n, ref in enumerate((even_ref, odd_ref))
     ]
+    starts = [base_prev, base_next]
+    if gives_edge:
+        base_give = pl.multiple_of(jnp.where(flip == 1, 0, line_count - SUB), SUB)
+        starts.append(base_give)
     edges = [
-        pltpu.make_async_copy(x_hbm.at[:, pl.ds(start, SUB), :], near_ref.at[n], sems.at[3 + n])
-        for n, start in enumerate((base_prev, base_next))
+        pltpu.make_async_copy(x_hbm.at[:, pl.ds(start, SUB), :], near_ref.at[n], sems.at[(3, 4, 6)[n]])
+        for n, start in enumerate(starts)
     ]
-    for copy in [own] + edges + tables:
+    for copy in [first_copy] + tables + edges + [own]:
         copy.start()
 
     at_start, at_end = tile == 0, tile == count - 1
@@ -83,26 +98,13 @@
         level_ref[r, :lines, :] = scale_ref[r, :, pl.ds(base, lines)].T
         level_prev = scale_ref[r, :, whole_prev].T[lines - SUB :]
         level_next = scale_ref[r, :, whole_next].T[:SUB]
-        outside = ext_ref[2 * r : 2 * r + 2, samples : samples + blocks]
+        if outer[0] or outer[1]:
+            outside = ext_ref[2 * r : 2 * r + 2, samples : samples + blocks]
         if outer[0]:
             level_prev = jnp.where(at_start, placed(outside, SUB - 2), level_prev)
         if outer[1]:
             level_next = jnp.where(at_end, placed(outside, 0), level_next)
         level_ref[r, lines:, :] = jnp.where(row_of < 2, level_next, level_prev)
-
-    for copy in [own] + edges:
-        copy.wait()
-    for r in range(REPEATS):
-        for kb in range(blocks):
-            columns = slice(kb * LANES, (kb + 1) * LANES)
-            a = near_ref[0, r, :, columns].astype(jnp.float32)
-            b = near_ref[1, r, :, columns].astype(jnp.float32)
-            if outer[0]:
-                a = jnp.where(at_start, placed(ext_ref[2 * r : 2 * r + 2, columns], SUB - 2), a)
-            if outer[1]:
-                b = jnp.where(at_end, placed(ext_ref[2 * r : 2 * r + 2, columns], 0), b)
-            low = lax.broadcasted_iota(jnp.int32, (SUB, LANES), 0) < 2
-            x_ref[r, lines:, columns] = jnp.where(low, b, a).astype(jnp.bfloat16)
 
     def fold(s, buffers):
         even_in, odd_in, edge_in = buffers
@@ -204,9 +206,45 @@
                     struct_ref[pl.ds(line0, 8), columns] = struct
 
     bufs = [scratch[0:3], scratch[3:6]]
+    first_copy.wait()
     fold(0, bufs[0])
-    for copy in tables:
+    for copy in [own] + edges + tables:
         copy.wait()
+    for r in range(REPEATS):
+        for kb in range(blocks):
+            columns = slice(kb * LANES, (kb + 1) * LANES)
+            a = near_ref[0, r, :, columns].astype(jnp.float32)
+            b = near_ref[1, r, :, columns].astype(jnp.float32)
+            if outer[0]:
+                a = jnp.where(at_start, placed(ext_ref[2 * r : 2 * r + 2, columns], SUB - 2), a)
+            if outer[1]:
+                b = jnp.where(at_end, placed(ext_ref[2 * r : 2 * r + 2, columns], 0), b)
+            low = lax.broadcasted_iota(jnp.int32, (SUB, LANES), 0) < 2
+            x_ref[r, lines:, columns] = jnp.where(low, b, a).astype(jnp.bfloat16)
+
+    if gives_edge:
+        give_cols = pl.ds(pl.multiple_of(jnp.where(flip == 1, 0, line_count - lines), lines), lines)
+        give_tile = jnp.where(flip == 1, 0, count - 1)
+        for r in range(REPEATS):
+            at = slice(2 * r, 2 * r + 2)
+            for kb in range(blocks):
+                columns = slice(kb * LANES, (kb + 1) * LANES)
+                piece = near_ref[2, r, :, columns].astype(jnp.float32)
+                give_ref[at, columns] = jnp.where(flip == 1, piece[:2], piece[SUB - 2 :])
+            level = scale_ref[r, :, give_cols].T
+            level = jnp.where(flip == 1, level[:2], level[lines - 2 :])
+            edge_first = info[2 + 2 * give_tile].astype(jnp.float32)
+            edge_last = info[3 + 2 * give_tile].astype(jnp.float32)
+            give_ref[at, samples:] = jnp.concatenate(
+                [
+                    level,
+                    jnp.full((2, 1), edge_first, jnp.float32),
+                    jnp.full((2, 1), edge_last, jnp.float32),
+                    jnp.zeros((2, LANES - blocks - 2), jnp.float32),
+                ],
+                axis=1,
+            )
+
 
     def pair(i, carry):
         dots(2 * i, bufs[0], False)
@@ -246,121 +284,119 @@
 SPLIT = 2
 
 
-def maps_call(step, count, outer, info, bias, spectra, scales, ext, even, odd, norms, edge, strips):
+def maps_call(step, count, outer, gives_edge, info, bias, spectra, scales, extra, table, norms, edge, strips):
     samples = spectra.shape[-1]
     rows = BANDS * REPEATS * SUB
     out = jax.ShapeDtypeStruct((DEPTH + 8, LANES), jnp.float32)
     half = samples // 2
     whole = pl.BlockSpec(memory_space=pltpu.VMEM)
-    remote = pl.BlockSpec(memory_space=pl.ANY)
+    remote = pl.BlockSpec(memory_space=pltpu.HBM)
+    scales = jnp.swapaxes(scales, 1, 2)
+    has_ext = outer[0] or outer[1]
+    waits = len(extra) > has_ext
+    outs = [out, out]
+    if gives_edge:
+        outs.append(jax.ShapeDtypeStruct((2 * REPEATS, samples + LANES), jnp.float32))
     pair = [
         pltpu.VMEM((rows, half), jnp.bfloat16),
         pltpu.VMEM((rows, half), jnp.bfloat16),
         pltpu.VMEM((rows, LANES), jnp.float32),
     ]
     return pl.pallas_call(
-        functools.partial(maps_kernel, norms, edge, strips, step, count, outer),
-        in_specs=[pl.BlockSpec(memory_space=pltpu.SMEM)] * 2 + [remote, whole, whole, remote, remote],
-        out_specs=[whole] * 2,
+        functools.partial(
+            maps_kernel, norms, edge, strips, step, count, outer, gives_edge, waits
+        ),
+        in_specs=[pl.BlockSpec(memory_space=pltpu.SMEM)] * 2
+        + [remote, whole, remote]
+        + [whole] * has_ext + [pl.BlockSpec(memory_space=pl.ANY)] * waits,
+        out_specs=[whole] * len(outs),
         scratch_shapes=[
             pltpu.VMEM((LANES + 2 * SUB, DEPTH), jnp.float32),
             pltpu.VMEM((LANES, DEPTH), jnp.float32),
             pltpu.VMEM((REPEATS, LANES + SUB, samples), jnp.bfloat16),
             pltpu.VMEM((REPEATS, LANES + SUB, samples // LANES), jnp.float32),
-            pltpu.VMEM((2, REPEATS, SUB, samples), jnp.bfloat16),
+            pltpu.VMEM((3, REPEATS, SUB, samples), jnp.bfloat16),
             pltpu.VMEM((half, DEPTH), jnp.bfloat16),
             pltpu.VMEM((half, DEPTH), jnp.bfloat16),
-            pltpu.SemaphoreType.DMA((5,)),
+            pltpu.SemaphoreType.DMA((7,)),
         ] + pair + pair,
-        out_shape=[out, out],
-        compiler_params=pltpu.CompilerParams(vmem_limit_bytes=48 * 1024 * 1024),
+        out_shape=outs,
+        compiler_params=pltpu.CompilerParams(vmem_limit_bytes=25 * 1024 * 1024 * 5 // 2),
         name="maps",
-    )(info, bias, spectra, jnp.swapaxes(scales, 1, 2), ext, even, odd)
-
-
-def part_rows(half):
-    return 3 * half + 16
-
-
-def merged(stage_raw, keep_ref, recv_ref, rows):
-    if stage_raw:
-        half = rows
-        top_a, top_b = keep_ref[2 * half : 2 * half + 1], recv_ref[2 * half : 2 * half + 1]
-        top = jnp.maximum(top_a, top_b)
-        wa, wb = jnp.exp(top_a - top), jnp.exp(top_b - top)
-        sa, sb = keep_ref[:half], recv_ref[:half]
-        first = wa * sa
-        other = wb * sb
-        maps = [
-            first + other,
-            first * sa + other * sb,
-            wa * keep_ref[half : 2 * half] + wb * recv_ref[half : 2 * half],
-        ]
-        return maps, top, wa + wb
-    at = 3 * rows
-    top_a, top_b = keep_ref[at : at + 1], recv_ref[at : at + 1]
+    )(info, bias, spectra, scales, table, *extra)
+
+
+def merge_kernel(rows, strip, shares, vol, keep_ref, recv_ref, *outs):
+    top_a, top_b = keep_ref[2 * rows : 2 * rows + 8], recv_ref[2 * rows : 2 * rows + 8]
     top = jnp.maximum(top_a, top_b)
     wa, wb = jnp.exp(top_a - top), jnp.exp(top_b - top)
-    maps = [
-        wa * keep_ref[m * rows : (m + 1) * rows] + wb * recv_ref[m * rows : (m + 1) * rows]
-        for m in range(3)
-    ]
-    return maps, top, wa * keep_ref[at + 8 : at + 9] + wb * recv_ref[at + 8 : at + 9]
-
-
-def merge_kernel(stage_raw, rows, strip, bit, keep_ref, recv_ref, send_out, keep_out):
-    maps, top, weight = merged(stage_raw, keep_ref, recv_ref, rows)
-    low = bit[0] == 0
-    half = rows // 2
-    for m, whole in enumerate(maps):
-        for s in range(half // strip):
-            a = whole[2 * s * strip : (2 * s + 1) * strip]
-            b = whole[(2 * s + 1) * strip : (2 * s + 2) * strip]
-            at = m * half + s * strip
-            keep_out[at : at + strip] = jnp.where(low, a, b)
-            send_out[at : at + strip] = jnp.where(low, b, a)
-    tail = 3 * half
-    for out in (keep_out, send_out):
-        out[tail : tail + 8] = jnp.broadcast_to(top, (8, LANES))
-        out[tail + 8 : tail + 16] = jnp.broadcast_to(weight, (8, LANES))
-
-
-def merge_call(bit, keep, recv, rows, strip, stage_raw):
-    out = jax.ShapeDtypeStruct((part_rows(rows // 2), LANES), jnp.float32)
+    row = lax.broadcasted_iota(jnp.int32, (8, LANES), 0)
+    tail = jnp.where(row < 4, top, wa + wb)
+    wa, wb = wa[:1], wb[:1]
+    mine = vol[0] // 2
+    for d in range(shares):
+        t = jnp.bitwise_xor(mine, d)
+        at = pl.ds(pl.multiple_of(t * strip, strip), strip)
+        struct = pl.ds(pl.multiple_of(rows + t * strip, strip), strip)
+        sa, sb = keep_ref[at, :], recv_ref[at, :]
+        first, other = wa * sa, wb * sb
+        outs[d][:strip] = first + other
+        outs[d][strip : 2 * strip] = first * sa + other * sb
+        outs[d][2 * strip : 3 * strip] = wa * keep_ref[struct, :] + wb * recv_ref[struct, :]
+        outs[d][3 * strip :] = tail
+
+
+def merge_call(vol, keep, recv, strips):
+    strip, shares = DEPTH // strips, strips // 2
     whole = pl.BlockSpec(memory_space=pltpu.VMEM)
+    out = jax.ShapeDtypeStruct((3 * strip + 8, LANES), jnp.float32)
     return pl.pallas_call(
-        functools.partial(merge_kernel, stage_raw, rows, strip),
+        functools.partial(merge_kernel, DEPTH // 2, strip, shares),
         in_specs=[pl.BlockSpec(memory_space=pltpu.SMEM), whole, whole],
-        out_specs=[whole, whole],
-        out_shape=[out, out],
+        out_specs=[whole] * shares,
+        out_shape=[out] * shares,
+        compiler_params=pltpu.CompilerParams(vmem_limit_bytes=4 * 1024 * 1024),
         name="merge",
-    )(bit, keep, recv)
-
-
-def final_kernel(stage_raw, rows, count, order, *refs):
-    keeps, recvs = refs[:count], refs[count : 2 * count]
-    angio_ref, joined_ref, spread_ref = refs[2 * count :]
+    )(vol, keep, recv)
+
+
+def final_kernel(strip, count, shares, info, *refs):
+    parts, (angio_ref, joined_ref, spread_ref) = refs[: count * shares], refs[count * shares :]
     for i in range(count):
-        maps, _, weight = merged(stage_raw, keeps[i], recvs[i], rows)
-        scale = 1.0 / weight
-        mean = maps[0] * scale
-        columns = pl.ds(pl.multiple_of(order[i] * LANES, LANES), LANES)
+        mine = parts[i * shares : (i + 1) * shares]
+        tops = [p[3 * strip : 3 * strip + 1] for p in mine]
+        top = functools.reduce(jnp.maximum, tops)
+        scales = [jnp.exp(t - top) for t in tops]
+        weight = functools.reduce(
+            lambda a, b: a + b, [w * p[3 * strip + 4 : 3 * strip + 5] for w, p in zip(scales, mine)]
+        )
+        scales = [w / weight for w in scales]
+        mean, second, joined = (
+            functools.reduce(
+                lambda a, b: a + b,
+                [w * p[m * strip : (m + 1) * strip] for w, p in zip(scales, mine)],
+            )
+            for m in range(3)
+        )
+        tile = jnp.where(info[0] == 1, count - 1 - i, i)
+        columns = pl.ds(pl.multiple_of(tile * LANES, LANES), LANES)
         angio_ref[:, columns] = mean
-        joined_ref[:, columns] = maps[2] * scale
-        spread_ref[:, columns] = jnp.sqrt(maps[1] * scale - mean * mean + 0.01)
-
-
-def final_call(order, keeps, recvs, rows, stage_raw):
-    count = len(keeps)
+        joined_ref[:, columns] = joined
+        spread_ref[:, columns] = jnp.sqrt(second - mean * mean + 0.01)
+
+
+def final_call(info, parts, count, strips):
+    strip, shares = DEPTH // strips, strips // 2
     whole = pl.BlockSpec(memory_space=pltpu.VMEM)
-    out = jax.ShapeDtypeStruct((rows, count * LANES), jnp.float32)
+    out = jax.ShapeDtypeStruct((strip, count * LANES), jnp.float32)
     return pl.pallas_call(
-        functools.partial(final_kernel, stage_raw, rows, count),
-        in_specs=[pl.BlockSpec(memory_space=pltpu.SMEM)] + [whole] * (2 * count),
+        functools.partial(final_kernel, strip, count, shares),
+        in_specs=[pl.BlockSpec(memory_space=pltpu.SMEM)] + [whole] * len(parts),
         out_specs=[whole] * 3,
         out_shape=[out] * 3,
+        compiler_params=pltpu.CompilerParams(vmem_limit_bytes=4 * 1024 * 1024),
         name="final",
-    )(order, *keeps, *recvs)
+    )(info, *parts)
 
 
 def edge_rows(spectra, scales, start, block):
@@ -378,60 +414,74 @@
     spectra, scales, quality, bias = spectra[0], scales[0], quality[0], bias[0]
     samples = spectra.shape[-1]
     count = retina.shape[0]
-    even, odd, norms, edge = constants(samples)
-    even, odd = jnp.asarray(even), jnp.asarray(odd)
+    table, norms, edge = constants(samples)
+    table = jnp.asarray(table)
     here = lax.axis_index("tile")
     vol = lax.axis_index("vol")
     lines = spectra.shape[1]
 
+    at = samples + scales.shape[2]
+    none = jnp.array([1 << 20, -1], jnp.int32)
+    flip = (here == 1).astype(jnp.int32) if tiles == 2 else jnp.zeros((), jnp.int32)
+    info = jnp.concatenate(
+        [flip[None], vol[None].astype(jnp.int32), retina.reshape(-1), quality]
+    ).astype(jnp.int32)
+
+    def with_limits(before, after):
+        before_block = jnp.where(here == 0, none, before[0, at : at + 2].astype(jnp.int32))
+        after_block = jnp.where(here == tiles - 1, none, after[0, at : at + 2].astype(jnp.int32))
+        return jnp.concatenate([info, before_block, after_block])
+
     if tiles == 2:
-        flip = (here == 1).astype(jnp.int32)
-        start = jnp.where(here == 1, 0, lines - 2)
-        own = edge_rows(spectra, scales, start, jnp.where(here == 1, retina[0], retina[count - 1]))
-        before = after = lax.ppermute(own, "tile", [(0, 1), (1, 0)])
         outside = [(False, False)] * (count - 1) + [(True, True)]
     else:
-        flip = jnp.zeros((), jnp.int32)
         up = [(i, i + 1) for i in range(tiles - 1)]
         down = [(i + 1, i) for i in range(tiles - 1)]
         before = lax.ppermute(edge_rows(spectra, scales, lines - 2, retina[count - 1]), "tile", up)
         after = lax.ppermute(edge_rows(spectra, scales, 0, retina[0]), "tile", down)
+        info = with_limits(before, after)
         outside = [(i == 0, i == count - 1) for i in range(count)]
-    info = jnp.concatenate([flip[None], vol[None], retina.reshape(-1), quality]).astype(jnp.int32)
-    none = jnp.array([1 << 20, -1], jnp.int32)
-    at = samples + scales.shape[2]
-    before_block = jnp.where(here == 0, none, before[0, at : at + 2].astype(jnp.int32))
-    after_block = jnp.where(here == tiles - 1, none, after[0, at : at + 2].astype(jnp.int32))
-    info_outer = jnp.concatenate([info, before_block, after_block])
-
-    bits = strips.bit_length() - 1
-    order, keeps, sends = [], [], []
+
+    shares = strips // 2
+    swap = [(v, v ^ 1) for v in range(strips)]
+    kept, arrived, parts = [], [], []
+
+    def merge(i):
+        own, *rest = merge_call(vol[None], kept[i], arrived[i], strips)
+        got = [
+            lax.ppermute(p, "vol", [(v, v ^ (2 * d)) for v in range(strips)])
+            for d, p in zip(range(1, shares), rest)
+        ]
+        parts.append([own] + got)
+
     for i in range(count):
-        order.append(jnp.where(flip == 1, count - 1 - i, i))
         outer = outside[i]
-        ext = after if outer[1] else (before if outer[0] else jnp.zeros((2 * REPEATS, samples + LANES), jnp.float32))
-        if tiles != 2 and outer[0] and outer[1]:
-            raise ValueError("one tile")
-        send, keep = maps_call(
-            i, count, outer, info_outer if outer[0] or outer[1] else info, bias,
-            spectra, scales, ext, even, odd, norms, edge, strips,
+        gives_edge = tiles == 2 and i == 0
+        extra = []
+        if outer[0] or outer[1]:
+            if tiles == 2:
+                after = lax.ppermute(given, "tile", [(0, 1), (1, 0)])
+                step_info = with_limits(after, after)
+            else:
+                step_info = info
+            extra.append(after if outer[1] else before)
+        else:
+            step_info = info
+        if i >= 2:
+            merge(i - 2)
+            extra.append(parts[i - 2][0])
+        send, keep, *rest = maps_call(
+            i, count, outer, gives_edge, step_info, bias,
+            spectra, scales, extra, table, norms, edge, strips,
         )
-        keeps.append(keep)
-        sends.append(send)
-
-    strip = DEPTH // strips
-    rows = DEPTH // 2
-    for stage in range(bits):
-        pairs = [(v, v ^ (1 << stage)) for v in range(strips)]
-        recvs = [lax.ppermute(s, "vol", pairs) for s in sends]
-        if stage == bits - 1:
-            return tuple(final_call(jnp.stack(order), keeps, recvs, rows, stage == 0))
-        bit = ((vol >> (stage + 1)) & 1)[None]
-        both = [
-            merge_call(bit, k, r, rows, strip, stage == 0) for k, r in zip(keeps, recvs)
-        ]
-        sends, keeps = [b[0] for b in both], [b[1] for b in both]
-        rows //= 2
+        if gives_edge:
+            given = rest[0]
+        kept.append(keep)
+        arrived.append(lax.ppermute(send, "vol", swap))
+    for i in range(max(count - 2, 0), count):
+        merge(i)
+    flat = [p for own in parts for p in own]
+    return tuple(final_call(info, flat, count, strips))
 
 
 def solution(mesh):

time: 80.5 us -> 76.1 us (0.945)
  starting transfers between devices: 13.9 us -> 24.9 us
  local copies, waits for them, and re-layouts: 12.2 us -> 3.14 us
  Pallas kernels: 43.5 us -> 36.7 us
  waiting for transfers between devices: 7.04 us -> 8.97 us
  other arithmetic: 2.4 us -> 1.35 us
    pallas_call x7 -> x4, Pallas kernels: 12.8 us -> 1.55 us  [the longest x1 1.37 us: final_call(): pl.pallas_call(functools.partial(final_kernel, strip, count, shares), in_...]
    ppermute x10 -> x13, starting transfers between devices: 13.9 us -> 24.9 us  [the longest x9 19.7 us: merge(): lax.ppermute(p, 'vol', [(v, v ^ 2 * d) for v in range(strips)])]
    unnamed x43 -> x19, local copies, waits for them, and re-layouts: 11 us -> 2.39 us
    pallas_call x3, Pallas kernels: 30.7 us -> 35.1 us  [maps_call(): pl.pallas_call(functools.partial(maps_kernel, norms, edge, strips, step,...]
    ppermute x10 -> x13, waiting for transfers between devices: 7.04 us -> 8.97 us  [the longest x9 7.46 us: merge(): lax.ppermute(p, 'vol', [(v, v ^ 2 * d) for v in range(strips)])]
    convert_element_type x1 -> x0, other arithmetic: 0.94 us -> none  [edge_rows(): lax.dynamic_slice_in_dim(spectra, start, 2, axis=1).astype(jnp.float32)]
    dynamic_slice x2 -> x0, local copies, waits for them, and re-layouts: 0.93 us -> none  [edge_rows(): level = lax.dynamic_slice_in_dim(scales, start, 2, axis=1)]
  transfers between devices with their start and end apart: 10 -> 13, of which waited for: 3 -> 4; matrix products, arithmetic and copies ran while one was open for 2% -> 1% of each run, Pallas kernels for 52% -> 31%
where the time goes in v3:
time: 76.1 us; the launch traced here: 75.8 us
  Pallas kernels  36.7 us (48%)
  starting transfers between devices  24.9 us (33%)
  waiting for transfers between devices  8.97 us (12%)
  local copies, waits for them, and re-layouts  3.14 us (4%)
  other arithmetic  1.35 us (2%)
  between operations  0.79 us (1%)
    pallas_call x3, Pallas kernels, maps_call(): pl.pallas_call(functools.partial(maps_kernel, norms, edge, strips, step,...  35.1 us
    ppermute x9, starting transfers between devices, merge(): lax.ppermute(p, 'vol', [(v, v ^ 2 * d) for v in range(strips)])  19.7 us
    ppermute x9, waiting for transfers between devices, merge(): lax.ppermute(p, 'vol', [(v, v ^ 2 * d) for v in range(strips)])  7.46 us
    ppermute x3, starting transfers between devices, on_device(): arrived.append(lax.ppermute(send, 'vol', swap))  4.71 us
    unnamed x19, local copies, waits for them, and re-layouts  2.39 us
  transfers between devices with their start and end apart: 13, of which 4 were waited for; matrix products, arithmetic and copies ran while one was open for 1% of the time, Pallas kernels for 31%

profile of v3, /device:TPU:0, one launch (start us, length us, event | category | flops | bytes accessed | tf_op | source)
XLA Modules:
  0.0 75.8 jit_solution(7083409036061813521)
XLA Ops:
  0.6 0.8 %copy.11 = s32[3,2]{1,0:T(4,128)S(1)} copy(s32[3,2]{0,1:T(2,128)} %param.9) | data formatting | bytes 48 | tf_op args[2]
  1.4 0.1 reshape.10
  1.5 1.3 %pad_add_fusion.info = s32[11]{0:T(128)} fusion(s32[3]{0:T(128)} %bitcast.21, s32[6]{0:T(128)S(1)} %reshape.10, s32[1]{0:T(128)} %bitcast.1.vol, s32[1]{0:T(128)} %bitcast), kind=kLoop, calls=%fused_computation.5 | loop fusion | flops 33 | bytes 88 | tf_op jit(solution)/shard_map/concatenate | solution.py:426
  2.8 11.8 %maps.3 = (f32[520,128]{1,0:T(8,128)}, f32[520,128]{1,0:T(8,128)}, f32[8,2176]{1,0:T(8,128)}) custom-call(s32[11]{0:T(128)} %pad_add_fusion.info, f32[3]{0:T(128)} %bitcast.18, bf16[4,384,2048]{2,1,0:T(8,128)(2,1)} %bitcast.12, f32[4,16,384]{2,1,0:T(8,128)} %bitcast.15, bf16[2,1024,512]{2,1,0:T(8,128)(2,1)} %constant.16.clone.table_hbm), custom_call_target="tpu_custom_call" | custom-call | tf_op jit(solution)/shard_map/maps/pallas_call | solution.py:305
  14.5 0.0 copy-start.8
  14.6 0.0 copy-start.7
  14.6 0.5 collective-permute-start.8
  15.1 2.6 %collective-permute-start = (f32[520,128]{1,0:T(8,128)}, f32[520,128]{1,0:T(8,128)S(1)}, u32[]{:S(2)}, u32[]{:S(2)}) collective-permute-start(f32[520,128]{1,0:T(8,128)} %get-tuple-element.23), channel_id=1, source_target_pairs={{0,2},{2,0},{4,6},{6,4},{8,10},{10,8},{12,14},{14,12},{1,3},{3,1},... | collective-permute-start | bytes 798728 | tf_op jit(solution)/shard_map/ppermute | solution.py:480
  17.7 11.6 %maps.4 = (f32[520,128]{1,0:T(8,128)}, f32[520,128]{1,0:T(8,128)}) custom-call(s32[11]{0:T(128)} %pad_add_fusion.info, f32[3]{0:T(128)} %bitcast.19, bf16[4,384,2048]{2,1,0:T(8,128)(2,1)} %bitcast.13, f32[4,16,384]{2,1,0:T(8,128)} %bitcast.16, bf16[2,1024,512]{2,1,0:T(8,128)(2,1)} %constant.16.clone.table_hbm), custom_call_target="tpu_custom_call" | custom-call | tf_op jit(solution)/shard_map/maps/pallas_call | solution.py:305
  29.3 0.0 copy-start.2
  29.3 0.0 copy-start.5
  29.3 0.1 collective-permute-start.4
  29.4 0.0 collective-permute-done.8.refs_0_
  29.4 0.0 copy-start.6
  29.4 0.1 fusion.1
  29.5 0.7 concatenate.8.info
  30.1 0.0 collective-permute-done.recv_ref
  30.2 0.0 copy-done.4
  30.2 0.1 merge.3
  30.2 0.0 copy-done.6
  30.2 0.0 copy-start
  30.2 0.6 copy-done
  30.9 11.8 %maps.5 = (f32[520,128]{1,0:T(8,128)}, f32[520,128]{1,0:T(8,128)}) custom-call(s32[15]{0:T(128)} %concatenate.8.info, f32[3]{0:T(128)} %bitcast.20, bf16[4,384,2048]{2,1,0:T(8,128)(2,1)} %bitcast.14, f32[4,16,384]{2,1,0:T(8,128)} %bitcast.17, bf16[2,1024,512]{2,1,0:T(8,128)(2,1)} %constant.16.clone.table_hbm, f32[8,2176]{1,0:T(8,128)} %copy-done.6, ...), custom_call_target="tpu_custom_call" | custom-call | tf_op jit(solution)/shard_map/maps/pallas_call | solution.py:305
  42.7 2.0 %collective-permute-start.9 = (f32[520,128]{1,0:T(8,128)}, f32[520,128]{1,0:T(8,128)S(1)}, u32[]{:S(2)}, u32[]{:S(2)}) collective-permute-start(f32[520,128]{1,0:T(8,128)} %get-tuple-element.36), channel_id=1, source_target_pairs={{0,2},{2,0},{4,6},{6,4},{8,10},{10,8},{12,14},{14,12},{1,3},{3,1},... | collective-permute-start | bytes 798728 | tf_op jit(solution)/shard_map/ppermute | solution.py:480
  44.7 0.0 collective-permute-done.4.recv_ref
  44.7 0.1 merge.4
  44.8 1.6 %collective-permute-start.5 = (f32[200,128]{1,0:T(8,128)S(1)}, f32[200,128]{1,0:T(8,128)S(1)}, u32[]{:S(2)}, u32[]{:S(2)}) collective-permute-start(f32[200,128]{1,0:T(8,128)S(1)} %get-tuple-element.31), channel_id=1, source_target_pairs={{0,4},{2,6},{4,0},{6,2},{8,12},{10,14},{12,8},{14,10},{1,5},{3,7},... | collective-permute-start | bytes 307208 | tf_op jit(solution)/shard_map/ppermute | solution.py:452
  46.4 2.6 %collective-permute-start.6 = (f32[200,128]{1,0:T(8,128)S(1)}, f32[200,128]{1,0:T(8,128)S(1)}, u32[]{:S(2)}, u32[]{:S(2)}) collective-permute-start(f32[200,128]{1,0:T(8,128)S(1)} %get-tuple-element.32), channel_id=1, source_target_pairs={{0,8},{2,10},{4,12},{6,14},{8,0},{10,2},{12,4},{14,6},{1,9},{3,11}... | collective-permute-start | bytes 307208 | tf_op jit(solution)/shard_map/ppermute | solution.py:452
  49.0 0.2 collective-permute-start.7
  49.2 0.7 collective-permute-start.1
  49.9 1.5 %collective-permute-done.9.recv_ref = f32[520,128]{1,0:T(8,128)S(1)} collective-permute-done((f32[520,128]{1,0:T(8,128)}, f32[520,128]{1,0:T(8,128)S(1)}, u32[]{:S(2)}, u32[]{:S(2)}) %collective-permute-start.9) | collective-permute-done | bytes 266272 | tf_op jit(solution)/shard_map/ppermute | solution.py:480
  51.4 2.8 %collective-permute-start.2 = (f32[200,128]{1,0:T(8,128)S(1)}, f32[200,128]{1,0:T(8,128)S(1)}, u32[]{:S(2)}, u32[]{:S(2)}) collective-permute-start(f32[200,128]{1,0:T(8,128)S(1)} %get-tuple-element.26), channel_id=1, source_target_pairs={{0,8},{2,10},{4,12},{6,14},{8,0},{10,2},{12,4},{14,6},{1,9},{3,11}... | collective-permute-start | bytes 307208 | tf_op jit(solution)/shard_map/ppermute | solution.py:452
  54.2 0.9 %copy-done.3 = f32[520,128]{1,0:T(8,128)S(1)} copy-done((f32[520,128]{1,0:T(8,128)S(1)}, f32[520,128]{1,0:T(8,128)}, u32[]{:S(2)}) %copy-start.3) | copy-done | bytes 266264
  55.1 0.1 merge.5
  55.2 0.0 collective-permute-done.5.refs_5_
  55.2 1.4 %collective-permute-start.3 = (f32[200,128]{1,0:T(8,128)S(1)}, f32[200,128]{1,0:T(8,128)S(1)}, u32[]{:S(2)}, u32[]{:S(2)}) collective-permute-start(f32[200,128]{1,0:T(8,128)S(1)} %get-tuple-element.27), channel_id=1, source_target_pairs={{0,12},{2,14},{4,8},{6,10},{8,4},{10,6},{12,0},{14,2},{1,13},{3,15... | collective-permute-start | bytes 307208 | tf_op jit(solution)/shard_map/ppermute | solution.py:452
  56.6 0.5 collective-permute-done.6.refs_6_
  57.1 0.8 %collective-permute-start.10 = (f32[200,128]{1,0:T(8,128)S(1)}, f32[200,128]{1,0:T(8,128)S(1)}, u32[]{:S(2)}, u32[]{:S(2)}) collective-permute-start(f32[200,128]{1,0:T(8,128)S(1)} %get-tuple-element.38), channel_id=1, source_target_pairs={{0,4},{2,6},{4,0},{6,2},{8,12},{10,14},{12,8},{14,10},{1,5},{3,7},... | collective-permute-start | bytes 307208 | tf_op jit(solution)/shard_map/ppermute | solution.py:452
  57.9 0.0 collective-permute-done.7.refs_7_
  57.9 9.5 %collective-permute-start.11 = (f32[200,128]{1,0:T(8,128)S(1)}, f32[200,128]{1,0:T(8,128)S(1)}, u32[]{:S(2)}, u32[]{:S(2)}) collective-permute-start(f32[200,128]{1,0:T(8,128)S(1)} %get-tuple-element.39), channel_id=1, source_target_pairs={{0,8},{2,10},{4,12},{6,14},{8,0},{10,2},{12,4},{14,6},{1,9},{3,11}... | collective-permute-start | bytes 307208 | tf_op jit(solution)/shard_map/ppermute | solution.py:452
  67.4 0.0 collective-permute-done.1.refs_1_
  67.4 0.1 collective-permute-start.12
  67.5 0.4 collective-permute-done.2.refs_2_
  68.0 0.0 collective-permute-done.3.refs_3_
  68.0 0.0 collective-permute-done.10.refs_9_
  68.0 6.5 %collective-permute-done.11.refs_10_ = f32[200,128]{1,0:T(8,128)S(1)} collective-permute-done((f32[200,128]{1,0:T(8,128)S(1)}, f32[200,128]{1,0:T(8,128)S(1)}, u32[]{:S(2)}, u32[]{:S(2)}) %collective-permute-start.11) | collective-permute-done | bytes 102432 | tf_op jit(solution)/shard_map/ppermute | solution.py:452
  74.5 0.0 collective-permute-done.12.refs_11_
  74.5 1.4 %final.1 = (f32[64,384]{1,0:T(8,128)}, f32[64,384]{1,0:T(8,128)}, f32[64,384]{1,0:T(8,128)}) custom-call(s32[11]{0:T(128)S(1)} %copy-done.5, f32[200,128]{1,0:T(8,128)S(1)} %copy-done.1, f32[200,128]{1,0:T(8,128)S(1)} %collective-permute-done.1.refs_1_, f32[200,128]{1,0:T(8,128)S(1)} %collective-permute-done.2.refs_2_, ...), custom_call_target="tpu_custom_call" | custom-call | tf_op jit(solution)/shard_map/final/pallas_call | solution.py:392
  (8 shorter events, 0.0 us)
Async XLA Ops:
  14.5 14.8 %copy-start.8 = (s32[1,2]{1,0:T(1,128)S(1)}, s32[1,2]{1,0:T(1,128)}, u32[]{:S(2)}) copy-start(s32[1,2]{1,0:T(1,128)} %constant.23) | copy-start | bytes 28
  14.6 14.9 %copy-start.7 = (s32[1,3]{1,0:T(1,128)S(1)}, s32[1,3]{1,0:T(1,128)}, u32[]{:S(2)}) copy-start(s32[1,3]{1,0:T(1,128)} %param.10) | copy-start | bytes 40
  14.6 15.6 %copy-start.4 = (f32[520,128]{1,0:T(8,128)S(1)}, f32[520,128]{1,0:T(8,128)}, u32[]{:S(2)}) copy-start(f32[520,128]{1,0:T(8,128)} %get-tuple-element.22.keep_ref) | copy-start | bytes 798724
  14.6 14.8 %collective-permute-start.8 = (f32[8,2176]{1,0:T(8,128)}, f32[8,2176]{1,0:T(8,128)S(1)}, u32[]{:S(2)}, u32[]{:S(2)}) collective-permute-start(f32[8,2176]{1,0:T(8,128)} %get-tuple-element.34), channel_id=1, source_target_pairs={{0,1},{1,0},{2,3},{3,2},{4,5},{5,4},{6,7},{7,6},{8,9},{9,8},{10,11... | collective-permute-start | bytes 208904 | tf_op jit(solution)/shard_map/ppermute | solution.py:463
  15.1 15.1 %collective-permute-start = (f32[520,128]{1,0:T(8,128)}, f32[520,128]{1,0:T(8,128)S(1)}, u32[]{:S(2)}, u32[]{:S(2)}) collective-permute-start(f32[520,128]{1,0:T(8,128)} %get-tuple-element.23), channel_id=1, source_target_pairs={{0,2},{2,0},{4,6},{6,4},{8,10},{10,8},{12,14},{14,12},{1,3},{3,1},... | collective-permute-start | bytes 798728 | tf_op jit(solution)/shard_map/ppermute | solution.py:480
  29.3 15.4 %copy-start.2 = (f32[520,128]{1,0:T(8,128)S(1)}, f32[520,128]{1,0:T(8,128)}, u32[]{:S(2)}) copy-start(f32[520,128]{1,0:T(8,128)} %get-tuple-element.28.keep_ref) | copy-start | bytes 798724
  29.3 45.2 %copy-start.5 = (s32[11]{0:T(128)S(1)}, s32[11]{0:T(128)}, u32[]{:S(2)}) copy-start(s32[11]{0:T(128)} %pad_add_fusion.info) | copy-start | bytes 136
  29.3 15.4 %collective-permute-start.4 = (f32[520,128]{1,0:T(8,128)}, f32[520,128]{1,0:T(8,128)S(1)}, u32[]{:S(2)}, u32[]{:S(2)}) collective-permute-start(f32[520,128]{1,0:T(8,128)} %get-tuple-element.29), channel_id=1, source_target_pairs={{0,2},{2,0},{4,6},{6,4},{8,10},{10,8},{12,14},{14,12},{1,3},{3,1},... | collective-permute-start | bytes 798728 | tf_op jit(solution)/shard_map/ppermute | solution.py:480
  29.4 0.8 %copy-start.6 = (f32[8,2176]{1,0:T(8,128)}, f32[8,2176]{1,0:T(8,128)S(1)}, u32[]{:S(2)}) copy-start(f32[8,2176]{1,0:T(8,128)S(1)} %collective-permute-done.8.refs_0_) | copy-start | bytes 208900
  30.2 0.6 copy-start
  30.9 43.6 %copy-start.1 = (f32[200,128]{1,0:T(8,128)S(1)}, f32[200,128]{1,0:T(8,128)}, u32[]{:S(2)}) copy-start(f32[200,128]{1,0:T(8,128)} %copy-done) | copy-start | bytes 307204
  42.7 8.7 %collective-permute-start.9 = (f32[520,128]{1,0:T(8,128)}, f32[520,128]{1,0:T(8,128)S(1)}, u32[]{:S(2)}, u32[]{:S(2)}) collective-permute-start(f32[520,128]{1,0:T(8,128)} %get-tuple-element.36), channel_id=1, source_target_pairs={{0,2},{2,0},{4,6},{6,4},{8,10},{10,8},{12,14},{14,12},{1,3},{3,1},... | collective-permute-start | bytes 798728 | tf_op jit(solution)/shard_map/ppermute | solution.py:480
  44.8 10.4 %collective-permute-start.5 = (f32[200,128]{1,0:T(8,128)S(1)}, f32[200,128]{1,0:T(8,128)S(1)}, u32[]{:S(2)}, u32[]{:S(2)}) collective-permute-start(f32[200,128]{1,0:T(8,128)S(1)} %get-tuple-element.31), channel_id=1, source_target_pairs={{0,4},{2,6},{4,0},{6,2},{8,12},{10,14},{12,8},{14,10},{1,5},{3,7},... | collective-permute-start | bytes 307208 | tf_op jit(solution)/shard_map/ppermute | solution.py:452
  46.4 10.7 %collective-permute-start.6 = (f32[200,128]{1,0:T(8,128)S(1)}, f32[200,128]{1,0:T(8,128)S(1)}, u32[]{:S(2)}, u32[]{:S(2)}) collective-permute-start(f32[200,128]{1,0:T(8,128)S(1)} %get-tuple-element.32), channel_id=1, source_target_pairs={{0,8},{2,10},{4,12},{6,14},{8,0},{10,2},{12,4},{14,6},{1,9},{3,11}... | collective-permute-start | bytes 307208 | tf_op jit(solution)/shard_map/ppermute | solution.py:452
  49.0 8.9 %collective-permute-start.7 = (f32[200,128]{1,0:T(8,128)S(1)}, f32[200,128]{1,0:T(8,128)S(1)}, u32[]{:S(2)}, u32[]{:S(2)}) collective-permute-start(f32[200,128]{1,0:T(8,128)S(1)} %get-tuple-element.33), channel_id=1, source_target_pairs={{0,12},{2,14},{4,8},{6,10},{8,4},{10,6},{12,0},{14,2},{1,13},{3,15... | collective-permute-start | bytes 307208 | tf_op jit(solution)/shard_map/ppermute | solution.py:452
  49.2 18.2 %collective-permute-start.1 = (f32[200,128]{1,0:T(8,128)S(1)}, f32[200,128]{1,0:T(8,128)S(1)}, u32[]{:S(2)}, u32[]{:S(2)}) collective-permute-start(f32[200,128]{1,0:T(8,128)S(1)} %get-tuple-element.25), channel_id=1, source_target_pairs={{0,4},{2,6},{4,0},{6,2},{8,12},{10,14},{12,8},{14,10},{1,5},{3,7},... | collective-permute-start | bytes 307208 | tf_op jit(solution)/shard_map/ppermute | solution.py:452
  51.4 16.6 %collective-permute-start.2 = (f32[200,128]{1,0:T(8,128)S(1)}, f32[200,128]{1,0:T(8,128)S(1)}, u32[]{:S(2)}, u32[]{:S(2)}) collective-permute-start(f32[200,128]{1,0:T(8,128)S(1)} %get-tuple-element.26), channel_id=1, source_target_pairs={{0,8},{2,10},{4,12},{6,14},{8,0},{10,2},{12,4},{14,6},{1,9},{3,11}... | collective-permute-start | bytes 307208 | tf_op jit(solution)/shard_map/ppermute | solution.py:452
  54.2 1.0 %copy-start.3 = (f32[520,128]{1,0:T(8,128)S(1)}, f32[520,128]{1,0:T(8,128)}, u32[]{:S(2)}) copy-start(f32[520,128]{1,0:T(8,128)} %get-tuple-element.35.keep_ref) | copy-start | bytes 798724
  55.2 12.8 %collective-permute-start.3 = (f32[200,128]{1,0:T(8,128)S(1)}, f32[200,128]{1,0:T(8,128)S(1)}, u32[]{:S(2)}, u32[]{:S(2)}) collective-permute-start(f32[200,128]{1,0:T(8,128)S(1)} %get-tuple-element.27), channel_id=1, source_target_pairs={{0,12},{2,14},{4,8},{6,10},{8,4},{10,6},{12,0},{14,2},{1,13},{3,15... | collective-permute-start | bytes 307208 | tf_op jit(solution)/shard_map/ppermute | solution.py:452
  57.1 10.9 %collective-permute-start.10 = (f32[200,128]{1,0:T(8,128)S(1)}, f32[200,128]{1,0:T(8,128)S(1)}, u32[]{:S(2)}, u32[]{:S(2)}) collective-permute-start(f32[200,128]{1,0:T(8,128)S(1)} %get-tuple-element.38), channel_id=1, source_target_pairs={{0,4},{2,6},{4,0},{6,2},{8,12},{10,14},{12,8},{14,10},{1,5},{3,7},... | collective-permute-start | bytes 307208 | tf_op jit(solution)/shard_map/ppermute | solution.py:452
  57.9 16.6 %collective-permute-start.11 = (f32[200,128]{1,0:T(8,128)S(1)}, f32[200,128]{1,0:T(8,128)S(1)}, u32[]{:S(2)}, u32[]{:S(2)}) collective-permute-start(f32[200,128]{1,0:T(8,128)S(1)} %get-tuple-element.39), channel_id=1, source_target_pairs={{0,8},{2,10},{4,12},{6,14},{8,0},{10,2},{12,4},{14,6},{1,9},{3,11}... | collective-permute-start | bytes 307208 | tf_op jit(solution)/shard_map/ppermute | solution.py:452
  67.4 7.1 %collective-permute-start.12 = (f32[200,128]{1,0:T(8,128)S(1)}, f32[200,128]{1,0:T(8,128)S(1)}, u32[]{:S(2)}, u32[]{:S(2)}) collective-permute-start(f32[200,128]{1,0:T(8,128)S(1)} %get-tuple-element.40), channel_id=1, source_target_pairs={{0,12},{2,14},{4,8},{6,10},{8,4},{10,6},{12,0},{14,2},{1,13},{3,15... | collective-permute-start | bytes 307208 | tf_op jit(solution)/shard_map/ppermute | solution.py:452

commit v4 on v3

--- a/solution.py
+++ b/solution.py
@@ -322,11 +322,17 @@
         ] + pair + pair,
         out_shape=outs,
         compiler_params=pltpu.CompilerParams(vmem_limit_bytes=25 * 1024 * 1024 * 5 // 2),
+        cost_estimate=pl.CostEstimate(
+            flops=5 * BANDS * REPEATS * (LANES + SUB) * samples * DEPTH,
+            bytes_accessed=2 * REPEATS * LANES * samples + 4 * samples * DEPTH,
+            transcendentals=0,
+        ),
         name="maps",
     )(info, bias, spectra, scales, table, *extra)
 
 
-def merge_kernel(rows, strip, shares, vol, keep_ref, recv_ref, *outs):
+def merge_kernel(rows, strip, shares, tied, vol, keep_ref, recv_ref, *outs):
+    outs = outs[len(outs) - shares - tied : len(outs) - tied]
     top_a, top_b = keep_ref[2 * rows : 2 * rows + 8], recv_ref[2 * rows : 2 * rows + 8]
     top = jnp.maximum(top_a, top_b)
     wa, wb = jnp.exp(top_a - top), jnp.exp(top_b - top)
@@ -346,18 +352,21 @@
         outs[d][3 * strip :] = tail
 
 
-def merge_call(vol, keep, recv, strips):
+def merge_call(vol, keep, recv, later, strips):
     strip, shares = DEPTH // strips, strips // 2
     whole = pl.BlockSpec(memory_space=pltpu.VMEM)
+    remote = pl.BlockSpec(memory_space=pl.ANY)
     out = jax.ShapeDtypeStruct((3 * strip + 8, LANES), jnp.float32)
+    tied = [jax.ShapeDtypeStruct(a.shape, a.dtype) for a in later[:1]]
     return pl.pallas_call(
-        functools.partial(merge_kernel, DEPTH // 2, strip, shares),
-        in_specs=[pl.BlockSpec(memory_space=pltpu.SMEM), whole, whole],
-        out_specs=[whole] * shares,
-        out_shape=[out] * shares,
+        functools.partial(merge_kernel, DEPTH // 2, strip, shares, len(tied)),
+        in_specs=[pl.BlockSpec(memory_space=pltpu.SMEM), whole, whole] + [remote] * len(later),
+        out_specs=[whole] * shares + [remote] * len(tied),
+        out_shape=[out] * shares + tied,
+        input_output_aliases={3: shares} if tied else {},
         compiler_params=pltpu.CompilerParams(vmem_limit_bytes=4 * 1024 * 1024),
         name="merge",
-    )(vol, keep, recv)
+    )(vol, keep, recv, *later)
 
 
 def final_kernel(strip, count, shares, info, *refs):
@@ -446,13 +455,14 @@
     swap = [(v, v ^ 1) for v in range(strips)]
     kept, arrived, parts = [], [], []
 
-    def merge(i):
-        own, *rest = merge_call(vol[None], kept[i], arrived[i], strips)
+    def merge(i, later):
+        outs = merge_call(vol[None], kept[i], arrived[i], later, strips)
         got = [
             lax.ppermute(p, "vol", [(v, v ^ (2 * d)) for v in range(strips)])
-            for d, p in zip(range(1, shares), rest)
+            for d, p in zip(range(1, shares), outs[1:])
         ]
-        parts.append([own] + got)
+        parts.append([outs[0]] + got)
+        return outs[-1]
 
     for i in range(count):
         outer = outside[i]
@@ -468,7 +478,8 @@
         else:
             step_info = info
         if i >= 2:
-            merge(i - 2)
+            if i == 2:
+                merge(0, [])
             extra.append(parts[i - 2][0])
         send, keep, *rest = maps_call(
             i, count, outer, gives_edge, step_info, bias,
@@ -477,9 +488,11 @@
         if gives_edge:
             given = rest[0]
         kept.append(keep)
+        if i >= 2:
+            send = merge(i - 1, [send] + parts[i - 2][1:])
         arrived.append(lax.ppermute(send, "vol", swap))
-    for i in range(max(count - 2, 0), count):
-        merge(i)
+    for i in range(len(parts), count):
+        merge(i, [])
     flat = [p for own in parts for p in own]
     return tuple(final_call(info, flat, count, strips))
 

time: 76.1 us -> 71.8 us (0.943)
  starting transfers between devices: 24.9 us -> 18.5 us
  waiting for transfers between devices: 8.97 us -> 10.1 us
  local copies, waits for them, and re-layouts: 3.14 us -> 4.07 us
    ppermute x9, starting transfers between devices: 19.7 us -> 13.5 us  [merge(): lax.ppermute(p, 'vol', [(v, v ^ 2 * d) for v in range(strips)])]
    ppermute x9, waiting for transfers between devices: 7.46 us -> 8.61 us  [merge(): lax.ppermute(p, 'vol', [(v, v ^ 2 * d) for v in range(strips)])]
    unnamed x19 -> x21, local copies, waits for them, and re-layouts: 2.39 us -> 3.32 us
  transfers between devices with their start and end apart: 13 -> 13, of which waited for: 4 -> 4; matrix products, arithmetic and copies ran while one was open for 1% -> 1% of each run, Pallas kernels for 31% -> 33%
where the time goes in v4:
time: 71.8 us; the launch traced here: 71.5 us
  Pallas kernels  36.7 us (51%)
  starting transfers between devices  18.5 us (26%)
  waiting for transfers between devices  10.1 us (14%)
  local copies, waits for them, and re-layouts  4.07 us (6%)
  other arithmetic  1.39 us (2%)
  between operations  0.8 us (1%)
    pallas_call x3, Pallas kernels, maps_call(): pl.pallas_call(functools.partial(maps_kernel, norms, edge, strips, step,...  35.1 us
    ppermute x9, starting transfers between devices, merge(): lax.ppermute(p, 'vol', [(v, v ^ 2 * d) for v in range(strips)])  13.5 us
    ppermute x9, waiting for transfers between devices, merge(): lax.ppermute(p, 'vol', [(v, v ^ 2 * d) for v in range(strips)])  8.61 us
    ppermute x3, starting transfers between devices, on_device(): arrived.append(lax.ppermute(send, 'vol', swap))  4.5 us
    unnamed x21, local copies, waits for them, and re-layouts  3.32 us
    ppermute x3, waiting for transfers between devices, on_device(): arrived.append(lax.ppermute(send, 'vol', swap))  1.49 us
  transfers between devices with their start and end apart: 13, of which 4 were waited for; matrix products, arithmetic and copies ran while one was open for 1% of the time, Pallas kernels for 33%

profile of v4, /device:TPU:0, one launch (start us, length us, event | category | flops | bytes accessed | tf_op | source)
XLA Modules:
  0.0 71.5 jit_solution(13551398656687058964)
XLA Ops:
  0.6 0.8 %copy.12 = s32[3,2]{1,0:T(4,128)S(1)} copy(s32[3,2]{0,1:T(2,128)} %param.9) | data formatting | bytes 48 | tf_op args[2]
  1.4 0.1 reshape.10
  1.5 1.3 %pad_add_fusion.info = s32[11]{0:T(128)} fusion(s32[3]{0:T(128)} %bitcast.12, s32[6]{0:T(128)S(1)} %reshape.10, s32[1]{0:T(128)} %bitcast.1.vol, s32[1]{0:T(128)} %bitcast), kind=kLoop, calls=%fused_computation.5 | loop fusion | flops 33 | bytes 88 | tf_op jit(solution)/shard_map/concatenate | solution.py:435
  2.8 11.8 %maps.3 = (f32[520,128]{1,0:T(8,128)}, f32[520,128]{1,0:T(8,128)}, f32[8,2176]{1,0:T(8,128)}) custom-call(s32[11]{0:T(128)} %pad_add_fusion.info, f32[3]{0:T(128)} %bitcast.20, bf16[4,384,2048]{2,1,0:T(8,128)(2,1)} %bitcast.14, f32[4,16,384]{2,1,0:T(8,128)} %bitcast.17, bf16[2,1024,512]{2,1,0:T(8,128)(2,1)} %constant.16.clone.table_hbm), custom_call_target="tpu_custom_call" | custom-call | flops 12079595520 | bytes 6291456 | tf_op jit(solution)/shard_map/maps/pallas_call | solution.py:305
  14.6 0.5 collective-permute-start.5
  15.1 2.6 %collective-permute-start = (f32[520,128]{1,0:T(8,128)}, f32[520,128]{1,0:T(8,128)S(1)}, u32[]{:S(2)}, u32[]{:S(2)}) collective-permute-start(f32[520,128]{1,0:T(8,128)} %get-tuple-element.24), channel_id=1, source_target_pairs={{0,2},{2,0},{4,6},{6,4},{8,10},{10,8},{12,14},{14,12},{1,3},{3,1},... | collective-permute-start | bytes 798728 | tf_op jit(solution)/shard_map/ppermute | solution.py:493
  17.7 11.6 %maps.4 = (f32[520,128]{1,0:T(8,128)}, f32[520,128]{1,0:T(8,128)}) custom-call(s32[11]{0:T(128)} %pad_add_fusion.info, f32[3]{0:T(128)} %bitcast.21, bf16[4,384,2048]{2,1,0:T(8,128)(2,1)} %bitcast.15, f32[4,16,384]{2,1,0:T(8,128)} %bitcast.18, bf16[2,1024,512]{2,1,0:T(8,128)(2,1)} %constant.16.clone.table_hbm), custom_call_target="tpu_custom_call" | custom-call | flops 12079595520 | bytes 6291456 | tf_op jit(solution)/shard_map/maps/pallas_call | solution.py:305
  29.3 0.1 collective-permute-start.4
  29.4 0.0 collective-permute-done.5.refs_0_
  29.4 0.0 copy-done.8
  29.4 0.0 copy-start.9
  29.4 0.1 fusion.1
  29.5 0.7 concatenate.8.info
  30.2 0.0 collective-permute-done.recv_ref
  30.2 0.0 copy-done.1
  30.2 0.1 merge.3
  30.2 0.0 copy-start.4
  30.2 0.6 copy-done.4
  30.9 2.0 %collective-permute-start.1 = (f32[200,128]{1,0:T(8,128)S(1)}, f32[200,128]{1,0:T(8,128)S(1)}, u32[]{:S(2)}, u32[]{:S(2)}) collective-permute-start(f32[200,128]{1,0:T(8,128)S(1)} %get-tuple-element.26), channel_id=1, source_target_pairs={{0,4},{2,6},{4,0},{6,2},{8,12},{10,14},{12,8},{14,10},{1,5},{3,7},... | collective-permute-start | bytes 307208 | tf_op jit(solution)/shard_map/ppermute | solution.py:461
  32.9 2.6 %collective-permute-start.2 = (f32[200,128]{1,0:T(8,128)S(1)}, f32[200,128]{1,0:T(8,128)S(1)}, u32[]{:S(2)}, u32[]{:S(2)}) collective-permute-start(f32[200,128]{1,0:T(8,128)S(1)} %get-tuple-element.27), channel_id=1, source_target_pairs={{0,8},{2,10},{4,12},{6,14},{8,0},{10,2},{12,4},{14,6},{1,9},{3,11}... | collective-permute-start | bytes 307208 | tf_op jit(solution)/shard_map/ppermute | solution.py:461
  35.5 0.0 collective-permute-start.3
  35.5 0.0 copy-done.9
  35.5 0.0 copy-start.6
  35.5 11.8 %maps.5 = (f32[520,128]{1,0:T(8,128)}, f32[520,128]{1,0:T(8,128)}) custom-call(s32[15]{0:T(128)} %concatenate.8.info, f32[3]{0:T(128)} %bitcast.22, bf16[4,384,2048]{2,1,0:T(8,128)(2,1)} %bitcast.16, f32[4,16,384]{2,1,0:T(8,128)} %bitcast.19, bf16[2,1024,512]{2,1,0:T(8,128)(2,1)} %constant.16.clone.table_hbm, f32[8,2176]{1,0:T(8,128)} %copy-done.9, ...), custom_call_target="tpu_custom_call" | custom-call | flops 12079595520 | bytes 6291456 | tf_op jit(solution)/shard_map/maps/pallas_call | solution.py:305
  47.3 0.0 collective-permute-done.4.recv_ref
  47.3 0.0 collective-permute-done.1.outs_1_.refs_1_
  47.3 0.0 collective-permute-done.2.outs_2_.refs_2_
  47.3 0.0 collective-permute-done.3.outs_3_.refs_3_
  47.4 0.9 %copy-done.3 = f32[520,128]{1,0:T(8,128)S(1)} copy-done((f32[520,128]{1,0:T(8,128)S(1)}, f32[520,128]{1,0:T(8,128)}, u32[]{:S(2)}) %copy-start.3) | copy-done | bytes 266264
  48.3 0.1 merge.4
  48.4 1.8 %collective-permute-start.9 = (f32[520,128]{1,0:T(8,128)S(1)}, f32[520,128]{1,0:T(8,128)S(1)}, u32[]{:S(2)}, u32[]{:S(2)}) collective-permute-start(f32[520,128]{1,0:T(8,128)S(1)} %get-tuple-element.38), channel_id=1, source_target_pairs={{0,2},{2,0},{4,6},{6,4},{8,10},{10,8},{12,14},{14,12},{1,3},{3,1},... | collective-permute-start | bytes 798728 | tf_op jit(solution)/shard_map/ppermute | solution.py:493
  50.2 0.7 collective-permute-start.6
  50.8 3.5 %collective-permute-start.7 = (f32[200,128]{1,0:T(8,128)S(1)}, f32[200,128]{1,0:T(8,128)S(1)}, u32[]{:S(2)}, u32[]{:S(2)}) collective-permute-start(f32[200,128]{1,0:T(8,128)S(1)} %get-tuple-element.35), channel_id=1, source_target_pairs={{0,8},{2,10},{4,12},{6,14},{8,0},{10,2},{12,4},{14,6},{1,9},{3,11}... | collective-permute-start | bytes 307208 | tf_op jit(solution)/shard_map/ppermute | solution.py:461
  54.3 0.2 collective-permute-start.8
  54.6 1.5 %collective-permute-done.9.recv_ref = f32[520,128]{1,0:T(8,128)S(1)} collective-permute-done((f32[520,128]{1,0:T(8,128)S(1)}, f32[520,128]{1,0:T(8,128)S(1)}, u32[]{:S(2)}, u32[]{:S(2)}) %collective-permute-start.9) | collective-permute-done | bytes 266272 | tf_op jit(solution)/shard_map/ppermute | solution.py:493
  56.0 0.9 %copy-done = f32[520,128]{1,0:T(8,128)S(1)} copy-done((f32[520,128]{1,0:T(8,128)S(1)}, f32[520,128]{1,0:T(8,128)}, u32[]{:S(2)}) %copy-start) | copy-done | bytes 266264
  57.0 0.1 merge.5
  57.1 0.7 collective-permute-start.10
  57.7 3.5 %collective-permute-start.11 = (f32[200,128]{1,0:T(8,128)S(1)}, f32[200,128]{1,0:T(8,128)S(1)}, u32[]{:S(2)}, u32[]{:S(2)}) collective-permute-start(f32[200,128]{1,0:T(8,128)S(1)} %get-tuple-element.41), channel_id=1, source_target_pairs={{0,8},{2,10},{4,12},{6,14},{8,0},{10,2},{12,4},{14,6},{1,9},{3,11}... | collective-permute-start | bytes 307208 | tf_op jit(solution)/shard_map/ppermute | solution.py:461
  61.2 0.0 collective-permute-done.6.refs_5_
  61.2 0.3 collective-permute-start.12
  61.5 0.0 collective-permute-done.7.refs_6_
  61.5 0.5 collective-permute-done.8.refs_7_
  62.0 1.2 %collective-permute-done.10.refs_9_ = f32[200,128]{1,0:T(8,128)S(1)} collective-permute-done((f32[200,128]{1,0:T(8,128)S(1)}, f32[200,128]{1,0:T(8,128)S(1)}, u32[]{:S(2)}, u32[]{:S(2)}) %collective-permute-start.10) | collective-permute-done | bytes 102432 | tf_op jit(solution)/shard_map/ppermute | solution.py:461
  63.2 7.0 %collective-permute-done.11.refs_10_ = f32[200,128]{1,0:T(8,128)S(1)} collective-permute-done((f32[200,128]{1,0:T(8,128)S(1)}, f32[200,128]{1,0:T(8,128)S(1)}, u32[]{:S(2)}, u32[]{:S(2)}) %collective-permute-start.11) | collective-permute-done | bytes 102432 | tf_op jit(solution)/shard_map/ppermute | solution.py:461
  70.1 0.0 collective-permute-done.12.refs_11_
  70.1 0.0 copy-done.5
  70.1 1.4 %final.1 = (f32[64,384]{1,0:T(8,128)}, f32[64,384]{1,0:T(8,128)}, f32[64,384]{1,0:T(8,128)}) custom-call(s32[11]{0:T(128)S(1)} %copy-done.6, f32[200,128]{1,0:T(8,128)S(1)} %copy-done.5, f32[200,128]{1,0:T(8,128)S(1)} %collective-permute-done.1.outs_1_.refs_1_, f32[200,128]{1,0:T(8,128)S(1)} %collective-permute-done.2.outs_2_.refs_2_, ...), custom_call_target="tpu_custom_call" | custom-call | tf_op jit(solution)/shard_map/final/pallas_call | solution.py:401
  (10 shorter events, 0.0 us)
Async XLA Ops:
  14.6 14.8 %collective-permute-start.5 = (f32[8,2176]{1,0:T(8,128)}, f32[8,2176]{1,0:T(8,128)S(1)}, u32[]{:S(2)}, u32[]{:S(2)}) collective-permute-start(f32[8,2176]{1,0:T(8,128)} %get-tuple-element.31), channel_id=1, source_target_pairs={{0,1},{1,0},{2,3},{3,2},{4,5},{5,4},{6,7},{7,6},{8,9},{9,8},{10,11... | collective-permute-start | bytes 208904 | tf_op jit(solution)/shard_map/ppermute | solution.py:473
  15.1 14.3 %copy-start.8 = (s32[1,2]{1,0:T(1,128)S(1)}, s32[1,2]{1,0:T(1,128)}, u32[]{:S(2)}) copy-start(s32[1,2]{1,0:T(1,128)} %constant.23) | copy-start | bytes 28
  15.1 14.4 %copy-start.7 = (s32[1,3]{1,0:T(1,128)S(1)}, s32[1,3]{1,0:T(1,128)}, u32[]{:S(2)}) copy-start(s32[1,3]{1,0:T(1,128)} %param.10) | copy-start | bytes 40
  15.1 15.1 %copy-start.1 = (f32[520,128]{1,0:T(8,128)S(1)}, f32[520,128]{1,0:T(8,128)}, u32[]{:S(2)}) copy-start(f32[520,128]{1,0:T(8,128)} %get-tuple-element.23.keep_ref) | copy-start | bytes 798724
  15.1 15.1 %collective-permute-start = (f32[520,128]{1,0:T(8,128)}, f32[520,128]{1,0:T(8,128)S(1)}, u32[]{:S(2)}, u32[]{:S(2)}) collective-permute-start(f32[520,128]{1,0:T(8,128)} %get-tuple-element.24), channel_id=1, source_target_pairs={{0,2},{2,0},{4,6},{6,4},{8,10},{10,8},{12,14},{14,12},{1,3},{3,1},... | collective-permute-start | bytes 798728 | tf_op jit(solution)/shard_map/ppermute | solution.py:493
  29.3 18.0 %collective-permute-start.4 = (f32[520,128]{1,0:T(8,128)}, f32[520,128]{1,0:T(8,128)S(1)}, u32[]{:S(2)}, u32[]{:S(2)}) collective-permute-start(f32[520,128]{1,0:T(8,128)} %get-tuple-element.30), channel_id=1, source_target_pairs={{0,2},{2,0},{4,6},{6,4},{8,10},{10,8},{12,14},{14,12},{1,3},{3,1},... | collective-permute-start | bytes 798728 | tf_op jit(solution)/shard_map/ppermute | solution.py:493
  29.4 6.1 %copy-start.9 = (f32[8,2176]{1,0:T(8,128)}, f32[8,2176]{1,0:T(8,128)S(1)}, u32[]{:S(2)}) copy-start(f32[8,2176]{1,0:T(8,128)S(1)} %collective-permute-done.5.refs_0_) | copy-start | bytes 208900
  30.2 0.6 copy-start.4
  30.9 16.4 %collective-permute-start.1 = (f32[200,128]{1,0:T(8,128)S(1)}, f32[200,128]{1,0:T(8,128)S(1)}, u32[]{:S(2)}, u32[]{:S(2)}) collective-permute-start(f32[200,128]{1,0:T(8,128)S(1)} %get-tuple-element.26), channel_id=1, source_target_pairs={{0,4},{2,6},{4,0},{6,2},{8,12},{10,14},{12,8},{14,10},{1,5},{3,7},... | collective-permute-start | bytes 307208 | tf_op jit(solution)/shard_map/ppermute | solution.py:461
  32.9 14.4 %collective-permute-start.2 = (f32[200,128]{1,0:T(8,128)S(1)}, f32[200,128]{1,0:T(8,128)S(1)}, u32[]{:S(2)}, u32[]{:S(2)}) collective-permute-start(f32[200,128]{1,0:T(8,128)S(1)} %get-tuple-element.27), channel_id=1, source_target_pairs={{0,8},{2,10},{4,12},{6,14},{8,0},{10,2},{12,4},{14,6},{1,9},{3,11}... | collective-permute-start | bytes 307208 | tf_op jit(solution)/shard_map/ppermute | solution.py:461
  35.5 11.8 %collective-permute-start.3 = (f32[200,128]{1,0:T(8,128)S(1)}, f32[200,128]{1,0:T(8,128)S(1)}, u32[]{:S(2)}, u32[]{:S(2)}) collective-permute-start(f32[200,128]{1,0:T(8,128)S(1)} %get-tuple-element.28), channel_id=1, source_target_pairs={{0,12},{2,14},{4,8},{6,10},{8,4},{10,6},{12,0},{14,2},{1,13},{3,15... | collective-permute-start | bytes 307208 | tf_op jit(solution)/shard_map/ppermute | solution.py:461
  35.5 11.8 %copy-start.2 = (f32[520,128]{1,0:T(8,128)S(1)}, f32[520,128]{1,0:T(8,128)}, u32[]{:S(2)}) copy-start(f32[520,128]{1,0:T(8,128)} %get-tuple-element.29.keep_ref) | copy-start | bytes 798724
  35.5 34.6 %copy-start.5 = (f32[200,128]{1,0:T(8,128)S(1)}, f32[200,128]{1,0:T(8,128)}, u32[]{:S(2)}) copy-start(f32[200,128]{1,0:T(8,128)} %copy-done.4) | copy-start | bytes 307204
  35.5 34.6 %copy-start.6 = (s32[11]{0:T(128)S(1)}, s32[11]{0:T(128)}, u32[]{:S(2)}) copy-start(s32[11]{0:T(128)} %pad_add_fusion.info) | copy-start | bytes 136
  47.3 1.0 %copy-start.3 = (f32[520,128]{1,0:T(8,128)S(1)}, f32[520,128]{1,0:T(8,128)}, u32[]{:S(2)}) copy-start(f32[520,128]{1,0:T(8,128)} %get-tuple-element.32.outs_0_) | copy-start | bytes 798724
  48.4 7.7 %collective-permute-start.9 = (f32[520,128]{1,0:T(8,128)S(1)}, f32[520,128]{1,0:T(8,128)S(1)}, u32[]{:S(2)}, u32[]{:S(2)}) collective-permute-start(f32[520,128]{1,0:T(8,128)S(1)} %get-tuple-element.38), channel_id=1, source_target_pairs={{0,2},{2,0},{4,6},{6,4},{8,10},{10,8},{12,14},{14,12},{1,3},{3,1},... | collective-permute-start | bytes 798728 | tf_op jit(solution)/shard_map/ppermute | solution.py:493
  50.2 11.1 %collective-permute-start.6 = (f32[200,128]{1,0:T(8,128)S(1)}, f32[200,128]{1,0:T(8,128)S(1)}, u32[]{:S(2)}, u32[]{:S(2)}) collective-permute-start(f32[200,128]{1,0:T(8,128)S(1)} %get-tuple-element.34), channel_id=1, source_target_pairs={{0,4},{2,6},{4,0},{6,2},{8,12},{10,14},{12,8},{14,10},{1,5},{3,7},... | collective-permute-start | bytes 307208 | tf_op jit(solution)/shard_map/ppermute | solution.py:461
  50.8 10.7 %collective-permute-start.7 = (f32[200,128]{1,0:T(8,128)S(1)}, f32[200,128]{1,0:T(8,128)S(1)}, u32[]{:S(2)}, u32[]{:S(2)}) collective-permute-start(f32[200,128]{1,0:T(8,128)S(1)} %get-tuple-element.35), channel_id=1, source_target_pairs={{0,8},{2,10},{4,12},{6,14},{8,0},{10,2},{12,4},{14,6},{1,9},{3,11}... | collective-permute-start | bytes 307208 | tf_op jit(solution)/shard_map/ppermute | solution.py:461
  54.3 7.7 %collective-permute-start.8 = (f32[200,128]{1,0:T(8,128)S(1)}, f32[200,128]{1,0:T(8,128)S(1)}, u32[]{:S(2)}, u32[]{:S(2)}) collective-permute-start(f32[200,128]{1,0:T(8,128)S(1)} %get-tuple-element.36), channel_id=1, source_target_pairs={{0,12},{2,14},{4,8},{6,10},{8,4},{10,6},{12,0},{14,2},{1,13},{3,15... | collective-permute-start | bytes 307208 | tf_op jit(solution)/shard_map/ppermute | solution.py:461
  56.0 1.0 %copy-start = (f32[520,128]{1,0:T(8,128)S(1)}, f32[520,128]{1,0:T(8,128)}, u32[]{:S(2)}) copy-start(f32[520,128]{1,0:T(8,128)} %get-tuple-element.37.keep_ref) | copy-start | bytes 798724
  57.1 6.1 %collective-permute-start.10 = (f32[200,128]{1,0:T(8,128)S(1)}, f32[200,128]{1,0:T(8,128)S(1)}, u32[]{:S(2)}, u32[]{:S(2)}) collective-permute-start(f32[200,128]{1,0:T(8,128)S(1)} %get-tuple-element.40), channel_id=1, source_target_pairs={{0,4},{2,6},{4,0},{6,2},{8,12},{10,14},{12,8},{14,10},{1,5},{3,7},... | collective-permute-start | bytes 307208 | tf_op jit(solution)/shard_map/ppermute | solution.py:461
  57.7 12.4 %collective-permute-start.11 = (f32[200,128]{1,0:T(8,128)S(1)}, f32[200,128]{1,0:T(8,128)S(1)}, u32[]{:S(2)}, u32[]{:S(2)}) collective-permute-start(f32[200,128]{1,0:T(8,128)S(1)} %get-tuple-element.41), channel_id=1, source_target_pairs={{0,8},{2,10},{4,12},{6,14},{8,0},{10,2},{12,4},{14,6},{1,9},{3,11}... | collective-permute-start | bytes 307208 | tf_op jit(solution)/shard_map/ppermute | solution.py:461
  61.2 8.9 %collective-permute-start.12 = (f32[200,128]{1,0:T(8,128)S(1)}, f32[200,128]{1,0:T(8,128)S(1)}, u32[]{:S(2)}, u32[]{:S(2)}) collective-permute-start(f32[200,128]{1,0:T(8,128)S(1)} %get-tuple-element.42), channel_id=1, source_target_pairs={{0,12},{2,14},{4,8},{6,10},{8,4},{10,6},{12,0},{14,2},{1,13},{3,15... | collective-permute-start | bytes 307208 | tf_op jit(solution)/shard_map/ppermute | solution.py:461

commit v5 on v4

--- a/solution.py
+++ b/solution.py
@@ -35,9 +35,17 @@
     return np.stack([even, odd]).astype(ml_dtypes.bfloat16), norms, edge
 
 
+class Whole:
+    def __init__(self, ref):
+        self.ref = ref
+
+    def __getitem__(self, at):
+        return self.ref[at].astype(jnp.int32)
+
+
 def maps_kernel(
-    norms, edge, strips, step, count, outer, gives_edge, waits, info, bias, x_hbm, scale_ref,
-    table_hbm, *refs,
+    norms, edge, strips, step, count, outer, gives_edge, waits, near_tables, values, x_hbm, scale_ref,
+    table_in, *refs,
 ):
     refs = list(refs)
     ext_ref = refs.pop(0) if outer[0] or outer[1] else None
@@ -45,12 +53,16 @@
         refs.pop(0)
     send_ref, keep_ref = refs.pop(0), refs.pop(0)
     give_ref = refs.pop(0) if gives_edge else None
-    rough_ref, struct_ref, x_ref, level_ref, near_ref, even_ref, odd_ref, sems, *scratch = refs
+    rough_ref, struct_ref, x_ref, level_ref, near_ref, sems = refs[:6]
+    scratch = refs[6:]
+    if not near_tables:
+        table_ref = scratch.pop()
     lines = LANES
     samples = x_hbm.shape[-1]
     blocks = samples // LANES
     parts = lines // SUB
     rows = REPEATS * SUB
+    info = Whole(values)
     flip = info[0]
     tile = jnp.where(flip == 1, count - 1 - step, step)
     lane = lax.broadcasted_iota(jnp.int32, (SUB, LANES), 1)
@@ -69,10 +81,12 @@
         x_ref.at[:, SUB:lines, :],
         sems.at[5],
     )
-    tables = [
-        pltpu.make_async_copy(table_hbm.at[n], ref, sems.at[1 + n])
-        for n, ref in enumerate((even_ref, odd_ref))
-    ]
+    tables = []
+    if near_tables:
+        even_ref, odd_ref = table_in.at[0], table_in.at[1]
+    else:
+        even_ref, odd_ref = table_ref.at[0], table_ref.at[1]
+        tables.append(pltpu.make_async_copy(table_in, table_ref, sems.at[1]))
     starts = [base_prev, base_next]
     if gives_edge:
         base_give = pl.multiple_of(jnp.where(flip == 1, 0, line_count - SUB), SUB)
@@ -152,7 +166,7 @@
     first, last = limits(tile)
     prev_first, prev_last = limits(jnp.maximum(tile - 1, 0))
     next_first, next_last = limits(jnp.minimum(tile + 1, count - 1))
-    out_at = 2 + 3 * count
+    out_at = 2 + 4 * count
     prev_first = jnp.where(at_start, info[out_at] if outer[0] else 1 << 20, prev_first)
     prev_last = jnp.where(at_start, info[out_at + 1] if outer[0] else -1, prev_last)
     next_first = jnp.where(at_end, info[out_at + 2] if outer[1] else 1 << 20, next_first)
@@ -258,7 +272,7 @@
 
     pick = info[2 + 2 * count + tile]
     chosen = struct_ref[:, pl.ds(pl.multiple_of(pick * LANES, LANES), LANES)]
-    score = jnp.sum(chosen) * (1.0 / (LANES * lines)) + bias[tile]
+    score = jnp.sum(chosen) * (1.0 / (LANES * lines)) + values[2 + 3 * count + tile]
     smooth = TAPS[0] * rough_ref[SUB - 2 : SUB - 2 + lines, :]
     for k in range(1, 5):
         smooth = smooth + TAPS[k] * rough_ref[SUB - 2 + k : SUB - 2 + k + lines, :]
@@ -281,10 +295,13 @@
 
 
 SUB = 16
+MIB = 1024 * 1024
+NEAR = (True, True, True)
+LIMIT = (48 * MIB, 48 * MIB, 48 * MIB)
 SPLIT = 2
 
 
-def maps_call(step, count, outer, gives_edge, info, bias, spectra, scales, extra, table, norms, edge, strips):
+def maps_call(step, count, outer, gives_edge, info, spectra, scales, extra, table, norms, edge, strips):
     samples = spectra.shape[-1]
     rows = BANDS * REPEATS * SUB
     out = jax.ShapeDtypeStruct((DEPTH + 8, LANES), jnp.float32)
@@ -302,33 +319,35 @@
         pltpu.VMEM((rows, half), jnp.bfloat16),
         pltpu.VMEM((rows, LANES), jnp.float32),
     ]
+    scratch = [
+        pltpu.VMEM((LANES + 2 * SUB, DEPTH), jnp.float32),
+        pltpu.VMEM((LANES, DEPTH), jnp.float32),
+        pltpu.VMEM((REPEATS, LANES + SUB, samples), jnp.bfloat16),
+        pltpu.VMEM((REPEATS, LANES + SUB, samples // LANES), jnp.float32),
+        pltpu.VMEM((3, REPEATS, SUB, samples), jnp.bfloat16),
+        pltpu.SemaphoreType.DMA((7,)),
+    ] + pair + pair
+    near_tables = NEAR[step]
+    if not near_tables:
+        scratch.append(pltpu.VMEM((2, half, DEPTH), jnp.bfloat16))
     return pl.pallas_call(
         functools.partial(
-            maps_kernel, norms, edge, strips, step, count, outer, gives_edge, waits
+            maps_kernel, norms, edge, strips, step, count, outer, gives_edge, waits, near_tables
         ),
-        in_specs=[pl.BlockSpec(memory_space=pltpu.SMEM)] * 2
-        + [remote, whole, remote]
+        in_specs=[pl.BlockSpec(memory_space=pltpu.SMEM)]
+        + [remote, whole, whole if near_tables else remote]
         + [whole] * has_ext + [pl.BlockSpec(memory_space=pl.ANY)] * waits,
         out_specs=[whole] * len(outs),
-        scratch_shapes=[
-            pltpu.VMEM((LANES + 2 * SUB, DEPTH), jnp.float32),
-            pltpu.VMEM((LANES, DEPTH), jnp.float32),
-            pltpu.VMEM((REPEATS, LANES + SUB, samples), jnp.bfloat16),
-            pltpu.VMEM((REPEATS, LANES + SUB, samples // LANES), jnp.float32),
-            pltpu.VMEM((3, REPEATS, SUB, samples), jnp.bfloat16),
-            pltpu.VMEM((half, DEPTH), jnp.bfloat16),
-            pltpu.VMEM((half, DEPTH), jnp.bfloat16),
-            pltpu.SemaphoreType.DMA((7,)),
-        ] + pair + pair,
+        scratch_shapes=scratch,
         out_shape=outs,
-        compiler_params=pltpu.CompilerParams(vmem_limit_bytes=25 * 1024 * 1024 * 5 // 2),
+        compiler_params=pltpu.CompilerParams(vmem_limit_bytes=LIMIT[step]),
         cost_estimate=pl.CostEstimate(
             flops=5 * BANDS * REPEATS * (LANES + SUB) * samples * DEPTH,
             bytes_accessed=2 * REPEATS * LANES * samples + 4 * samples * DEPTH,
             transcendentals=0,
         ),
         name="maps",
-    )(info, bias, spectra, scales, table, *extra)
+    )(info, spectra, scales, table, *extra)
 
 
 def merge_kernel(rows, strip, shares, tied, vol, keep_ref, recv_ref, *outs):
@@ -430,15 +449,21 @@
     lines = spectra.shape[1]
 
     at = samples + scales.shape[2]
-    none = jnp.array([1 << 20, -1], jnp.int32)
+    none = jnp.array([1 << 20, -1], jnp.float32)
     flip = (here == 1).astype(jnp.int32) if tiles == 2 else jnp.zeros((), jnp.int32)
     info = jnp.concatenate(
-        [flip[None], vol[None].astype(jnp.int32), retina.reshape(-1), quality]
-    ).astype(jnp.int32)
+        [
+            flip[None].astype(jnp.float32),
+            vol[None].astype(jnp.float32),
+            retina.reshape(-1).astype(jnp.float32),
+            quality.astype(jnp.float32),
+            bias,
+        ]
+    )
 
     def with_limits(before, after):
-        before_block = jnp.where(here == 0, none, before[0, at : at + 2].astype(jnp.int32))
-        after_block = jnp.where(here == tiles - 1, none, after[0, at : at + 2].astype(jnp.int32))
+        before_block = jnp.where(here == 0, none, before[0, at : at + 2])
+        after_block = jnp.where(here == tiles - 1, none, after[0, at : at + 2])
         return jnp.concatenate([info, before_block, after_block])
 
     if tiles == 2:
@@ -482,7 +507,7 @@
                 merge(0, [])
             extra.append(parts[i - 2][0])
         send, keep, *rest = maps_call(
-            i, count, outer, gives_edge, step_info, bias,
+            i, count, outer, gives_edge, step_info,
             spectra, scales, extra, table, norms, edge, strips,
         )
         if gives_edge:

time: 71.8 us -> 68.4 us (0.953)
  Pallas kernels: 36.7 us -> 31.2 us
  local copies, waits for them, and re-layouts: 4.07 us -> 5.08 us
  waiting for transfers between devices: 10.1 us -> 11 us
    pallas_call x3, Pallas kernels: 35.1 us -> 29.7 us  [maps_call(): pl.pallas_call(functools.partial(maps_kernel, norms, edge, strips, step,...]
    convert_element_type x0 -> x2, other arithmetic: none -> 1.34 us  [the longest x1 0.68 us: on_device(): retina.reshape(-1).astype(jnp.float32)]
    concatenate x1 -> x0, other arithmetic: 1.31 us -> none  [on_device(): jnp.concatenate([flip[None], vol[None].astype(jnp.int32), retina.reshape(...]
    ppermute x9, waiting for transfers between devices: 8.61 us -> 9.57 us  [merge(): lax.ppermute(p, 'vol', [(v, v ^ 2 * d) for v in range(strips)])]
    unnamed x21 -> x12, local copies, waits for them, and re-layouts: 3.32 us -> 4.09 us
    concatenate x0 -> x1, local copies, waits for them, and re-layouts: none -> 0.73 us  [on_device(): jnp.concatenate([flip[None].astype(jnp.float32), vol[None].astype(jnp.flo...]
  transfers between devices with their start and end apart: 13 -> 13, of which waited for: 4 -> 3; matrix products, arithmetic and copies ran while one was open for 1% -> 0% of each run, Pallas kernels for 33% -> 29%
where the time goes in v5:
time: 68.4 us; the launch traced here: 68.1 us
  Pallas kernels  31.2 us (46%)
  starting transfers between devices  18.6 us (27%)
  waiting for transfers between devices  11 us (16%)
  local copies, waits for them, and re-layouts  5.08 us (7%)
  other arithmetic  1.41 us (2%)
  between operations  0.73 us (1%)
    pallas_call x3, Pallas kernels, maps_call(): pl.pallas_call(functools.partial(maps_kernel, norms, edge, strips, step,...  29.7 us
    ppermute x9, starting transfers between devices, merge(): lax.ppermute(p, 'vol', [(v, v ^ 2 * d) for v in range(strips)])  13.5 us
    ppermute x9, waiting for transfers between devices, merge(): lax.ppermute(p, 'vol', [(v, v ^ 2 * d) for v in range(strips)])  9.57 us
    ppermute x3, starting transfers between devices, on_device(): arrived.append(lax.ppermute(send, 'vol', swap))  4.56 us
    unnamed x12, local copies, waits for them, and re-layouts  4.09 us
    ppermute x3, waiting for transfers between devices, on_device(): arrived.append(lax.ppermute(send, 'vol', swap))  1.48 us
  transfers between devices with their start and end apart: 13, of which 3 were waited for; matrix products, arithmetic and copies ran while one was open for 0% of the time, Pallas kernels for 29%

profile of v5, /device:TPU:0, one launch (start us, length us, event | category | flops | bytes accessed | tf_op | source)
XLA Modules:
  0.0 68.1 jit_solution(5055557374336830899)
XLA Ops:
  0.6 0.7 convert_bitcast_fusion
  1.3 0.7 convert_element_type.28
  2.0 0.1 copy.12
  2.1 0.1 convert_element_type.29
  2.2 0.7 %concatenate.7.values.info = f32[14]{0:T(128)S(1)} concatenate(f32[1]{0:T(128)} %bitcast, f32[1]{0:T(128)S(6)} %convert_element_type.27, f32[6]{0:T(128)S(1)} %convert_element_type.29, f32[3]{0:T(128)S(1)} %convert_bitcast_fusion, f32[3]{0:T(128)} %bitcast.16), dimensions={0} | concatenate | bytes 112 | tf_op jit(solution)/shard_map/concatenate | solution.py:454
  2.9 0.0 copy-start
  2.9 0.9 %copy-done = f32[1,4,384,16]{2,3,1,0:T(8,128)S(1)} copy-done((f32[1,4,384,16]{2,3,1,0:T(8,128)S(1)}, f32[1,4,384,16]{2,3,1,0:T(8,128)}, u32[]{:S(2)}) %copy-start) | copy-done | bytes 98328
  3.8 0.0 copy-start.2
  3.8 1.6 %copy-done.2 = bf16[2,1024,512]{2,1,0:T(8,128)(2,1)S(1)} copy-done((bf16[2,1024,512]{2,1,0:T(8,128)(2,1)S(1)}, bf16[2,1024,512]{2,1,0:T(8,128)(2,1)}, u32[]{:S(2)}) %copy-start.2) | copy-done | bytes 2097176
  5.4 10.0 %maps.3 = (f32[520,128]{1,0:T(8,128)S(1)}, f32[520,128]{1,0:T(8,128)S(1)}, f32[8,2176]{1,0:T(8,128)S(1)}) custom-call(f32[14]{0:T(128)S(1)} %concatenate.7.values.info, bf16[4,384,2048]{2,1,0:T(8,128)(2,1)} %bitcast.18, f32[4,16,384]{2,1,0:T(8,128)S(1)} %bitcast.13, bf16[2,1024,512]{2,1,0:T(8,128)(2,1)S(1)} %copy-done.2), custom_call_target="tpu_custom_call" | custom-call | flops 12079595520 | bytes 6291456 | tf_op jit(solution)/shard_map/maps/pallas_call | solution.py:333
  15.4 0.5 collective-permute-start.5
  15.9 2.6 %collective-permute-start = (f32[520,128]{1,0:T(8,128)S(1)}, f32[520,128]{1,0:T(8,128)S(1)}, u32[]{:S(2)}, u32[]{:S(2)}) collective-permute-start(f32[520,128]{1,0:T(8,128)S(1)} %get-tuple-element.24), channel_id=1, source_target_pairs={{0,2},{2,0},{4,6},{6,4},{8,10},{10,8},{12,14},{14,12},{1,3},{3,1},... | collective-permute-start | bytes 798728 | tf_op jit(solution)/shard_map/ppermute | solution.py:518
  18.5 9.8 %maps.4 = (f32[520,128]{1,0:T(8,128)S(1)}, f32[520,128]{1,0:T(8,128)S(1)}) custom-call(f32[14]{0:T(128)S(1)} %concatenate.7.values.info, bf16[4,384,2048]{2,1,0:T(8,128)(2,1)} %bitcast.19, f32[4,16,384]{2,1,0:T(8,128)S(1)} %bitcast.14, bf16[2,1024,512]{2,1,0:T(8,128)(2,1)S(1)} %copy-done.2), custom_call_target="tpu_custom_call" | custom-call | flops 12079595520 | bytes 6291456 | tf_op jit(solution)/shard_map/maps/pallas_call | solution.py:333
  28.3 0.1 collective-permute-start.4
  28.4 0.0 collective-permute-done.5.refs_0_
  28.4 0.0 copy-done.5
  28.4 0.1 fusion.1
  28.5 0.0 copy-done.4
  28.5 0.1 concatenate.8.values
  28.6 0.0 collective-permute-done.recv_ref
  28.6 0.1 merge.3
  28.7 2.1 %collective-permute-start.1 = (f32[200,128]{1,0:T(8,128)S(1)}, f32[200,128]{1,0:T(8,128)S(1)}, u32[]{:S(2)}, u32[]{:S(2)}) collective-permute-start(f32[200,128]{1,0:T(8,128)S(1)} %get-tuple-element.26), channel_id=1, source_target_pairs={{0,4},{2,6},{4,0},{6,2},{8,12},{10,14},{12,8},{14,10},{1,5},{3,7},... | collective-permute-start | bytes 307208 | tf_op jit(solution)/shard_map/ppermute | solution.py:486
  30.7 2.6 %collective-permute-start.2 = (f32[200,128]{1,0:T(8,128)S(1)}, f32[200,128]{1,0:T(8,128)S(1)}, u32[]{:S(2)}, u32[]{:S(2)}) collective-permute-start(f32[200,128]{1,0:T(8,128)S(1)} %get-tuple-element.27), channel_id=1, source_target_pairs={{0,8},{2,10},{4,12},{6,14},{8,0},{10,2},{12,4},{14,6},{1,9},{3,11}... | collective-permute-start | bytes 307208 | tf_op jit(solution)/shard_map/ppermute | solution.py:486
  33.3 0.0 collective-permute-start.3
  33.3 0.0 copy-done.1
  33.3 1.6 %copy-done.3 = bf16[2,1024,512]{2,1,0:T(8,128)(2,1)S(1)} copy-done((bf16[2,1024,512]{2,1,0:T(8,128)(2,1)S(1)}, bf16[2,1024,512]{2,1,0:T(8,128)(2,1)}, u32[]{:S(2)}) %copy-start.3) | copy-done | bytes 2097176
  34.9 9.9 %maps.5 = (f32[520,128]{1,0:T(8,128)S(1)}, f32[520,128]{1,0:T(8,128)S(1)}) custom-call(f32[18]{0:T(128)S(1)} %concatenate.8.values, bf16[4,384,2048]{2,1,0:T(8,128)(2,1)} %bitcast.20, f32[4,16,384]{2,1,0:T(8,128)S(1)} %bitcast.15, bf16[2,1024,512]{2,1,0:T(8,128)(2,1)S(1)} %copy-done.3, f32[8,2176]{1,0:T(8,128)S(1)} %collective-permute-done.5.refs_0_, ...), custom_call_target="tpu_custom_call" | custom-call | flops 12079595520 | bytes 6291456 | tf_op jit(solution)/shard_map/maps/pallas_call | solution.py:333
  44.9 0.0 collective-permute-done.4.recv_ref
  44.9 0.0 collective-permute-done.1.outs_1_.refs_1_
  44.9 0.0 collective-permute-done.2.outs_2_.refs_2_
  44.9 0.0 collective-permute-done.3.outs_3_.refs_3_
  44.9 0.1 merge.4
  45.0 1.8 %collective-permute-start.9 = (f32[520,128]{1,0:T(8,128)S(1)}, f32[520,128]{1,0:T(8,128)S(1)}, u32[]{:S(2)}, u32[]{:S(2)}) collective-permute-start(f32[520,128]{1,0:T(8,128)S(1)} %get-tuple-element.38), channel_id=1, source_target_pairs={{0,2},{2,0},{4,6},{6,4},{8,10},{10,8},{12,14},{14,12},{1,3},{3,1},... | collective-permute-start | bytes 798728 | tf_op jit(solution)/shard_map/ppermute | solution.py:518
  46.8 0.7 collective-permute-start.6
  47.5 3.5 %collective-permute-start.7 = (f32[200,128]{1,0:T(8,128)S(1)}, f32[200,128]{1,0:T(8,128)S(1)}, u32[]{:S(2)}, u32[]{:S(2)}) collective-permute-start(f32[200,128]{1,0:T(8,128)S(1)} %get-tuple-element.35), channel_id=1, source_target_pairs={{0,8},{2,10},{4,12},{6,14},{8,0},{10,2},{12,4},{14,6},{1,9},{3,11}... | collective-permute-start | bytes 307208 | tf_op jit(solution)/shard_map/ppermute | solution.py:486
  51.0 0.2 collective-permute-start.8
  51.2 1.5 %collective-permute-done.9.recv_ref = f32[520,128]{1,0:T(8,128)S(1)} collective-permute-done((f32[520,128]{1,0:T(8,128)S(1)}, f32[520,128]{1,0:T(8,128)S(1)}, u32[]{:S(2)}, u32[]{:S(2)}) %collective-permute-start.9) | collective-permute-done | bytes 266272 | tf_op jit(solution)/shard_map/ppermute | solution.py:518
  52.6 0.1 merge.5
  52.7 0.7 %collective-permute-start.10 = (f32[200,128]{1,0:T(8,128)S(1)}, f32[200,128]{1,0:T(8,128)S(1)}, u32[]{:S(2)}, u32[]{:S(2)}) collective-permute-start(f32[200,128]{1,0:T(8,128)S(1)} %get-tuple-element.40), channel_id=1, source_target_pairs={{0,4},{2,6},{4,0},{6,2},{8,12},{10,14},{12,8},{14,10},{1,5},{3,7},... | collective-permute-start | bytes 307208 | tf_op jit(solution)/shard_map/ppermute | solution.py:486
  53.4 3.5 %collective-permute-start.11 = (f32[200,128]{1,0:T(8,128)S(1)}, f32[200,128]{1,0:T(8,128)S(1)}, u32[]{:S(2)}, u32[]{:S(2)}) collective-permute-start(f32[200,128]{1,0:T(8,128)S(1)} %get-tuple-element.41), channel_id=1, source_target_pairs={{0,8},{2,10},{4,12},{6,14},{8,0},{10,2},{12,4},{14,6},{1,9},{3,11}... | collective-permute-start | bytes 307208 | tf_op jit(solution)/shard_map/ppermute | solution.py:486
  56.9 0.0 collective-permute-done.6.refs_5_
  56.9 0.3 collective-permute-start.12
  57.2 2.0 %collective-permute-done.7.refs_6_ = f32[200,128]{1,0:T(8,128)S(1)} collective-permute-done((f32[200,128]{1,0:T(8,128)S(1)}, f32[200,128]{1,0:T(8,128)S(1)}, u32[]{:S(2)}, u32[]{:S(2)}) %collective-permute-start.7) | collective-permute-done | bytes 102432 | tf_op jit(solution)/shard_map/ppermute | solution.py:486
  59.2 0.0 collective-permute-done.8.refs_7_
  59.2 0.0 collective-permute-done.10.refs_9_
  59.2 7.5 %collective-permute-done.11.refs_10_ = f32[200,128]{1,0:T(8,128)S(1)} collective-permute-done((f32[200,128]{1,0:T(8,128)S(1)}, f32[200,128]{1,0:T(8,128)S(1)}, u32[]{:S(2)}, u32[]{:S(2)}) %collective-permute-start.11) | collective-permute-done | bytes 102432 | tf_op jit(solution)/shard_map/ppermute | solution.py:486
  66.7 0.0 collective-permute-done.12.refs_11_
  66.7 1.4 %final.1 = (f32[64,384]{1,0:T(8,128)}, f32[64,384]{1,0:T(8,128)}, f32[64,384]{1,0:T(8,128)}) custom-call(f32[14]{0:T(128)S(1)} %concatenate.7.values.info, f32[200,128]{1,0:T(8,128)S(1)} %get-tuple-element.25.refs_1_.refs_0_, f32[200,128]{1,0:T(8,128)S(1)} %collective-permute-done.1.outs_1_.refs_1_, f32[200,128]{1,0:T(8,128)S(1)} %collective-permute-done.2.outs_2_.refs_2_, ...), custom_call_target="tpu_custom_call" | custom-call | tf_op jit(solution)/shard_map/final/pallas_call | solution.py:420
  (4 shorter events, 0.0 us)
Async XLA Ops:
  2.9 0.9 %copy-start = (f32[1,4,384,16]{2,3,1,0:T(8,128)S(1)}, f32[1,4,384,16]{2,3,1,0:T(8,128)}, u32[]{:S(2)}) copy-start(f32[1,4,384,16]{2,3,1,0:T(8,128)} %param.8) | copy-start | bytes 294916
  3.8 1.6 %copy-start.2 = (bf16[2,1024,512]{2,1,0:T(8,128)(2,1)S(1)}, bf16[2,1024,512]{2,1,0:T(8,128)(2,1)}, u32[]{:S(2)}) copy-start(bf16[2,1024,512]{2,1,0:T(8,128)(2,1)} %constant.16.clone.table_in) | copy-start | bytes 6291460
  15.4 13.0 %collective-permute-start.5 = (f32[8,2176]{1,0:T(8,128)S(1)}, f32[8,2176]{1,0:T(8,128)S(1)}, u32[]{:S(2)}, u32[]{:S(2)}) collective-permute-start(f32[8,2176]{1,0:T(8,128)S(1)} %get-tuple-element.31), channel_id=1, source_target_pairs={{0,1},{1,0},{2,3},{3,2},{4,5},{5,4},{6,7},{7,6},{8,9},{9,8},{10,11... | collective-permute-start | bytes 208904 | tf_op jit(solution)/shard_map/ppermute | solution.py:498
  15.9 12.5 %copy-start.5 = (f32[1,2]{1,0:T(1,128)S(1)}, f32[1,2]{1,0:T(1,128)}, u32[]{:S(2)}) copy-start(f32[1,2]{1,0:T(1,128)} %constant.23) | copy-start | bytes 28
  15.9 12.6 %copy-start.4 = (f32[1,3]{1,0:T(1,128)S(1)}, f32[1,3]{1,0:T(1,128)}, u32[]{:S(2)}) copy-start(f32[1,3]{1,0:T(1,128)} %param.11) | copy-start | bytes 40
  15.9 17.4 %copy-start.1 = (f32[1,4,384,16]{2,3,1,0:T(8,128)S(1)}, f32[1,4,384,16]{2,3,1,0:T(8,128)}, u32[]{:S(2)}) copy-start(f32[1,4,384,16]{2,3,1,0:T(8,128)} %param.8) | copy-start | bytes 294916
  15.9 12.7 %collective-permute-start = (f32[520,128]{1,0:T(8,128)S(1)}, f32[520,128]{1,0:T(8,128)S(1)}, u32[]{:S(2)}, u32[]{:S(2)}) collective-permute-start(f32[520,128]{1,0:T(8,128)S(1)} %get-tuple-element.24), channel_id=1, source_target_pairs={{0,2},{2,0},{4,6},{6,4},{8,10},{10,8},{12,14},{14,12},{1,3},{3,1},... | collective-permute-start | bytes 798728 | tf_op jit(solution)/shard_map/ppermute | solution.py:518
  28.3 16.6 %collective-permute-start.4 = (f32[520,128]{1,0:T(8,128)S(1)}, f32[520,128]{1,0:T(8,128)S(1)}, u32[]{:S(2)}, u32[]{:S(2)}) collective-permute-start(f32[520,128]{1,0:T(8,128)S(1)} %get-tuple-element.30), channel_id=1, source_target_pairs={{0,2},{2,0},{4,6},{6,4},{8,10},{10,8},{12,14},{14,12},{1,3},{3,1},... | collective-permute-start | bytes 798728 | tf_op jit(solution)/shard_map/ppermute | solution.py:518
  28.7 16.2 %collective-permute-start.1 = (f32[200,128]{1,0:T(8,128)S(1)}, f32[200,128]{1,0:T(8,128)S(1)}, u32[]{:S(2)}, u32[]{:S(2)}) collective-permute-start(f32[200,128]{1,0:T(8,128)S(1)} %get-tuple-element.26), channel_id=1, source_target_pairs={{0,4},{2,6},{4,0},{6,2},{8,12},{10,14},{12,8},{14,10},{1,5},{3,7},... | collective-permute-start | bytes 307208 | tf_op jit(solution)/shard_map/ppermute | solution.py:486
  30.7 14.1 %collective-permute-start.2 = (f32[200,128]{1,0:T(8,128)S(1)}, f32[200,128]{1,0:T(8,128)S(1)}, u32[]{:S(2)}, u32[]{:S(2)}) collective-permute-start(f32[200,128]{1,0:T(8,128)S(1)} %get-tuple-element.27), channel_id=1, source_target_pairs={{0,8},{2,10},{4,12},{6,14},{8,0},{10,2},{12,4},{14,6},{1,9},{3,11}... | collective-permute-start | bytes 307208 | tf_op jit(solution)/shard_map/ppermute | solution.py:486
  33.3 11.6 %collective-permute-start.3 = (f32[200,128]{1,0:T(8,128)S(1)}, f32[200,128]{1,0:T(8,128)S(1)}, u32[]{:S(2)}, u32[]{:S(2)}) collective-permute-start(f32[200,128]{1,0:T(8,128)S(1)} %get-tuple-element.28), channel_id=1, source_target_pairs={{0,12},{2,14},{4,8},{6,10},{8,4},{10,6},{12,0},{14,2},{1,13},{3,15... | collective-permute-start | bytes 307208 | tf_op jit(solution)/shard_map/ppermute | solution.py:486
  33.3 1.6 %copy-start.3 = (bf16[2,1024,512]{2,1,0:T(8,128)(2,1)S(1)}, bf16[2,1024,512]{2,1,0:T(8,128)(2,1)}, u32[]{:S(2)}) copy-start(bf16[2,1024,512]{2,1,0:T(8,128)(2,1)} %constant.16.clone.table_in) | copy-start | bytes 6291460
  45.0 7.7 %collective-permute-start.9 = (f32[520,128]{1,0:T(8,128)S(1)}, f32[520,128]{1,0:T(8,128)S(1)}, u32[]{:S(2)}, u32[]{:S(2)}) collective-permute-start(f32[520,128]{1,0:T(8,128)S(1)} %get-tuple-element.38), channel_id=1, source_target_pairs={{0,2},{2,0},{4,6},{6,4},{8,10},{10,8},{12,14},{14,12},{1,3},{3,1},... | collective-permute-start | bytes 798728 | tf_op jit(solution)/shard_map/ppermute | solution.py:518
  46.8 10.1 %collective-permute-start.6 = (f32[200,128]{1,0:T(8,128)S(1)}, f32[200,128]{1,0:T(8,128)S(1)}, u32[]{:S(2)}, u32[]{:S(2)}) collective-permute-start(f32[200,128]{1,0:T(8,128)S(1)} %get-tuple-element.34), channel_id=1, source_target_pairs={{0,4},{2,6},{4,0},{6,2},{8,12},{10,14},{12,8},{14,10},{1,5},{3,7},... | collective-permute-start | bytes 307208 | tf_op jit(solution)/shard_map/ppermute | solution.py:486
  47.5 11.7 %collective-permute-start.7 = (f32[200,128]{1,0:T(8,128)S(1)}, f32[200,128]{1,0:T(8,128)S(1)}, u32[]{:S(2)}, u32[]{:S(2)}) collective-permute-start(f32[200,128]{1,0:T(8,128)S(1)} %get-tuple-element.35), channel_id=1, source_target_pairs={{0,8},{2,10},{4,12},{6,14},{8,0},{10,2},{12,4},{14,6},{1,9},{3,11}... | collective-permute-start | bytes 307208 | tf_op jit(solution)/shard_map/ppermute | solution.py:486
  51.0 8.2 %collective-permute-start.8 = (f32[200,128]{1,0:T(8,128)S(1)}, f32[200,128]{1,0:T(8,128)S(1)}, u32[]{:S(2)}, u32[]{:S(2)}) collective-permute-start(f32[200,128]{1,0:T(8,128)S(1)} %get-tuple-element.36), channel_id=1, source_target_pairs={{0,12},{2,14},{4,8},{6,10},{8,4},{10,6},{12,0},{14,2},{1,13},{3,15... | collective-permute-start | bytes 307208 | tf_op jit(solution)/shard_map/ppermute | solution.py:486
  52.7 6.5 %collective-permute-start.10 = (f32[200,128]{1,0:T(8,128)S(1)}, f32[200,128]{1,0:T(8,128)S(1)}, u32[]{:S(2)}, u32[]{:S(2)}) collective-permute-start(f32[200,128]{1,0:T(8,128)S(1)} %get-tuple-element.40), channel_id=1, source_target_pairs={{0,4},{2,6},{4,0},{6,2},{8,12},{10,14},{12,8},{14,10},{1,5},{3,7},... | collective-permute-start | bytes 307208 | tf_op jit(solution)/shard_map/ppermute | solution.py:486
  53.4 13.3 %collective-permute-start.11 = (f32[200,128]{1,0:T(8,128)S(1)}, f32[200,128]{1,0:T(8,128)S(1)}, u32[]{:S(2)}, u32[]{:S(2)}) collective-permute-start(f32[200,128]{1,0:T(8,128)S(1)} %get-tuple-element.41), channel_id=1, source_target_pairs={{0,8},{2,10},{4,12},{6,14},{8,0},{10,2},{12,4},{14,6},{1,9},{3,11}... | collective-permute-start | bytes 307208 | tf_op jit(solution)/shard_map/ppermute | solution.py:486
  56.9 9.8 %collective-permute-start.12 = (f32[200,128]{1,0:T(8,128)S(1)}, f32[200,128]{1,0:T(8,128)S(1)}, u32[]{:S(2)}, u32[]{:S(2)}) collective-permute-start(f32[200,128]{1,0:T(8,128)S(1)} %get-tuple-element.42), channel_id=1, source_target_pairs={{0,12},{2,14},{4,8},{6,10},{8,4},{10,6},{12,0},{14,2},{1,13},{3,15... | collective-permute-start | bytes 307208 | tf_op jit(solution)/shard_map/ppermute | solution.py:486

commit v6 on v5

--- a/solution.py
+++ b/solution.py
@@ -196,10 +196,13 @@
     def dots(s, buffers, border):
         even_in, odd_in, edge_in = buffers
         wide = DEPTH // SPLIT
-        for part in range(SPLIT):
+
+        def product(part, source, table):
             columns = slice(part * wide, (part + 1) * wide)
-            re = jnp.dot(even_in[...], even_ref[:, columns], preferred_element_type=jnp.float32)
-            im = jnp.dot(odd_in[...], odd_ref[:, columns], preferred_element_type=jnp.float32)
+            return jnp.dot(source[...], table[:, columns], preferred_element_type=jnp.float32)
+
+        def complete(part, re, im):
+            columns = slice(part * wide, (part + 1) * wide)
             block0 = part * (wide // LANES)
             for g in range(SUB // 8):
 
@@ -218,6 +221,13 @@
                     line0 = pl.multiple_of(s * SUB + g * 8, 8)
                     rough_ref[pl.ds(line0 + SUB, 8), columns] = shut(rough, first, last, block0)
                     struct_ref[pl.ds(line0, 8), columns] = struct
+
+        re0 = product(0, even_in, even_ref)
+        im0 = product(0, odd_in, odd_ref)
+        re1 = product(1, even_in, even_ref)
+        complete(0, re0, im0)
+        im1 = product(1, odd_in, odd_ref)
+        complete(1, re1, im1)
 
     bufs = [scratch[0:3], scratch[3:6]]
     first_copy.wait()
@@ -483,8 +493,8 @@
     def merge(i, later):
         outs = merge_call(vol[None], kept[i], arrived[i], later, strips)
         got = [
-            lax.ppermute(p, "vol", [(v, v ^ (2 * d)) for v in range(strips)])
-            for d, p in zip(range(1, shares), outs[1:])
+            lax.ppermute(outs[d], "vol", [(v, v ^ (2 * d)) for v in range(strips)])
+            for d in [*range(2, shares), 1][: shares - 1]
         ]
         parts.append([outs[0]] + got)
         return outs[-1]

time: 68.4 us -> 66.3 us (0.969)
  Pallas kernels: 31.2 us -> 30.3 us
  starting transfers between devices: 18.6 us -> 17.8 us
    pallas_call x3, Pallas kernels: 29.7 us -> 28.7 us  [maps_call(): pl.pallas_call(functools.partial(maps_kernel, norms, edge, strips, step,...]
    ppermute x9, waiting for transfers between devices: 9.57 us -> 8.76 us  [merge(): lax.ppermute(outs[d], 'vol', [(v, v ^ 2 * d) for v in range(strips)])]
where the time goes in v6:
time: 66.3 us; the launch traced here: 65.9 us
  Pallas kernels  30.3 us (46%)
  starting transfers between devices  17.8 us (27%)
  waiting for transfers between devices  10.7 us (16%)
  local copies, waits for them, and re-layouts  5.08 us (8%)
  other arithmetic  1.41 us (2%)
  between operations  0.73 us (1%)
    pallas_call x3, Pallas kernels, maps_call(): pl.pallas_call(functools.partial(maps_kernel, norms, edge, strips, step,...  28.7 us
    ppermute x9, starting transfers between devices, merge(): lax.ppermute(outs[d], 'vol', [(v, v ^ 2 * d) for v in range(strips)])  12.9 us
    ppermute x9, waiting for transfers between devices, merge(): lax.ppermute(outs[d], 'vol', [(v, v ^ 2 * d) for v in range(strips)])  8.76 us
    ppermute x3, starting transfers between devices, on_device(): arrived.append(lax.ppermute(send, 'vol', swap))  4.33 us
    unnamed x12, local copies, waits for them, and re-layouts  4.09 us
    ppermute x3, waiting for transfers between devices, on_device(): arrived.append(lax.ppermute(send, 'vol', swap))  1.93 us
    pallas_call x1, Pallas kernels, final_call(): pl.pallas_call(functools.partial(final_kernel, strip, count, shares), in_...  1.37 us
  transfers between devices with their start and end apart: 13, of which 3 were waited for; matrix products, arithmetic and copies ran while one was open for 0% of the time, Pallas kernels for 29%

profile of v6, /device:TPU:0, one launch (start us, length us, event | category | flops | bytes accessed | tf_op | source)
XLA Modules:
  0.0 65.9 jit_solution(10708695870966986215)
XLA Ops:
  0.6 0.7 convert_bitcast_fusion
  1.3 0.7 %convert_element_type.28 = f32[3,2]{0,1:T(2,128)S(1)} convert(s32[3,2]{0,1:T(2,128)} %param.9) | non-fusion elementwise | flops 6 | bytes 48 | tf_op jit(solution)/shard_map/convert_element_type | solution.py:468
  2.0 0.1 copy.12
  2.1 0.1 convert_element_type.29
  2.2 0.7 %concatenate.7.values.info = f32[14]{0:T(128)S(1)} concatenate(f32[1]{0:T(128)} %bitcast, f32[1]{0:T(128)S(6)} %convert_element_type.27, f32[6]{0:T(128)S(1)} %convert_element_type.29, f32[3]{0:T(128)S(1)} %convert_bitcast_fusion, f32[3]{0:T(128)} %bitcast.16), dimensions={0} | concatenate | bytes 112 | tf_op jit(solution)/shard_map/concatenate | solution.py:464
  2.9 0.0 copy-start
  2.9 0.9 %copy-done = f32[1,4,384,16]{2,3,1,0:T(8,128)S(1)} copy-done((f32[1,4,384,16]{2,3,1,0:T(8,128)S(1)}, f32[1,4,384,16]{2,3,1,0:T(8,128)}, u32[]{:S(2)}) %copy-start) | copy-done | bytes 98328
  3.8 0.0 copy-start.2
  3.8 1.6 %copy-done.2 = bf16[2,1024,512]{2,1,0:T(8,128)(2,1)S(1)} copy-done((bf16[2,1024,512]{2,1,0:T(8,128)(2,1)S(1)}, bf16[2,1024,512]{2,1,0:T(8,128)(2,1)}, u32[]{:S(2)}) %copy-start.2) | copy-done | bytes 2097176
  5.4 9.7 %maps.3 = (f32[520,128]{1,0:T(8,128)S(1)}, f32[520,128]{1,0:T(8,128)S(1)}, f32[8,2176]{1,0:T(8,128)S(1)}) custom-call(f32[14]{0:T(128)S(1)} %concatenate.7.values.info, bf16[4,384,2048]{2,1,0:T(8,128)(2,1)} %bitcast.18, f32[4,16,384]{2,1,0:T(8,128)S(1)} %bitcast.13, bf16[2,1024,512]{2,1,0:T(8,128)(2,1)S(1)} %copy-done.2), custom_call_target="tpu_custom_call" | custom-call | flops 12079595520 | bytes 6291456 | tf_op jit(solution)/shard_map/maps/pallas_call | solution.py:343
  15.1 0.5 collective-permute-start.5
  15.6 2.6 %collective-permute-start = (f32[520,128]{1,0:T(8,128)S(1)}, f32[520,128]{1,0:T(8,128)S(1)}, u32[]{:S(2)}, u32[]{:S(2)}) collective-permute-start(f32[520,128]{1,0:T(8,128)S(1)} %get-tuple-element.24), channel_id=1, source_target_pairs={{0,2},{2,0},{4,6},{6,4},{8,10},{10,8},{12,14},{14,12},{1,3},{3,1},... | collective-permute-start | bytes 798728 | tf_op jit(solution)/shard_map/ppermute | solution.py:528
  18.2 9.4 %maps.4 = (f32[520,128]{1,0:T(8,128)S(1)}, f32[520,128]{1,0:T(8,128)S(1)}) custom-call(f32[14]{0:T(128)S(1)} %concatenate.7.values.info, bf16[4,384,2048]{2,1,0:T(8,128)(2,1)} %bitcast.19, f32[4,16,384]{2,1,0:T(8,128)S(1)} %bitcast.14, bf16[2,1024,512]{2,1,0:T(8,128)(2,1)S(1)} %copy-done.2), custom_call_target="tpu_custom_call" | custom-call | flops 12079595520 | bytes 6291456 | tf_op jit(solution)/shard_map/maps/pallas_call | solution.py:343
  27.6 0.1 collective-permute-start.4
  27.8 0.0 collective-permute-done.5.refs_0_
  27.8 0.0 copy-done.5
  27.8 0.1 fusion.1
  27.8 0.0 copy-done.4
  27.8 0.1 concatenate.8.values
  27.9 0.0 collective-permute-done.recv_ref
  27.9 0.1 merge.3
  28.0 3.1 %collective-permute-start.1 = (f32[200,128]{1,0:T(8,128)S(1)}, f32[200,128]{1,0:T(8,128)S(1)}, u32[]{:S(2)}, u32[]{:S(2)}) collective-permute-start(f32[200,128]{1,0:T(8,128)S(1)} %get-tuple-element.26), channel_id=1, source_target_pairs={{0,8},{2,10},{4,12},{6,14},{8,0},{10,2},{12,4},{14,6},{1,9},{3,11}... | collective-permute-start | bytes 307208 | tf_op jit(solution)/shard_map/ppermute | solution.py:496
  31.1 1.3 %collective-permute-start.2 = (f32[200,128]{1,0:T(8,128)S(1)}, f32[200,128]{1,0:T(8,128)S(1)}, u32[]{:S(2)}, u32[]{:S(2)}) collective-permute-start(f32[200,128]{1,0:T(8,128)S(1)} %get-tuple-element.27), channel_id=1, source_target_pairs={{0,12},{2,14},{4,8},{6,10},{8,4},{10,6},{12,0},{14,2},{1,13},{3,15... | collective-permute-start | bytes 307208 | tf_op jit(solution)/shard_map/ppermute | solution.py:496
  32.5 0.2 collective-permute-start.3
  32.7 0.0 copy-done.1
  32.7 1.6 %copy-done.3 = bf16[2,1024,512]{2,1,0:T(8,128)(2,1)S(1)} copy-done((bf16[2,1024,512]{2,1,0:T(8,128)(2,1)S(1)}, bf16[2,1024,512]{2,1,0:T(8,128)(2,1)}, u32[]{:S(2)}) %copy-start.3) | copy-done | bytes 2097176
  34.3 9.6 %maps.5 = (f32[520,128]{1,0:T(8,128)S(1)}, f32[520,128]{1,0:T(8,128)S(1)}) custom-call(f32[18]{0:T(128)S(1)} %concatenate.8.values, bf16[4,384,2048]{2,1,0:T(8,128)(2,1)} %bitcast.20, f32[4,16,384]{2,1,0:T(8,128)S(1)} %bitcast.15, bf16[2,1024,512]{2,1,0:T(8,128)(2,1)S(1)} %copy-done.3, f32[8,2176]{1,0:T(8,128)S(1)} %collective-permute-done.5.refs_0_, ...), custom_call_target="tpu_custom_call" | custom-call | flops 12079595520 | bytes 6291456 | tf_op jit(solution)/shard_map/maps/pallas_call | solution.py:343
  43.9 0.0 collective-permute-done.4.recv_ref
  43.9 0.0 collective-permute-done.1.outs_1_.refs_1_
  43.9 0.0 collective-permute-done.2.outs_2_.refs_2_
  43.9 0.0 collective-permute-done.3.outs_3_.refs_3_
  43.9 0.1 merge.4
  44.0 1.6 %collective-permute-start.9 = (f32[520,128]{1,0:T(8,128)S(1)}, f32[520,128]{1,0:T(8,128)S(1)}, u32[]{:S(2)}, u32[]{:S(2)}) collective-permute-start(f32[520,128]{1,0:T(8,128)S(1)} %get-tuple-element.38), channel_id=1, source_target_pairs={{0,2},{2,0},{4,6},{6,4},{8,10},{10,8},{12,14},{14,12},{1,3},{3,1},... | collective-permute-start | bytes 798728 | tf_op jit(solution)/shard_map/ppermute | solution.py:528
  45.6 2.8 %collective-permute-start.6 = (f32[200,128]{1,0:T(8,128)S(1)}, f32[200,128]{1,0:T(8,128)S(1)}, u32[]{:S(2)}, u32[]{:S(2)}) collective-permute-start(f32[200,128]{1,0:T(8,128)S(1)} %get-tuple-element.34), channel_id=1, source_target_pairs={{0,8},{2,10},{4,12},{6,14},{8,0},{10,2},{12,4},{14,6},{1,9},{3,11}... | collective-permute-start | bytes 307208 | tf_op jit(solution)/shard_map/ppermute | solution.py:496
  48.4 1.3 %collective-permute-start.7 = (f32[200,128]{1,0:T(8,128)S(1)}, f32[200,128]{1,0:T(8,128)S(1)}, u32[]{:S(2)}, u32[]{:S(2)}) collective-permute-start(f32[200,128]{1,0:T(8,128)S(1)} %get-tuple-element.35), channel_id=1, source_target_pairs={{0,12},{2,14},{4,8},{6,10},{8,4},{10,6},{12,0},{14,2},{1,13},{3,15... | collective-permute-start | bytes 307208 | tf_op jit(solution)/shard_map/ppermute | solution.py:496
  49.7 0.0 collective-permute-start.8
  49.7 1.9 %collective-permute-done.9.recv_ref = f32[520,128]{1,0:T(8,128)S(1)} collective-permute-done((f32[520,128]{1,0:T(8,128)S(1)}, f32[520,128]{1,0:T(8,128)S(1)}, u32[]{:S(2)}, u32[]{:S(2)}) %collective-permute-start.9) | collective-permute-done | bytes 266272 | tf_op jit(solution)/shard_map/ppermute | solution.py:528
  51.7 0.1 merge.5
  51.7 2.6 %collective-permute-start.10 = (f32[200,128]{1,0:T(8,128)S(1)}, f32[200,128]{1,0:T(8,128)S(1)}, u32[]{:S(2)}, u32[]{:S(2)}) collective-permute-start(f32[200,128]{1,0:T(8,128)S(1)} %get-tuple-element.40), channel_id=1, source_target_pairs={{0,8},{2,10},{4,12},{6,14},{8,0},{10,2},{12,4},{14,6},{1,9},{3,11}... | collective-permute-start | bytes 307208 | tf_op jit(solution)/shard_map/ppermute | solution.py:496
  54.3 1.4 %collective-permute-start.11 = (f32[200,128]{1,0:T(8,128)S(1)}, f32[200,128]{1,0:T(8,128)S(1)}, u32[]{:S(2)}, u32[]{:S(2)}) collective-permute-start(f32[200,128]{1,0:T(8,128)S(1)} %get-tuple-element.41), channel_id=1, source_target_pairs={{0,12},{2,14},{4,8},{6,10},{8,4},{10,6},{12,0},{14,2},{1,13},{3,15... | collective-permute-start | bytes 307208 | tf_op jit(solution)/shard_map/ppermute | solution.py:496
  55.7 0.6 collective-permute-done.6.refs_5_
  56.3 0.1 collective-permute-start.12
  56.4 0.0 collective-permute-done.7.refs_6_
  56.4 0.0 collective-permute-done.8.refs_7_
  56.4 8.1 %collective-permute-done.10.refs_9_ = f32[200,128]{1,0:T(8,128)S(1)} collective-permute-done((f32[200,128]{1,0:T(8,128)S(1)}, f32[200,128]{1,0:T(8,128)S(1)}, u32[]{:S(2)}, u32[]{:S(2)}) %collective-permute-start.10) | collective-permute-done | bytes 102432 | tf_op jit(solution)/shard_map/ppermute | solution.py:496
  64.6 0.0 collective-permute-done.11.refs_10_
  64.6 0.0 collective-permute-done.12.refs_11_
  64.6 1.4 %final.1 = (f32[64,384]{1,0:T(8,128)}, f32[64,384]{1,0:T(8,128)}, f32[64,384]{1,0:T(8,128)}) custom-call(f32[14]{0:T(128)S(1)} %concatenate.7.values.info, f32[200,128]{1,0:T(8,128)S(1)} %get-tuple-element.25.refs_1_.refs_0_, f32[200,128]{1,0:T(8,128)S(1)} %collective-permute-done.1.outs_1_.refs_1_, f32[200,128]{1,0:T(8,128)S(1)} %collective-permute-done.2.outs_2_.refs_2_, ...), custom_call_target="tpu_custom_call" | custom-call | tf_op jit(solution)/shard_map/final/pallas_call | solution.py:430
  (4 shorter events, 0.0 us)
Async XLA Ops:
  2.9 0.9 %copy-start = (f32[1,4,384,16]{2,3,1,0:T(8,128)S(1)}, f32[1,4,384,16]{2,3,1,0:T(8,128)}, u32[]{:S(2)}) copy-start(f32[1,4,384,16]{2,3,1,0:T(8,128)} %param.8) | copy-start | bytes 294916
  3.8 1.6 %copy-start.2 = (bf16[2,1024,512]{2,1,0:T(8,128)(2,1)S(1)}, bf16[2,1024,512]{2,1,0:T(8,128)(2,1)}, u32[]{:S(2)}) copy-start(bf16[2,1024,512]{2,1,0:T(8,128)(2,1)} %constant.16.clone.table_in) | copy-start | bytes 6291460
  15.1 12.7 %collective-permute-start.5 = (f32[8,2176]{1,0:T(8,128)S(1)}, f32[8,2176]{1,0:T(8,128)S(1)}, u32[]{:S(2)}, u32[]{:S(2)}) collective-permute-start(f32[8,2176]{1,0:T(8,128)S(1)} %get-tuple-element.31), channel_id=1, source_target_pairs={{0,1},{1,0},{2,3},{3,2},{4,5},{5,4},{6,7},{7,6},{8,9},{9,8},{10,11... | collective-permute-start | bytes 208904 | tf_op jit(solution)/shard_map/ppermute | solution.py:508
  15.6 12.2 %copy-start.5 = (f32[1,2]{1,0:T(1,128)S(1)}, f32[1,2]{1,0:T(1,128)}, u32[]{:S(2)}) copy-start(f32[1,2]{1,0:T(1,128)} %constant.23) | copy-start | bytes 28
  15.6 12.3 %copy-start.4 = (f32[1,3]{1,0:T(1,128)S(1)}, f32[1,3]{1,0:T(1,128)}, u32[]{:S(2)}) copy-start(f32[1,3]{1,0:T(1,128)} %param.11) | copy-start | bytes 40
  15.6 17.1 %copy-start.1 = (f32[1,4,384,16]{2,3,1,0:T(8,128)S(1)}, f32[1,4,384,16]{2,3,1,0:T(8,128)}, u32[]{:S(2)}) copy-start(f32[1,4,384,16]{2,3,1,0:T(8,128)} %param.8) | copy-start | bytes 294916
  15.6 12.3 %collective-permute-start = (f32[520,128]{1,0:T(8,128)S(1)}, f32[520,128]{1,0:T(8,128)S(1)}, u32[]{:S(2)}, u32[]{:S(2)}) collective-permute-start(f32[520,128]{1,0:T(8,128)S(1)} %get-tuple-element.24), channel_id=1, source_target_pairs={{0,2},{2,0},{4,6},{6,4},{8,10},{10,8},{12,14},{14,12},{1,3},{3,1},... | collective-permute-start | bytes 798728 | tf_op jit(solution)/shard_map/ppermute | solution.py:528
  27.6 16.2 %collective-permute-start.4 = (f32[520,128]{1,0:T(8,128)S(1)}, f32[520,128]{1,0:T(8,128)S(1)}, u32[]{:S(2)}, u32[]{:S(2)}) collective-permute-start(f32[520,128]{1,0:T(8,128)S(1)} %get-tuple-element.30), channel_id=1, source_target_pairs={{0,2},{2,0},{4,6},{6,4},{8,10},{10,8},{12,14},{14,12},{1,3},{3,1},... | collective-permute-start | bytes 798728 | tf_op jit(solution)/shard_map/ppermute | solution.py:528
  28.0 15.9 %collective-permute-start.1 = (f32[200,128]{1,0:T(8,128)S(1)}, f32[200,128]{1,0:T(8,128)S(1)}, u32[]{:S(2)}, u32[]{:S(2)}) collective-permute-start(f32[200,128]{1,0:T(8,128)S(1)} %get-tuple-element.26), channel_id=1, source_target_pairs={{0,8},{2,10},{4,12},{6,14},{8,0},{10,2},{12,4},{14,6},{1,9},{3,11}... | collective-permute-start | bytes 307208 | tf_op jit(solution)/shard_map/ppermute | solution.py:496
  31.1 12.8 %collective-permute-start.2 = (f32[200,128]{1,0:T(8,128)S(1)}, f32[200,128]{1,0:T(8,128)S(1)}, u32[]{:S(2)}, u32[]{:S(2)}) collective-permute-start(f32[200,128]{1,0:T(8,128)S(1)} %get-tuple-element.27), channel_id=1, source_target_pairs={{0,12},{2,14},{4,8},{6,10},{8,4},{10,6},{12,0},{14,2},{1,13},{3,15... | collective-permute-start | bytes 307208 | tf_op jit(solution)/shard_map/ppermute | solution.py:496
  32.5 11.5 %collective-permute-start.3 = (f32[200,128]{1,0:T(8,128)S(1)}, f32[200,128]{1,0:T(8,128)S(1)}, u32[]{:S(2)}, u32[]{:S(2)}) collective-permute-start(f32[200,128]{1,0:T(8,128)S(1)} %get-tuple-element.28), channel_id=1, source_target_pairs={{0,4},{2,6},{4,0},{6,2},{8,12},{10,14},{12,8},{14,10},{1,5},{3,7},... | collective-permute-start | bytes 307208 | tf_op jit(solution)/shard_map/ppermute | solution.py:496
  32.7 1.6 %copy-start.3 = (bf16[2,1024,512]{2,1,0:T(8,128)(2,1)S(1)}, bf16[2,1024,512]{2,1,0:T(8,128)(2,1)}, u32[]{:S(2)}) copy-start(bf16[2,1024,512]{2,1,0:T(8,128)(2,1)} %constant.16.clone.table_in) | copy-start | bytes 6291460
  44.0 7.7 %collective-permute-start.9 = (f32[520,128]{1,0:T(8,128)S(1)}, f32[520,128]{1,0:T(8,128)S(1)}, u32[]{:S(2)}, u32[]{:S(2)}) collective-permute-start(f32[520,128]{1,0:T(8,128)S(1)} %get-tuple-element.38), channel_id=1, source_target_pairs={{0,2},{2,0},{4,6},{6,4},{8,10},{10,8},{12,14},{14,12},{1,3},{3,1},... | collective-permute-start | bytes 798728 | tf_op jit(solution)/shard_map/ppermute | solution.py:528
  45.6 10.7 %collective-permute-start.6 = (f32[200,128]{1,0:T(8,128)S(1)}, f32[200,128]{1,0:T(8,128)S(1)}, u32[]{:S(2)}, u32[]{:S(2)}) collective-permute-start(f32[200,128]{1,0:T(8,128)S(1)} %get-tuple-element.34), channel_id=1, source_target_pairs={{0,8},{2,10},{4,12},{6,14},{8,0},{10,2},{12,4},{14,6},{1,9},{3,11}... | collective-permute-start | bytes 307208 | tf_op jit(solution)/shard_map/ppermute | solution.py:496
  48.4 8.0 %collective-permute-start.7 = (f32[200,128]{1,0:T(8,128)S(1)}, f32[200,128]{1,0:T(8,128)S(1)}, u32[]{:S(2)}, u32[]{:S(2)}) collective-permute-start(f32[200,128]{1,0:T(8,128)S(1)} %get-tuple-element.35), channel_id=1, source_target_pairs={{0,12},{2,14},{4,8},{6,10},{8,4},{10,6},{12,0},{14,2},{1,13},{3,15... | collective-permute-start | bytes 307208 | tf_op jit(solution)/shard_map/ppermute | solution.py:496
  49.7 6.7 %collective-permute-start.8 = (f32[200,128]{1,0:T(8,128)S(1)}, f32[200,128]{1,0:T(8,128)S(1)}, u32[]{:S(2)}, u32[]{:S(2)}) collective-permute-start(f32[200,128]{1,0:T(8,128)S(1)} %get-tuple-element.36), channel_id=1, source_target_pairs={{0,4},{2,6},{4,0},{6,2},{8,12},{10,14},{12,8},{14,10},{1,5},{3,7},... | collective-permute-start | bytes 307208 | tf_op jit(solution)/shard_map/ppermute | solution.py:496
  51.7 12.8 %collective-permute-start.10 = (f32[200,128]{1,0:T(8,128)S(1)}, f32[200,128]{1,0:T(8,128)S(1)}, u32[]{:S(2)}, u32[]{:S(2)}) collective-permute-start(f32[200,128]{1,0:T(8,128)S(1)} %get-tuple-element.40), channel_id=1, source_target_pairs={{0,8},{2,10},{4,12},{6,14},{8,0},{10,2},{12,4},{14,6},{1,9},{3,11}... | collective-permute-start | bytes 307208 | tf_op jit(solution)/shard_map/ppermute | solution.py:496
  54.3 10.2 %collective-permute-start.11 = (f32[200,128]{1,0:T(8,128)S(1)}, f32[200,128]{1,0:T(8,128)S(1)}, u32[]{:S(2)}, u32[]{:S(2)}) collective-permute-start(f32[200,128]{1,0:T(8,128)S(1)} %get-tuple-element.41), channel_id=1, source_target_pairs={{0,12},{2,14},{4,8},{6,10},{8,4},{10,6},{12,0},{14,2},{1,13},{3,15... | collective-permute-start | bytes 307208 | tf_op jit(solution)/shard_map/ppermute | solution.py:496
  56.3 8.3 %collective-permute-start.12 = (f32[200,128]{1,0:T(8,128)S(1)}, f32[200,128]{1,0:T(8,128)S(1)}, u32[]{:S(2)}, u32[]{:S(2)}) collective-permute-start(f32[200,128]{1,0:T(8,128)S(1)} %get-tuple-element.42), channel_id=1, source_target_pairs={{0,4},{2,6},{4,0},{6,2},{8,12},{10,14},{12,8},{14,10},{1,5},{3,7},... | collective-permute-start | bytes 307208 | tf_op jit(solution)/shard_map/ppermute | solution.py:496

commit v7 on v6

--- a/solution.py
+++ b/solution.py
@@ -74,11 +74,11 @@
     base_prev = pl.multiple_of(jnp.maximum(base - SUB, 0), SUB)
     base_next = pl.multiple_of(jnp.minimum(base + lines, line_count - SUB), SUB)
     first_copy = pltpu.make_async_copy(
-        x_hbm.at[:, pl.ds(base, SUB), :], x_ref.at[:, :SUB, :], sems.at[0]
+        x_hbm.at[:, pl.ds(base, 2 * SUB), :], x_ref.at[:, : 2 * SUB, :], sems.at[0]
     )
     own = pltpu.make_async_copy(
-        x_hbm.at[:, pl.ds(pl.multiple_of(base + SUB, SUB), lines - SUB), :],
-        x_ref.at[:, SUB:lines, :],
+        x_hbm.at[:, pl.ds(pl.multiple_of(base + 2 * SUB, SUB), lines - 2 * SUB), :],
+        x_ref.at[:, 2 * SUB : lines, :],
         sems.at[5],
     )
     tables = []
@@ -232,7 +232,11 @@
     bufs = [scratch[0:3], scratch[3:6]]
     first_copy.wait()
     fold(0, bufs[0])
-    for copy in [own] + edges + tables:
+    for copy in tables:
+        copy.wait()
+    dots(0, bufs[0], False)
+    fold(1, bufs[1])
+    for copy in [own] + edges:
         copy.wait()
     for r in range(REPEATS):
         for kb in range(blocks):
@@ -271,13 +275,15 @@
 
 
     def pair(i, carry):
-        dots(2 * i, bufs[0], False)
-        fold(2 * i + 1, bufs[1])
         dots(2 * i + 1, bufs[1], False)
         fold(2 * i + 2, bufs[0])
+        dots(2 * i + 2, bufs[0], False)
+        fold(2 * i + 3, bufs[1])
         return carry
 
-    lax.fori_loop(0, parts // 2, pair, 0)
+    lax.fori_loop(0, parts // 2 - 1, pair, 0)
+    dots(parts - 1, bufs[1], False)
+    fold(parts, bufs[0])
     dots(parts, bufs[0], True)
 
     pick = info[2 + 2 * count + tile]

time: 66.3 us -> 65.5 us (0.988)
  Pallas kernels: 30.3 us -> 29.5 us
    pallas_call x3, Pallas kernels: 28.7 us -> 27.9 us  [maps_call(): pl.pallas_call(functools.partial(maps_kernel, norms, edge, strips, step,...]
  transfers between devices with their start and end apart: 13 -> 13, of which waited for: 3 -> 4; matrix products, arithmetic and copies ran while one was open for 0% -> 0% of each run, Pallas kernels for 29% -> 29%
where the time goes in v7:
time: 65.5 us; the launch traced here: 65.2 us
  Pallas kernels  29.5 us (45%)
  starting transfers between devices  17.7 us (27%)
  waiting for transfers between devices  10.8 us (16%)
  local copies, waits for them, and re-layouts  5.08 us (8%)
  other arithmetic  1.41 us (2%)
  between operations  0.75 us (1%)
    pallas_call x3, Pallas kernels, maps_call(): pl.pallas_call(functools.partial(maps_kernel, norms, edge, strips, step,...  27.9 us
    ppermute x9, starting transfers between devices, merge(): lax.ppermute(outs[d], 'vol', [(v, v ^ 2 * d) for v in range(strips)])  12.9 us
    ppermute x9, waiting for transfers between devices, merge(): lax.ppermute(outs[d], 'vol', [(v, v ^ 2 * d) for v in range(strips)])  8.82 us
    ppermute x3, starting transfers between devices, on_device(): arrived.append(lax.ppermute(send, 'vol', swap))  4.3 us
    unnamed x12, local copies, waits for them, and re-layouts  4.09 us
    ppermute x3, waiting for transfers between devices, on_device(): arrived.append(lax.ppermute(send, 'vol', swap))  1.93 us
    pallas_call x1, Pallas kernels, final_call(): pl.pallas_call(functools.partial(final_kernel, strip, count, shares), in_...  1.37 us
  transfers between devices with their start and end apart: 13, of which 4 were waited for; matrix products, arithmetic and copies ran while one was open for 0% of the time, Pallas kernels for 29%

profile of v7, /device:TPU:0, one launch (start us, length us, event | category | flops | bytes accessed | tf_op | source)
XLA Modules:
  0.0 65.2 jit_solution(2400573815973512288)
XLA Ops:
  0.6 0.7 %convert_bitcast_fusion = f32[3]{0:T(128)S(1)} fusion(s32[1,3]{1,0:T(1,128)} %param.10), kind=kLoop, calls=%fused_computation.4 | loop fusion | flops 3 | bytes 24 | tf_op jit(solution)/shard_map/convert_element_type | solution.py:475
  1.3 0.7 %convert_element_type.28 = f32[3,2]{0,1:T(2,128)S(1)} convert(s32[3,2]{0,1:T(2,128)} %param.9) | non-fusion elementwise | flops 6 | bytes 48 | tf_op jit(solution)/shard_map/convert_element_type | solution.py:474
  2.0 0.1 copy.12
  2.1 0.1 convert_element_type.29
  2.2 0.7 %concatenate.7.values.info = f32[14]{0:T(128)S(1)} concatenate(f32[1]{0:T(128)} %bitcast, f32[1]{0:T(128)S(6)} %convert_element_type.27, f32[6]{0:T(128)S(1)} %convert_element_type.29, f32[3]{0:T(128)S(1)} %convert_bitcast_fusion, f32[3]{0:T(128)} %bitcast.16), dimensions={0} | concatenate | bytes 112 | tf_op jit(solution)/shard_map/concatenate | solution.py:470
  2.9 0.0 copy-start
  2.9 0.9 %copy-done = f32[1,4,384,16]{2,3,1,0:T(8,128)S(1)} copy-done((f32[1,4,384,16]{2,3,1,0:T(8,128)S(1)}, f32[1,4,384,16]{2,3,1,0:T(8,128)}, u32[]{:S(2)}) %copy-start) | copy-done | bytes 98328
  3.8 0.0 copy-start.2
  3.8 1.6 %copy-done.2 = bf16[2,1024,512]{2,1,0:T(8,128)(2,1)S(1)} copy-done((bf16[2,1024,512]{2,1,0:T(8,128)(2,1)S(1)}, bf16[2,1024,512]{2,1,0:T(8,128)(2,1)}, u32[]{:S(2)}) %copy-start.2) | copy-done | bytes 2097176
  5.4 9.4 %maps.3 = (f32[520,128]{1,0:T(8,128)S(1)}, f32[520,128]{1,0:T(8,128)S(1)}, f32[8,2176]{1,0:T(8,128)S(1)}) custom-call(f32[14]{0:T(128)S(1)} %concatenate.7.values.info, bf16[4,384,2048]{2,1,0:T(8,128)(2,1)} %bitcast.18, f32[4,16,384]{2,1,0:T(8,128)S(1)} %bitcast.13, bf16[2,1024,512]{2,1,0:T(8,128)(2,1)S(1)} %copy-done.2), custom_call_target="tpu_custom_call" | custom-call | flops 12079595520 | bytes 6291456 | tf_op jit(solution)/shard_map/maps/pallas_call | solution.py:349
  14.7 0.5 collective-permute-start.5
  15.3 2.6 %collective-permute-start = (f32[520,128]{1,0:T(8,128)S(1)}, f32[520,128]{1,0:T(8,128)S(1)}, u32[]{:S(2)}, u32[]{:S(2)}) collective-permute-start(f32[520,128]{1,0:T(8,128)S(1)} %get-tuple-element.24), channel_id=1, source_target_pairs={{0,2},{2,0},{4,6},{6,4},{8,10},{10,8},{12,14},{14,12},{1,3},{3,1},... | collective-permute-start | bytes 798728 | tf_op jit(solution)/shard_map/ppermute | solution.py:534
  17.9 9.2 %maps.4 = (f32[520,128]{1,0:T(8,128)S(1)}, f32[520,128]{1,0:T(8,128)S(1)}) custom-call(f32[14]{0:T(128)S(1)} %concatenate.7.values.info, bf16[4,384,2048]{2,1,0:T(8,128)(2,1)} %bitcast.19, f32[4,16,384]{2,1,0:T(8,128)S(1)} %bitcast.14, bf16[2,1024,512]{2,1,0:T(8,128)(2,1)S(1)} %copy-done.2), custom_call_target="tpu_custom_call" | custom-call | flops 12079595520 | bytes 6291456 | tf_op jit(solution)/shard_map/maps/pallas_call | solution.py:349
  27.1 0.1 collective-permute-start.4
  27.2 0.0 collective-permute-done.5.refs_0_
  27.2 0.0 copy-done.5
  27.2 0.1 fusion.1
  27.3 0.0 copy-done.4
  27.3 0.1 concatenate.8.values
  27.4 0.0 collective-permute-done.recv_ref
  27.4 0.1 merge.3
  27.4 3.1 %collective-permute-start.1 = (f32[200,128]{1,0:T(8,128)S(1)}, f32[200,128]{1,0:T(8,128)S(1)}, u32[]{:S(2)}, u32[]{:S(2)}) collective-permute-start(f32[200,128]{1,0:T(8,128)S(1)} %get-tuple-element.26), channel_id=1, source_target_pairs={{0,8},{2,10},{4,12},{6,14},{8,0},{10,2},{12,4},{14,6},{1,9},{3,11}... | collective-permute-start | bytes 307208 | tf_op jit(solution)/shard_map/ppermute | solution.py:502
  30.6 1.3 %collective-permute-start.2 = (f32[200,128]{1,0:T(8,128)S(1)}, f32[200,128]{1,0:T(8,128)S(1)}, u32[]{:S(2)}, u32[]{:S(2)}) collective-permute-start(f32[200,128]{1,0:T(8,128)S(1)} %get-tuple-element.27), channel_id=1, source_target_pairs={{0,12},{2,14},{4,8},{6,10},{8,4},{10,6},{12,0},{14,2},{1,13},{3,15... | collective-permute-start | bytes 307208 | tf_op jit(solution)/shard_map/ppermute | solution.py:502
  31.9 0.2 collective-permute-start.3
  32.1 0.0 copy-done.1
  32.1 1.6 %copy-done.3 = bf16[2,1024,512]{2,1,0:T(8,128)(2,1)S(1)} copy-done((bf16[2,1024,512]{2,1,0:T(8,128)(2,1)S(1)}, bf16[2,1024,512]{2,1,0:T(8,128)(2,1)}, u32[]{:S(2)}) %copy-start.3) | copy-done | bytes 2097176
  33.7 9.4 %maps.5 = (f32[520,128]{1,0:T(8,128)S(1)}, f32[520,128]{1,0:T(8,128)S(1)}) custom-call(f32[18]{0:T(128)S(1)} %concatenate.8.values, bf16[4,384,2048]{2,1,0:T(8,128)(2,1)} %bitcast.20, f32[4,16,384]{2,1,0:T(8,128)S(1)} %bitcast.15, bf16[2,1024,512]{2,1,0:T(8,128)(2,1)S(1)} %copy-done.3, f32[8,2176]{1,0:T(8,128)S(1)} %collective-permute-done.5.refs_0_, ...), custom_call_target="tpu_custom_call" | custom-call | flops 12079595520 | bytes 6291456 | tf_op jit(solution)/shard_map/maps/pallas_call | solution.py:349
  43.1 0.0 collective-permute-done.4.recv_ref
  43.1 0.0 collective-permute-done.1.outs_1_.refs_1_
  43.2 0.0 collective-permute-done.2.outs_2_.refs_2_
  43.2 0.0 collective-permute-done.3.outs_3_.refs_3_
  43.2 0.1 merge.4
  43.3 1.6 %collective-permute-start.9 = (f32[520,128]{1,0:T(8,128)S(1)}, f32[520,128]{1,0:T(8,128)S(1)}, u32[]{:S(2)}, u32[]{:S(2)}) collective-permute-start(f32[520,128]{1,0:T(8,128)S(1)} %get-tuple-element.38), channel_id=1, source_target_pairs={{0,2},{2,0},{4,6},{6,4},{8,10},{10,8},{12,14},{14,12},{1,3},{3,1},... | collective-permute-start | bytes 798728 | tf_op jit(solution)/shard_map/ppermute | solution.py:534
  44.8 2.8 %collective-permute-start.6 = (f32[200,128]{1,0:T(8,128)S(1)}, f32[200,128]{1,0:T(8,128)S(1)}, u32[]{:S(2)}, u32[]{:S(2)}) collective-permute-start(f32[200,128]{1,0:T(8,128)S(1)} %get-tuple-element.34), channel_id=1, source_target_pairs={{0,8},{2,10},{4,12},{6,14},{8,0},{10,2},{12,4},{14,6},{1,9},{3,11}... | collective-permute-start | bytes 307208 | tf_op jit(solution)/shard_map/ppermute | solution.py:502
  47.6 1.4 %collective-permute-start.7 = (f32[200,128]{1,0:T(8,128)S(1)}, f32[200,128]{1,0:T(8,128)S(1)}, u32[]{:S(2)}, u32[]{:S(2)}) collective-permute-start(f32[200,128]{1,0:T(8,128)S(1)} %get-tuple-element.35), channel_id=1, source_target_pairs={{0,12},{2,14},{4,8},{6,10},{8,4},{10,6},{12,0},{14,2},{1,13},{3,15... | collective-permute-start | bytes 307208 | tf_op jit(solution)/shard_map/ppermute | solution.py:502
  49.0 0.0 collective-permute-start.8
  49.0 1.9 %collective-permute-done.9.recv_ref = f32[520,128]{1,0:T(8,128)S(1)} collective-permute-done((f32[520,128]{1,0:T(8,128)S(1)}, f32[520,128]{1,0:T(8,128)S(1)}, u32[]{:S(2)}, u32[]{:S(2)}) %collective-permute-start.9) | collective-permute-done | bytes 266272 | tf_op jit(solution)/shard_map/ppermute | solution.py:534
  50.9 0.1 merge.5
  51.0 2.6 %collective-permute-start.10 = (f32[200,128]{1,0:T(8,128)S(1)}, f32[200,128]{1,0:T(8,128)S(1)}, u32[]{:S(2)}, u32[]{:S(2)}) collective-permute-start(f32[200,128]{1,0:T(8,128)S(1)} %get-tuple-element.40), channel_id=1, source_target_pairs={{0,8},{2,10},{4,12},{6,14},{8,0},{10,2},{12,4},{14,6},{1,9},{3,11}... | collective-permute-start | bytes 307208 | tf_op jit(solution)/shard_map/ppermute | solution.py:502
  53.6 1.4 %collective-permute-start.11 = (f32[200,128]{1,0:T(8,128)S(1)}, f32[200,128]{1,0:T(8,128)S(1)}, u32[]{:S(2)}, u32[]{:S(2)}) collective-permute-start(f32[200,128]{1,0:T(8,128)S(1)} %get-tuple-element.41), channel_id=1, source_target_pairs={{0,12},{2,14},{4,8},{6,10},{8,4},{10,6},{12,0},{14,2},{1,13},{3,15... | collective-permute-start | bytes 307208 | tf_op jit(solution)/shard_map/ppermute | solution.py:502
  55.0 0.6 collective-permute-done.6.refs_5_
  55.5 0.0 collective-permute-start.12
  55.6 0.0 collective-permute-done.7.refs_6_
  55.6 0.1 collective-permute-done.8.refs_7_
  55.6 8.2 %collective-permute-done.10.refs_9_ = f32[200,128]{1,0:T(8,128)S(1)} collective-permute-done((f32[200,128]{1,0:T(8,128)S(1)}, f32[200,128]{1,0:T(8,128)S(1)}, u32[]{:S(2)}, u32[]{:S(2)}) %collective-permute-start.10) | collective-permute-done | bytes 102432 | tf_op jit(solution)/shard_map/ppermute | solution.py:502
  63.8 0.0 collective-permute-done.11.refs_10_
  63.8 0.0 collective-permute-done.12.refs_11_
  63.8 1.4 %final.1 = (f32[64,384]{1,0:T(8,128)}, f32[64,384]{1,0:T(8,128)}, f32[64,384]{1,0:T(8,128)}) custom-call(f32[14]{0:T(128)S(1)} %concatenate.7.values.info, f32[200,128]{1,0:T(8,128)S(1)} %get-tuple-element.25.refs_1_.refs_0_, f32[200,128]{1,0:T(8,128)S(1)} %collective-permute-done.1.outs_1_.refs_1_, f32[200,128]{1,0:T(8,128)S(1)} %collective-permute-done.2.outs_2_.refs_2_, ...), custom_call_target="tpu_custom_call" | custom-call | tf_op jit(solution)/shard_map/final/pallas_call | solution.py:436
  (4 shorter events, 0.0 us)
Async XLA Ops:
  2.9 0.9 %copy-start = (f32[1,4,384,16]{2,3,1,0:T(8,128)S(1)}, f32[1,4,384,16]{2,3,1,0:T(8,128)}, u32[]{:S(2)}) copy-start(f32[1,4,384,16]{2,3,1,0:T(8,128)} %param.8) | copy-start | bytes 294916
  3.8 1.6 %copy-start.2 = (bf16[2,1024,512]{2,1,0:T(8,128)(2,1)S(1)}, bf16[2,1024,512]{2,1,0:T(8,128)(2,1)}, u32[]{:S(2)}) copy-start(bf16[2,1024,512]{2,1,0:T(8,128)(2,1)} %constant.16.clone.table_in) | copy-start | bytes 6291460
  14.7 12.4 %collective-permute-start.5 = (f32[8,2176]{1,0:T(8,128)S(1)}, f32[8,2176]{1,0:T(8,128)S(1)}, u32[]{:S(2)}, u32[]{:S(2)}) collective-permute-start(f32[8,2176]{1,0:T(8,128)S(1)} %get-tuple-element.31), channel_id=1, source_target_pairs={{0,1},{1,0},{2,3},{3,2},{4,5},{5,4},{6,7},{7,6},{8,9},{9,8},{10,11... | collective-permute-start | bytes 208904 | tf_op jit(solution)/shard_map/ppermute | solution.py:514
  15.3 11.9 %copy-start.5 = (f32[1,2]{1,0:T(1,128)S(1)}, f32[1,2]{1,0:T(1,128)}, u32[]{:S(2)}) copy-start(f32[1,2]{1,0:T(1,128)} %constant.23) | copy-start | bytes 28
  15.3 12.0 %copy-start.4 = (f32[1,3]{1,0:T(1,128)S(1)}, f32[1,3]{1,0:T(1,128)}, u32[]{:S(2)}) copy-start(f32[1,3]{1,0:T(1,128)} %param.11) | copy-start | bytes 40
  15.3 16.9 %copy-start.1 = (f32[1,4,384,16]{2,3,1,0:T(8,128)S(1)}, f32[1,4,384,16]{2,3,1,0:T(8,128)}, u32[]{:S(2)}) copy-start(f32[1,4,384,16]{2,3,1,0:T(8,128)} %param.8) | copy-start | bytes 294916
  15.3 12.1 %collective-permute-start = (f32[520,128]{1,0:T(8,128)S(1)}, f32[520,128]{1,0:T(8,128)S(1)}, u32[]{:S(2)}, u32[]{:S(2)}) collective-permute-start(f32[520,128]{1,0:T(8,128)S(1)} %get-tuple-element.24), channel_id=1, source_target_pairs={{0,2},{2,0},{4,6},{6,4},{8,10},{10,8},{12,14},{14,12},{1,3},{3,1},... | collective-permute-start | bytes 798728 | tf_op jit(solution)/shard_map/ppermute | solution.py:534
  27.1 16.0 %collective-permute-start.4 = (f32[520,128]{1,0:T(8,128)S(1)}, f32[520,128]{1,0:T(8,128)S(1)}, u32[]{:S(2)}, u32[]{:S(2)}) collective-permute-start(f32[520,128]{1,0:T(8,128)S(1)} %get-tuple-element.30), channel_id=1, source_target_pairs={{0,2},{2,0},{4,6},{6,4},{8,10},{10,8},{12,14},{14,12},{1,3},{3,1},... | collective-permute-start | bytes 798728 | tf_op jit(solution)/shard_map/ppermute | solution.py:534
  27.4 15.7 %collective-permute-start.1 = (f32[200,128]{1,0:T(8,128)S(1)}, f32[200,128]{1,0:T(8,128)S(1)}, u32[]{:S(2)}, u32[]{:S(2)}) collective-permute-start(f32[200,128]{1,0:T(8,128)S(1)} %get-tuple-element.26), channel_id=1, source_target_pairs={{0,8},{2,10},{4,12},{6,14},{8,0},{10,2},{12,4},{14,6},{1,9},{3,11}... | collective-permute-start | bytes 307208 | tf_op jit(solution)/shard_map/ppermute | solution.py:502
  30.6 12.6 %collective-permute-start.2 = (f32[200,128]{1,0:T(8,128)S(1)}, f32[200,128]{1,0:T(8,128)S(1)}, u32[]{:S(2)}, u32[]{:S(2)}) collective-permute-start(f32[200,128]{1,0:T(8,128)S(1)} %get-tuple-element.27), channel_id=1, source_target_pairs={{0,12},{2,14},{4,8},{6,10},{8,4},{10,6},{12,0},{14,2},{1,13},{3,15... | collective-permute-start | bytes 307208 | tf_op jit(solution)/shard_map/ppermute | solution.py:502
  31.9 11.3 %collective-permute-start.3 = (f32[200,128]{1,0:T(8,128)S(1)}, f32[200,128]{1,0:T(8,128)S(1)}, u32[]{:S(2)}, u32[]{:S(2)}) collective-permute-start(f32[200,128]{1,0:T(8,128)S(1)} %get-tuple-element.28), channel_id=1, source_target_pairs={{0,4},{2,6},{4,0},{6,2},{8,12},{10,14},{12,8},{14,10},{1,5},{3,7},... | collective-permute-start | bytes 307208 | tf_op jit(solution)/shard_map/ppermute | solution.py:502
  32.1 1.6 %copy-start.3 = (bf16[2,1024,512]{2,1,0:T(8,128)(2,1)S(1)}, bf16[2,1024,512]{2,1,0:T(8,128)(2,1)}, u32[]{:S(2)}) copy-start(bf16[2,1024,512]{2,1,0:T(8,128)(2,1)} %constant.16.clone.table_in) | copy-start | bytes 6291460
  43.3 7.7 %collective-permute-start.9 = (f32[520,128]{1,0:T(8,128)S(1)}, f32[520,128]{1,0:T(8,128)S(1)}, u32[]{:S(2)}, u32[]{:S(2)}) collective-permute-start(f32[520,128]{1,0:T(8,128)S(1)} %get-tuple-element.38), channel_id=1, source_target_pairs={{0,2},{2,0},{4,6},{6,4},{8,10},{10,8},{12,14},{14,12},{1,3},{3,1},... | collective-permute-start | bytes 798728 | tf_op jit(solution)/shard_map/ppermute | solution.py:534
  44.8 10.7 %collective-permute-start.6 = (f32[200,128]{1,0:T(8,128)S(1)}, f32[200,128]{1,0:T(8,128)S(1)}, u32[]{:S(2)}, u32[]{:S(2)}) collective-permute-start(f32[200,128]{1,0:T(8,128)S(1)} %get-tuple-element.34), channel_id=1, source_target_pairs={{0,8},{2,10},{4,12},{6,14},{8,0},{10,2},{12,4},{14,6},{1,9},{3,11}... | collective-permute-start | bytes 307208 | tf_op jit(solution)/shard_map/ppermute | solution.py:502
  47.6 7.9 %collective-permute-start.7 = (f32[200,128]{1,0:T(8,128)S(1)}, f32[200,128]{1,0:T(8,128)S(1)}, u32[]{:S(2)}, u32[]{:S(2)}) collective-permute-start(f32[200,128]{1,0:T(8,128)S(1)} %get-tuple-element.35), channel_id=1, source_target_pairs={{0,12},{2,14},{4,8},{6,10},{8,4},{10,6},{12,0},{14,2},{1,13},{3,15... | collective-permute-start | bytes 307208 | tf_op jit(solution)/shard_map/ppermute | solution.py:502
  49.0 6.6 %collective-permute-start.8 = (f32[200,128]{1,0:T(8,128)S(1)}, f32[200,128]{1,0:T(8,128)S(1)}, u32[]{:S(2)}, u32[]{:S(2)}) collective-permute-start(f32[200,128]{1,0:T(8,128)S(1)} %get-tuple-element.36), channel_id=1, source_target_pairs={{0,4},{2,6},{4,0},{6,2},{8,12},{10,14},{12,8},{14,10},{1,5},{3,7},... | collective-permute-start | bytes 307208 | tf_op jit(solution)/shard_map/ppermute | solution.py:502
  51.0 12.8 %collective-permute-start.10 = (f32[200,128]{1,0:T(8,128)S(1)}, f32[200,128]{1,0:T(8,128)S(1)}, u32[]{:S(2)}, u32[]{:S(2)}) collective-permute-start(f32[200,128]{1,0:T(8,128)S(1)} %get-tuple-element.40), channel_id=1, source_target_pairs={{0,8},{2,10},{4,12},{6,14},{8,0},{10,2},{12,4},{14,6},{1,9},{3,11}... | collective-permute-start | bytes 307208 | tf_op jit(solution)/shard_map/ppermute | solution.py:502
  53.6 10.2 %collective-permute-start.11 = (f32[200,128]{1,0:T(8,128)S(1)}, f32[200,128]{1,0:T(8,128)S(1)}, u32[]{:S(2)}, u32[]{:S(2)}) collective-permute-start(f32[200,128]{1,0:T(8,128)S(1)} %get-tuple-element.41), channel_id=1, source_target_pairs={{0,12},{2,14},{4,8},{6,10},{8,4},{10,6},{12,0},{14,2},{1,13},{3,15... | collective-permute-start | bytes 307208 | tf_op jit(solution)/shard_map/ppermute | solution.py:502
  55.5 8.3 %collective-permute-start.12 = (f32[200,128]{1,0:T(8,128)S(1)}, f32[200,128]{1,0:T(8,128)S(1)}, u32[]{:S(2)}, u32[]{:S(2)}) collective-permute-start(f32[200,128]{1,0:T(8,128)S(1)} %get-tuple-element.42), channel_id=1, source_target_pairs={{0,4},{2,6},{4,0},{6,2},{8,12},{10,14},{12,8},{14,10},{1,5},{3,7},... | collective-permute-start | bytes 307208 | tf_op jit(solution)/shard_map/ppermute | solution.py:502

commit v8 on v7

--- a/solution.py
+++ b/solution.py
@@ -236,8 +236,19 @@
         copy.wait()
     dots(0, bufs[0], False)
     fold(1, bufs[1])
-    for copy in [own] + edges:
+    own.wait()
+
+    def pair(i, carry):
+        dots(2 * i + 1, bufs[1], False)
+        fold(2 * i + 2, bufs[0])
+        dots(2 * i + 2, bufs[0], False)
+        fold(2 * i + 3, bufs[1])
+        return carry
+
+    lax.fori_loop(0, parts // 2 - 1, pair, 0)
+    for copy in edges:
         copy.wait()
+    dots(parts - 1, bufs[1], False)
     for r in range(REPEATS):
         for kb in range(blocks):
             columns = slice(kb * LANES, (kb + 1) * LANES)
@@ -272,17 +283,6 @@
                 ],
                 axis=1,
             )
-
-
-    def pair(i, carry):
-        dots(2 * i + 1, bufs[1], False)
-        fold(2 * i + 2, bufs[0])
-        dots(2 * i + 2, bufs[0], False)
-        fold(2 * i + 3, bufs[1])
-        return carry
-
-    lax.fori_loop(0, parts // 2 - 1, pair, 0)
-    dots(parts - 1, bufs[1], False)
     fold(parts, bufs[0])
     dots(parts, bufs[0], True)
 

time: 65.5 us -> 65.6 us (level)
  transfers between devices with their start and end apart: 13 -> 13, of which waited for: 4 -> 3; matrix products, arithmetic and copies ran while one was open for 0% -> 0% of each run, Pallas kernels for 29% -> 29%
where the time goes in v8:
time: 65.6 us; the launch traced here: 65.3 us
  Pallas kernels  29.6 us (45%)
  starting transfers between devices  17.7 us (27%)
  waiting for transfers between devices  10.7 us (16%)
  local copies, waits for them, and re-layouts  5.08 us (8%)
  other arithmetic  1.41 us (2%)
  between operations  0.75 us (1%)
    pallas_call x3, Pallas kernels, maps_call(): pl.pallas_call(functools.partial(maps_kernel, norms, edge, strips, step,...  28 us
    ppermute x9, starting transfers between devices, merge(): lax.ppermute(outs[d], 'vol', [(v, v ^ 2 * d) for v in range(strips)])  12.9 us
    ppermute x9, waiting for transfers between devices, merge(): lax.ppermute(outs[d], 'vol', [(v, v ^ 2 * d) for v in range(strips)])  8.79 us
    ppermute x3, starting transfers between devices, on_device(): arrived.append(lax.ppermute(send, 'vol', swap))  4.27 us
    unnamed x12, local copies, waits for them, and re-layouts  4.09 us
    ppermute x3, waiting for transfers between devices, on_device(): arrived.append(lax.ppermute(send, 'vol', swap))  1.94 us
    pallas_call x1, Pallas kernels, final_call(): pl.pallas_call(functools.partial(final_kernel, strip, count, shares), in_...  1.37 us
  transfers between devices with their start and end apart: 13, of which 3 were waited for; matrix products, arithmetic and copies ran while one was open for 0% of the time, Pallas kernels for 29%

profile of v8, /device:TPU:0, one launch (start us, length us, event | category | flops | bytes accessed | tf_op | source)
XLA Modules:
  0.0 65.3 jit_solution(14803190863904584011)
XLA Ops:
  0.6 0.7 %convert_bitcast_fusion = f32[3]{0:T(128)S(1)} fusion(s32[1,3]{1,0:T(1,128)} %param.10), kind=kLoop, calls=%fused_computation.4 | loop fusion | flops 3 | bytes 24 | tf_op jit(solution)/shard_map/convert_element_type | solution.py:475
  1.3 0.7 %convert_element_type.28 = f32[3,2]{0,1:T(2,128)S(1)} convert(s32[3,2]{0,1:T(2,128)} %param.9) | non-fusion elementwise | flops 6 | bytes 48 | tf_op jit(solution)/shard_map/convert_element_type | solution.py:474
  2.0 0.1 copy.12
  2.1 0.1 convert_element_type.29
  2.2 0.7 %concatenate.7.values.info = f32[14]{0:T(128)S(1)} concatenate(f32[1]{0:T(128)} %bitcast, f32[1]{0:T(128)S(6)} %convert_element_type.27, f32[6]{0:T(128)S(1)} %convert_element_type.29, f32[3]{0:T(128)S(1)} %convert_bitcast_fusion, f32[3]{0:T(128)} %bitcast.16), dimensions={0} | concatenate | bytes 112 | tf_op jit(solution)/shard_map/concatenate | solution.py:470
  2.9 0.0 copy-start
  2.9 0.9 %copy-done = f32[1,4,384,16]{2,3,1,0:T(8,128)S(1)} copy-done((f32[1,4,384,16]{2,3,1,0:T(8,128)S(1)}, f32[1,4,384,16]{2,3,1,0:T(8,128)}, u32[]{:S(2)}) %copy-start) | copy-done | bytes 98328
  3.8 0.0 copy-start.2
  3.8 1.6 %copy-done.2 = bf16[2,1024,512]{2,1,0:T(8,128)(2,1)S(1)} copy-done((bf16[2,1024,512]{2,1,0:T(8,128)(2,1)S(1)}, bf16[2,1024,512]{2,1,0:T(8,128)(2,1)}, u32[]{:S(2)}) %copy-start.2) | copy-done | bytes 2097176
  5.4 9.3 %maps.3 = (f32[520,128]{1,0:T(8,128)S(1)}, f32[520,128]{1,0:T(8,128)S(1)}, f32[8,2176]{1,0:T(8,128)S(1)}) custom-call(f32[14]{0:T(128)S(1)} %concatenate.7.values.info, bf16[4,384,2048]{2,1,0:T(8,128)(2,1)} %bitcast.18, f32[4,16,384]{2,1,0:T(8,128)S(1)} %bitcast.13, bf16[2,1024,512]{2,1,0:T(8,128)(2,1)S(1)} %copy-done.2), custom_call_target="tpu_custom_call" | custom-call | flops 12079595520 | bytes 6291456 | tf_op jit(solution)/shard_map/maps/pallas_call | solution.py:349
  14.7 0.5 collective-permute-start.5
  15.2 2.6 %collective-permute-start = (f32[520,128]{1,0:T(8,128)S(1)}, f32[520,128]{1,0:T(8,128)S(1)}, u32[]{:S(2)}, u32[]{:S(2)}) collective-permute-start(f32[520,128]{1,0:T(8,128)S(1)} %get-tuple-element.24), channel_id=1, source_target_pairs={{0,2},{2,0},{4,6},{6,4},{8,10},{10,8},{12,14},{14,12},{1,3},{3,1},... | collective-permute-start | bytes 798728 | tf_op jit(solution)/shard_map/ppermute | solution.py:534
  17.8 9.2 %maps.4 = (f32[520,128]{1,0:T(8,128)S(1)}, f32[520,128]{1,0:T(8,128)S(1)}) custom-call(f32[14]{0:T(128)S(1)} %concatenate.7.values.info, bf16[4,384,2048]{2,1,0:T(8,128)(2,1)} %bitcast.19, f32[4,16,384]{2,1,0:T(8,128)S(1)} %bitcast.14, bf16[2,1024,512]{2,1,0:T(8,128)(2,1)S(1)} %copy-done.2), custom_call_target="tpu_custom_call" | custom-call | flops 12079595520 | bytes 6291456 | tf_op jit(solution)/shard_map/maps/pallas_call | solution.py:349
  27.0 0.1 collective-permute-start.4
  27.1 0.0 collective-permute-done.5.refs_0_
  27.1 0.0 copy-done.5
  27.1 0.1 fusion.1
  27.2 0.0 copy-done.4
  27.2 0.1 concatenate.8.values
  27.3 0.0 collective-permute-done.recv_ref
  27.3 0.1 merge.3
  27.4 3.1 %collective-permute-start.1 = (f32[200,128]{1,0:T(8,128)S(1)}, f32[200,128]{1,0:T(8,128)S(1)}, u32[]{:S(2)}, u32[]{:S(2)}) collective-permute-start(f32[200,128]{1,0:T(8,128)S(1)} %get-tuple-element.26), channel_id=1, source_target_pairs={{0,8},{2,10},{4,12},{6,14},{8,0},{10,2},{12,4},{14,6},{1,9},{3,11}... | collective-permute-start | bytes 307208 | tf_op jit(solution)/shard_map/ppermute | solution.py:502
  30.5 1.4 %collective-permute-start.2 = (f32[200,128]{1,0:T(8,128)S(1)}, f32[200,128]{1,0:T(8,128)S(1)}, u32[]{:S(2)}, u32[]{:S(2)}) collective-permute-start(f32[200,128]{1,0:T(8,128)S(1)} %get-tuple-element.27), channel_id=1, source_target_pairs={{0,12},{2,14},{4,8},{6,10},{8,4},{10,6},{12,0},{14,2},{1,13},{3,15... | collective-permute-start | bytes 307208 | tf_op jit(solution)/shard_map/ppermute | solution.py:502
  31.8 0.2 collective-permute-start.3
  32.1 0.0 copy-done.1
  32.1 1.6 %copy-done.3 = bf16[2,1024,512]{2,1,0:T(8,128)(2,1)S(1)} copy-done((bf16[2,1024,512]{2,1,0:T(8,128)(2,1)S(1)}, bf16[2,1024,512]{2,1,0:T(8,128)(2,1)}, u32[]{:S(2)}) %copy-start.3) | copy-done | bytes 2097176
  33.7 9.6 %maps.5 = (f32[520,128]{1,0:T(8,128)S(1)}, f32[520,128]{1,0:T(8,128)S(1)}) custom-call(f32[18]{0:T(128)S(1)} %concatenate.8.values, bf16[4,384,2048]{2,1,0:T(8,128)(2,1)} %bitcast.20, f32[4,16,384]{2,1,0:T(8,128)S(1)} %bitcast.15, bf16[2,1024,512]{2,1,0:T(8,128)(2,1)S(1)} %copy-done.3, f32[8,2176]{1,0:T(8,128)S(1)} %collective-permute-done.5.refs_0_, ...), custom_call_target="tpu_custom_call" | custom-call | flops 12079595520 | bytes 6291456 | tf_op jit(solution)/shard_map/maps/pallas_call | solution.py:349
  43.2 0.0 collective-permute-done.4.recv_ref
  43.2 0.0 collective-permute-done.1.outs_1_.refs_1_
  43.2 0.0 collective-permute-done.2.outs_2_.refs_2_
  43.3 0.0 collective-permute-done.3.outs_3_.refs_3_
  43.3 0.1 merge.4
  43.3 1.6 %collective-permute-start.9 = (f32[520,128]{1,0:T(8,128)S(1)}, f32[520,128]{1,0:T(8,128)S(1)}, u32[]{:S(2)}, u32[]{:S(2)}) collective-permute-start(f32[520,128]{1,0:T(8,128)S(1)} %get-tuple-element.38), channel_id=1, source_target_pairs={{0,2},{2,0},{4,6},{6,4},{8,10},{10,8},{12,14},{14,12},{1,3},{3,1},... | collective-permute-start | bytes 798728 | tf_op jit(solution)/shard_map/ppermute | solution.py:534
  44.9 2.8 %collective-permute-start.6 = (f32[200,128]{1,0:T(8,128)S(1)}, f32[200,128]{1,0:T(8,128)S(1)}, u32[]{:S(2)}, u32[]{:S(2)}) collective-permute-start(f32[200,128]{1,0:T(8,128)S(1)} %get-tuple-element.34), channel_id=1, source_target_pairs={{0,8},{2,10},{4,12},{6,14},{8,0},{10,2},{12,4},{14,6},{1,9},{3,11}... | collective-permute-start | bytes 307208 | tf_op jit(solution)/shard_map/ppermute | solution.py:502
  47.7 1.3 %collective-permute-start.7 = (f32[200,128]{1,0:T(8,128)S(1)}, f32[200,128]{1,0:T(8,128)S(1)}, u32[]{:S(2)}, u32[]{:S(2)}) collective-permute-start(f32[200,128]{1,0:T(8,128)S(1)} %get-tuple-element.35), channel_id=1, source_target_pairs={{0,12},{2,14},{4,8},{6,10},{8,4},{10,6},{12,0},{14,2},{1,13},{3,15... | collective-permute-start | bytes 307208 | tf_op jit(solution)/shard_map/ppermute | solution.py:502
  49.1 0.0 collective-permute-start.8
  49.1 1.9 %collective-permute-done.9.recv_ref = f32[520,128]{1,0:T(8,128)S(1)} collective-permute-done((f32[520,128]{1,0:T(8,128)S(1)}, f32[520,128]{1,0:T(8,128)S(1)}, u32[]{:S(2)}, u32[]{:S(2)}) %collective-permute-start.9) | collective-permute-done | bytes 266272 | tf_op jit(solution)/shard_map/ppermute | solution.py:534
  51.0 0.1 merge.5
  51.1 2.6 %collective-permute-start.10 = (f32[200,128]{1,0:T(8,128)S(1)}, f32[200,128]{1,0:T(8,128)S(1)}, u32[]{:S(2)}, u32[]{:S(2)}) collective-permute-start(f32[200,128]{1,0:T(8,128)S(1)} %get-tuple-element.40), channel_id=1, source_target_pairs={{0,8},{2,10},{4,12},{6,14},{8,0},{10,2},{12,4},{14,6},{1,9},{3,11}... | collective-permute-start | bytes 307208 | tf_op jit(solution)/shard_map/ppermute | solution.py:502
  53.7 1.4 %collective-permute-start.11 = (f32[200,128]{1,0:T(8,128)S(1)}, f32[200,128]{1,0:T(8,128)S(1)}, u32[]{:S(2)}, u32[]{:S(2)}) collective-permute-start(f32[200,128]{1,0:T(8,128)S(1)} %get-tuple-element.41), channel_id=1, source_target_pairs={{0,12},{2,14},{4,8},{6,10},{8,4},{10,6},{12,0},{14,2},{1,13},{3,15... | collective-permute-start | bytes 307208 | tf_op jit(solution)/shard_map/ppermute | solution.py:502
  55.0 0.6 collective-permute-done.6.refs_5_
  55.6 0.1 collective-permute-start.12
  55.7 0.0 collective-permute-done.7.refs_6_
  55.7 0.0 collective-permute-done.8.refs_7_
  55.7 8.2 %collective-permute-done.10.refs_9_ = f32[200,128]{1,0:T(8,128)S(1)} collective-permute-done((f32[200,128]{1,0:T(8,128)S(1)}, f32[200,128]{1,0:T(8,128)S(1)}, u32[]{:S(2)}, u32[]{:S(2)}) %collective-permute-start.10) | collective-permute-done | bytes 102432 | tf_op jit(solution)/shard_map/ppermute | solution.py:502
  63.9 0.0 collective-permute-done.11.refs_10_
  63.9 0.0 collective-permute-done.12.refs_11_
  63.9 1.4 %final.1 = (f32[64,384]{1,0:T(8,128)}, f32[64,384]{1,0:T(8,128)}, f32[64,384]{1,0:T(8,128)}) custom-call(f32[14]{0:T(128)S(1)} %concatenate.7.values.info, f32[200,128]{1,0:T(8,128)S(1)} %get-tuple-element.25.refs_1_.refs_0_, f32[200,128]{1,0:T(8,128)S(1)} %collective-permute-done.1.outs_1_.refs_1_, f32[200,128]{1,0:T(8,128)S(1)} %collective-permute-done.2.outs_2_.refs_2_, ...), custom_call_target="tpu_custom_call" | custom-call | tf_op jit(solution)/shard_map/final/pallas_call | solution.py:436
  (4 shorter events, 0.0 us)
Async XLA Ops:
  2.9 0.9 %copy-start = (f32[1,4,384,16]{2,3,1,0:T(8,128)S(1)}, f32[1,4,384,16]{2,3,1,0:T(8,128)}, u32[]{:S(2)}) copy-start(f32[1,4,384,16]{2,3,1,0:T(8,128)} %param.8) | copy-start | bytes 294916
  3.8 1.6 %copy-start.2 = (bf16[2,1024,512]{2,1,0:T(8,128)(2,1)S(1)}, bf16[2,1024,512]{2,1,0:T(8,128)(2,1)}, u32[]{:S(2)}) copy-start(bf16[2,1024,512]{2,1,0:T(8,128)(2,1)} %constant.16.clone.table_in) | copy-start | bytes 6291460
  14.7 12.4 %collective-permute-start.5 = (f32[8,2176]{1,0:T(8,128)S(1)}, f32[8,2176]{1,0:T(8,128)S(1)}, u32[]{:S(2)}, u32[]{:S(2)}) collective-permute-start(f32[8,2176]{1,0:T(8,128)S(1)} %get-tuple-element.31), channel_id=1, source_target_pairs={{0,1},{1,0},{2,3},{3,2},{4,5},{5,4},{6,7},{7,6},{8,9},{9,8},{10,11... | collective-permute-start | bytes 208904 | tf_op jit(solution)/shard_map/ppermute | solution.py:514
  15.2 11.9 %copy-start.5 = (f32[1,2]{1,0:T(1,128)S(1)}, f32[1,2]{1,0:T(1,128)}, u32[]{:S(2)}) copy-start(f32[1,2]{1,0:T(1,128)} %constant.23) | copy-start | bytes 28
  15.2 12.0 %copy-start.4 = (f32[1,3]{1,0:T(1,128)S(1)}, f32[1,3]{1,0:T(1,128)}, u32[]{:S(2)}) copy-start(f32[1,3]{1,0:T(1,128)} %param.11) | copy-start | bytes 40
  15.2 16.9 %copy-start.1 = (f32[1,4,384,16]{2,3,1,0:T(8,128)S(1)}, f32[1,4,384,16]{2,3,1,0:T(8,128)}, u32[]{:S(2)}) copy-start(f32[1,4,384,16]{2,3,1,0:T(8,128)} %param.8) | copy-start | bytes 294916
  15.2 12.1 %collective-permute-start = (f32[520,128]{1,0:T(8,128)S(1)}, f32[520,128]{1,0:T(8,128)S(1)}, u32[]{:S(2)}, u32[]{:S(2)}) collective-permute-start(f32[520,128]{1,0:T(8,128)S(1)} %get-tuple-element.24), channel_id=1, source_target_pairs={{0,2},{2,0},{4,6},{6,4},{8,10},{10,8},{12,14},{14,12},{1,3},{3,1},... | collective-permute-start | bytes 798728 | tf_op jit(solution)/shard_map/ppermute | solution.py:534
  27.0 16.2 %collective-permute-start.4 = (f32[520,128]{1,0:T(8,128)S(1)}, f32[520,128]{1,0:T(8,128)S(1)}, u32[]{:S(2)}, u32[]{:S(2)}) collective-permute-start(f32[520,128]{1,0:T(8,128)S(1)} %get-tuple-element.30), channel_id=1, source_target_pairs={{0,2},{2,0},{4,6},{6,4},{8,10},{10,8},{12,14},{14,12},{1,3},{3,1},... | collective-permute-start | bytes 798728 | tf_op jit(solution)/shard_map/ppermute | solution.py:534
  27.4 15.9 %collective-permute-start.1 = (f32[200,128]{1,0:T(8,128)S(1)}, f32[200,128]{1,0:T(8,128)S(1)}, u32[]{:S(2)}, u32[]{:S(2)}) collective-permute-start(f32[200,128]{1,0:T(8,128)S(1)} %get-tuple-element.26), channel_id=1, source_target_pairs={{0,8},{2,10},{4,12},{6,14},{8,0},{10,2},{12,4},{14,6},{1,9},{3,11}... | collective-permute-start | bytes 307208 | tf_op jit(solution)/shard_map/ppermute | solution.py:502
  30.5 12.8 %collective-permute-start.2 = (f32[200,128]{1,0:T(8,128)S(1)}, f32[200,128]{1,0:T(8,128)S(1)}, u32[]{:S(2)}, u32[]{:S(2)}) collective-permute-start(f32[200,128]{1,0:T(8,128)S(1)} %get-tuple-element.27), channel_id=1, source_target_pairs={{0,12},{2,14},{4,8},{6,10},{8,4},{10,6},{12,0},{14,2},{1,13},{3,15... | collective-permute-start | bytes 307208 | tf_op jit(solution)/shard_map/ppermute | solution.py:502
  31.8 11.4 %collective-permute-start.3 = (f32[200,128]{1,0:T(8,128)S(1)}, f32[200,128]{1,0:T(8,128)S(1)}, u32[]{:S(2)}, u32[]{:S(2)}) collective-permute-start(f32[200,128]{1,0:T(8,128)S(1)} %get-tuple-element.28), channel_id=1, source_target_pairs={{0,4},{2,6},{4,0},{6,2},{8,12},{10,14},{12,8},{14,10},{1,5},{3,7},... | collective-permute-start | bytes 307208 | tf_op jit(solution)/shard_map/ppermute | solution.py:502
  32.1 1.6 %copy-start.3 = (bf16[2,1024,512]{2,1,0:T(8,128)(2,1)S(1)}, bf16[2,1024,512]{2,1,0:T(8,128)(2,1)}, u32[]{:S(2)}) copy-start(bf16[2,1024,512]{2,1,0:T(8,128)(2,1)} %constant.16.clone.table_in) | copy-start | bytes 6291460
  43.3 7.7 %collective-permute-start.9 = (f32[520,128]{1,0:T(8,128)S(1)}, f32[520,128]{1,0:T(8,128)S(1)}, u32[]{:S(2)}, u32[]{:S(2)}) collective-permute-start(f32[520,128]{1,0:T(8,128)S(1)} %get-tuple-element.38), channel_id=1, source_target_pairs={{0,2},{2,0},{4,6},{6,4},{8,10},{10,8},{12,14},{14,12},{1,3},{3,1},... | collective-permute-start | bytes 798728 | tf_op jit(solution)/shard_map/ppermute | solution.py:534
  44.9 10.7 %collective-permute-start.6 = (f32[200,128]{1,0:T(8,128)S(1)}, f32[200,128]{1,0:T(8,128)S(1)}, u32[]{:S(2)}, u32[]{:S(2)}) collective-permute-start(f32[200,128]{1,0:T(8,128)S(1)} %get-tuple-element.34), channel_id=1, source_target_pairs={{0,8},{2,10},{4,12},{6,14},{8,0},{10,2},{12,4},{14,6},{1,9},{3,11}... | collective-permute-start | bytes 307208 | tf_op jit(solution)/shard_map/ppermute | solution.py:502
  47.7 8.0 %collective-permute-start.7 = (f32[200,128]{1,0:T(8,128)S(1)}, f32[200,128]{1,0:T(8,128)S(1)}, u32[]{:S(2)}, u32[]{:S(2)}) collective-permute-start(f32[200,128]{1,0:T(8,128)S(1)} %get-tuple-element.35), channel_id=1, source_target_pairs={{0,12},{2,14},{4,8},{6,10},{8,4},{10,6},{12,0},{14,2},{1,13},{3,15... | collective-permute-start | bytes 307208 | tf_op jit(solution)/shard_map/ppermute | solution.py:502
  49.1 6.6 %collective-permute-start.8 = (f32[200,128]{1,0:T(8,128)S(1)}, f32[200,128]{1,0:T(8,128)S(1)}, u32[]{:S(2)}, u32[]{:S(2)}) collective-permute-start(f32[200,128]{1,0:T(8,128)S(1)} %get-tuple-element.36), channel_id=1, source_target_pairs={{0,4},{2,6},{4,0},{6,2},{8,12},{10,14},{12,8},{14,10},{1,5},{3,7},... | collective-permute-start | bytes 307208 | tf_op jit(solution)/shard_map/ppermute | solution.py:502
  51.1 12.8 %collective-permute-start.10 = (f32[200,128]{1,0:T(8,128)S(1)}, f32[200,128]{1,0:T(8,128)S(1)}, u32[]{:S(2)}, u32[]{:S(2)}) collective-permute-start(f32[200,128]{1,0:T(8,128)S(1)} %get-tuple-element.40), channel_id=1, source_target_pairs={{0,8},{2,10},{4,12},{6,14},{8,0},{10,2},{12,4},{14,6},{1,9},{3,11}... | collective-permute-start | bytes 307208 | tf_op jit(solution)/shard_map/ppermute | solution.py:502
  53.7 10.2 %collective-permute-start.11 = (f32[200,128]{1,0:T(8,128)S(1)}, f32[200,128]{1,0:T(8,128)S(1)}, u32[]{:S(2)}, u32[]{:S(2)}) collective-permute-start(f32[200,128]{1,0:T(8,128)S(1)} %get-tuple-element.41), channel_id=1, source_target_pairs={{0,12},{2,14},{4,8},{6,10},{8,4},{10,6},{12,0},{14,2},{1,13},{3,15... | collective-permute-start | bytes 307208 | tf_op jit(solution)/shard_map/ppermute | solution.py:502
  55.6 8.3 %collective-permute-start.12 = (f32[200,128]{1,0:T(8,128)S(1)}, f32[200,128]{1,0:T(8,128)S(1)}, u32[]{:S(2)}, u32[]{:S(2)}) collective-permute-start(f32[200,128]{1,0:T(8,128)S(1)} %get-tuple-element.42), channel_id=1, source_target_pairs={{0,4},{2,6},{4,0},{6,2},{8,12},{10,14},{12,8},{14,10},{1,5},{3,7},... | collective-permute-start | bytes 307208 | tf_op jit(solution)/shard_map/ppermute | solution.py:502
